TPU v7x, 32 devices: a whole 2x2x4 slice. The times are simulated.
32 devices in a mesh: parts: 1, ep: 16 (over z, y, x), fan: 2 (over core).
Axes of the slice: x: 2, y: 2, z: 4, core: 2. Of those that a mesh axis runs over, the one named last changes fastest.
Arguments:
- queries: bfloat16 [1024, 2, 8192], P(('parts', 'ep', 'fan')), may hold values from -300 to 300
- new_kv: bfloat16 [1024, 2, 1024], P(('parts', 'ep', 'fan')), may hold values from -6 to 6
- prompt_kv: bfloat16 [64, 1024, 1024], P(('parts', 'ep', 'fan')), may hold values from -6 to 6
- prompt_lens: int32 [64], P(('parts', 'ep')), may hold values from 1 to 1024, 40960 in all
- sample_prompt: int32 [1024], P(('parts', 'ep', 'fan')), may hold values from 0 to 3, as said below
- hidden: bfloat16 [1024, 4096], P(('parts', 'ep', 'fan')), may hold values from -6 to 6
- norm_gain: bfloat16 [4096], replicated, may hold values from 0.099609375 to 1.8984375
- route_ids: int32 [1024, 8], P(('parts', 'ep', 'fan')), may hold values from 0 to 15, all different within a row; in each aligned block of 32 rows (0 to 31, 32 to 63, ...) at most 32 rows name the same one
- route_logits: float32 [1024, 8], P(('parts', 'ep', 'fan')), may hold values from -8 to 8
- w_gate: bfloat16 [16, 4096, 1536], P('ep', None, 'fan'), may hold values from -0.09375 to 0.09375
- w_up: bfloat16 [16, 4096, 1536], P('ep', None, 'fan'), may hold values from -0.09375 to 0.09375
- w_down: bfloat16 [16, 1536, 4096], P('ep', 'fan'), may hold values from -0.15625 to 0.15625
Outputs:
- context: bfloat16 [1024, 2, 8192], P(('parts', 'ep', 'fan'))
- expert_out: bfloat16 [1024, 4096], P(('parts', 'ep', 'fan'))
Inputs may be any that keep to these rules, and one draw needn't show every extreme that they name: `sample_prompt`: each sample names one of the 4 prompts held by the devices of its chip, numbered by device then position; each of them has exactly 16 samples on that chip. `prompt_lens`: some prompt has exactly 1024. `route_ids`: each token names 8 different experts; among the tokens of one device no expert is named more than 32 times.
All inputs are finite; a program needn't handle non-finite values. No bound on the sum of `prompt_lens` on one device may be relied on, other than what follows from the above.
Results may differ from a plain program's by a relative error of at most 0.0071.
Values may be sent and summed in bfloat16 or wider, within the bound.
No kernel may reach another device: no remote copies, remote signals or barrier semaphores. Data moves between devices by JAX's collectives and lax.ppermute only.
A program may use at most 256 MiB of HBM per device.

v0:
```python
import jax
import jax.numpy as jnp
from jax import lax
from jax.sharding import PartitionSpec as P

HEADS = 64
KVH = 4
HD = 128
STEPS = 2
CAP = 32


def attend_block(query_block, own_block, cache, length, matches):
    width = KVH * HD
    groups = HEADS // KVH
    count = query_block.shape[0]
    key_rows = cache[:, :width].reshape(-1, KVH, HD)
    value_rows = cache[:, width:].reshape(-1, KVH, HD)
    own_keys = own_block[:, :, :width].reshape(count, STEPS, KVH, HD)
    own_values = own_block[:, :, width:].reshape(count, STEPS, KVH, HD)
    query_heads = query_block.reshape(count, STEPS, KVH, groups, HD)
    scaling = HD ** (-0.5)
    cache_scores = (
        jnp.einsum("rskgd,lkd->rkgsl", query_heads, key_rows, preferred_element_type=jnp.float32)
        * scaling
    )
    own_scores = (
        jnp.einsum("rskgd,rjkd->rkgsj", query_heads, own_keys, preferred_element_type=jnp.float32)
        * scaling
    )
    valid = jnp.arange(cache.shape[0], dtype=jnp.int32) < length
    usable = matches[:, None, None, None, None] & valid[None, None, None, None, :]
    cache_scores = jnp.where(usable, cache_scores, -1e30)
    causal = jnp.arange(STEPS)[None, :] <= jnp.arange(STEPS)[:, None]
    own_scores = jnp.where(causal, own_scores, -1e30)
    highest = jnp.maximum(jnp.max(cache_scores, axis=-1), jnp.max(own_scores, axis=-1))
    cache_exp = jnp.exp(cache_scores - highest[..., None])
    own_exp = jnp.exp(own_scores - highest[..., None])
    denominator = jnp.sum(cache_exp, axis=-1) + jnp.sum(own_exp, axis=-1)
    cache_weights = (cache_exp / denominator[..., None]).astype(jnp.bfloat16)
    own_weights = (own_exp / denominator[..., None]).astype(jnp.bfloat16)
    mixed = jnp.einsum(
        "rkgsl,lkd->rskgd", cache_weights, value_rows, preferred_element_type=jnp.float32
    )
    mixed = mixed + jnp.einsum(
        "rkgsj,rjkd->rskgd", own_weights, own_values, preferred_element_type=jnp.float32
    )
    return mixed.reshape(count, STEPS, HEADS * HD).astype(jnp.bfloat16)


def attend_all(query_block, own_block, prompt_index, caches, lengths):
    result = jnp.zeros(query_block.shape, jnp.bfloat16)
    for number in range(caches.shape[0]):
        matches = prompt_index == number
        part_out = attend_block(query_block, own_block, caches[number], lengths[number], matches)
        result = jnp.where(matches[:, None, None], part_out, result)
    return result


def on_device(
    queries,
    new_kv,
    prompt_kv,
    prompt_lens,
    sample_prompt,
    hidden,
    norm_gain,
    route_ids,
    route_logits,
    w_gate,
    w_up,
    w_down,
):
    all_caches = lax.all_gather(prompt_kv, "fan", axis=0, tiled=True)
    context = attend_all(queries, new_kv, sample_prompt, all_caches, prompt_lens)
    experts = lax.axis_size("ep")
    fan_count = lax.axis_size("fan")
    width = hidden.shape[1]
    hidden32 = hidden.astype(jnp.float32)
    meansq = jnp.mean(hidden32 * hidden32, axis=-1, keepdims=True)
    normed = (hidden32 * lax.rsqrt(meansq + 1e-06) * norm_gain.astype(jnp.float32)).astype(
        jnp.bfloat16
    )
    route_weights = jax.nn.softmax(route_logits, axis=-1)
    chosen = (route_ids[:, :, None] == jnp.arange(experts, dtype=jnp.int32)).astype(jnp.int32)
    per_token = jnp.sum(chosen, axis=1)
    earlier = jnp.cumsum(per_token, axis=0) - per_token
    slot_index = jnp.take_along_axis(earlier, route_ids, axis=1)
    target = route_ids * CAP + slot_index
    matched = target[:, :, None] == jnp.arange(experts * CAP, dtype=jnp.int32)
    dispatch = jnp.any(matched, axis=1).astype(jnp.bfloat16)
    combine = jnp.sum(jnp.where(matched, route_weights[:, :, None], 0.0), axis=1)
    outgoing = jnp.dot(dispatch.T, normed, preferred_element_type=jnp.float32).astype(jnp.bfloat16)
    outgoing = outgoing.reshape(experts, CAP, width)
    doubled = jnp.repeat(outgoing, fan_count, axis=0)
    arrived = lax.all_to_all(doubled, ("ep", "fan"), split_axis=0, concat_axis=0, tiled=True)
    sources, slots, cols = arrived.shape
    flat_rows = arrived.reshape(sources * slots, cols)
    gate_out = jnp.dot(flat_rows, w_gate[0], preferred_element_type=jnp.float32)
    up_out = jnp.dot(flat_rows, w_up[0], preferred_element_type=jnp.float32)
    units = (jax.nn.silu(gate_out) * up_out).astype(jnp.bfloat16)
    partial_out = jnp.dot(units, w_down[0], preferred_element_type=jnp.float32).astype(jnp.bfloat16)
    answers = lax.all_to_all(
        partial_out.reshape(sources, slots, cols),
        ("ep", "fan"),
        split_axis=0,
        concat_axis=0,
        tiled=True,
    )
    summed = jnp.sum(answers.reshape(experts, fan_count, CAP, width).astype(jnp.float32), axis=1)
    summed = summed.reshape(experts * CAP, width)
    expert_out = jnp.dot(
        combine, summed, precision=lax.Precision.HIGHEST, preferred_element_type=jnp.float32
    )
    return (context, expert_out.astype(jnp.bfloat16))


def solution(mesh):
    placed = (
        P(("parts", "ep", "fan"), None, None),
        P(("parts", "ep", "fan"), None, None),
        P(("parts", "ep", "fan"), None, None),
        P(("parts", "ep")),
        P(("parts", "ep", "fan")),
        P(("parts", "ep", "fan"), None),
        P(),
        P(("parts", "ep", "fan"), None),
        P(("parts", "ep", "fan"), None),
        P("ep", None, "fan"),
        P("ep", None, "fan"),
        P("ep", "fan", None),
    )
    return jax.shard_map(
        on_device,
        mesh=mesh,
        in_specs=placed,
        out_specs=(P(("parts", "ep", "fan"), None, None), P(("parts", "ep", "fan"), None)),
        check_vma=False,
    )
```

profile of v0, /device:TPU:0, one launch (start us, length us, event | category | flops | bytes accessed | tf_op | source)
XLA Modules:
  0.0 456.6 jit_solution(13439335275230268437)
XLA Ops:
  7.2 0.7 convert_reduce_fusion.1
  7.9 0.7 bitcast_or_fusion
  8.9 1.9 gather_fusion
  11.6 1.3 convolution_convert_fusion.1
  12.9 4.4 broadcast_in_dim.149
  17.2 7.4 %all-to-all-start = ((bf16[32,32,4096]{2,1,0:T(8,128)(2,1)}), bf16[32,32,4096]{2,1,0:T(8,128)(2,1)}, u32[]{:S(2)}, u32[]{:S(2)}) async-start(bf16[32,32,4096]{2,1,0:T(8,128)(2,1)} %bitcast.182), calls=%async_computation | async-start | bytes 16777216 | tf_op jit(solution)/shard_map/all_to_all | solution.py:96
  24.7 0.6 all-gather.2.cloned.1.call-start
  25.5 0.8 reshape.272
  26.3 3.3 fusion.84
  29.8 0.7 reshape.313
  30.6 0.7 fusion.83
  31.3 0.6 iota_compare_fusion.4
  31.9 0.6 iota_compare_fusion.5
  32.6 0.6 iota_compare_fusion.2
  33.2 0.6 iota_compare_fusion.3
  33.8 0.8 select_reduce_fusion
  35.3 12.8 %all-gather.2.cloned.1.call-done = bf16[4,1024,1024]{2,1,0:T(8,128)(2,1)} async-done(((bf16[2,1024,1024]{2,1,0:T(8,128)(2,1)}), bf16[4,1024,1024]{2,1,0:T(8,128)(2,1)}) %all-gather.2.cloned.1.call-update) | async-done | bytes 8388624 | tf_op jit(solution)/shard_map/all_gather | solution.py:74
  48.2 5.6 %fusion.77 = (bf16[1,1024,1024]{2,1,0:T(8,128)(2,1)}, bf16[1,1024,1024]{2,1,0:T(8,128)(2,1)}, bf16[1,1024,1024]{2,1,0:T(8,128)(2,1)}, bf16[1,1024,1024]{2,1,0:T(8,128)(2,1)S(1)}) fusion(bf16[4,1024,1024]{2,1,0:T(8,128)(2,1)} %all-gather.2.cloned.1.call-done), kind=kLoop, calls=%fused_computation.122 | loop fusion | bytes 16777216 | tf_op jit(solution)/shard_map/slice | solution.py:55
  53.8 3.9 copy.390
  57.7 3.9 copy.392
  61.7 2.5 copy.393
  64.2 2.9 copy.391
  67.1 2.8 fusion.81
  69.9 2.7 fusion.79
  72.6 1.1 fusion.78
  73.7 1.2 fusion.80
  74.9 7.4 %fusion.4 = (f32[32,4,16,2]{0,2,3,1:T(8,128)S(1)}, f32[4,1024,32,2,16]{1,2,4,3,0:T(8,128)}) fusion(pred[32,1024]{1,0:T(8,128)(4,1)S(1)} %get-tuple-element.55, bf16[1024,4,128,1,1]{0,2,4,3,1:T(8,128)(2,1)S(1)} %bitcast.192, bf16[32,2,4,16,128]{4,3,2,1,0:T(8,128)(2,1)S(1)} %reshape.272), kind=kOutput, calls=%fused_computation.18 | convolution fusion | flops 1086320640 | bytes 18923520 | tf_op jit(solution)/shard_map/rskgd,lkd->rkgsl/dot_general | solution.py:24
  82.3 7.3 %fusion.6 = (f32[32,4,16,2]{0,2,3,1:T(8,128)S(1)}, f32[4,1024,32,2,16]{1,2,4,3,0:T(8,128)}) fusion(pred[32,1024]{1,0:T(8,128)(4,1)S(1)} %get-tuple-element.53, bf16[1024,4,128,1,1]{0,2,4,3,1:T(8,128)(2,1)S(1)} %bitcast.193, bf16[32,2,4,16,128]{4,3,2,1,0:T(8,128)(2,1)S(1)} %reshape.272), kind=kOutput, calls=%fused_computation.20 | convolution fusion | flops 1086320640 | bytes 18923520 | tf_op jit(solution)/shard_map/rskgd,lkd->rkgsl/dot_general | solution.py:24
  89.6 7.3 %fusion.7 = (f32[32,4,16,2]{0,2,3,1:T(8,128)S(1)}, f32[4,1024,32,2,16]{1,2,4,3,0:T(8,128)}) fusion(pred[32,1024]{1,0:T(8,128)(4,1)S(1)} %get-tuple-element.52, bf16[1024,4,128,1,1]{0,2,4,3,1:T(8,128)(2,1)S(1)} %bitcast.191, bf16[32,2,4,16,128]{4,3,2,1,0:T(8,128)(2,1)S(1)} %reshape.272), kind=kOutput, calls=%fused_computation.21 | convolution fusion | flops 1086320640 | bytes 18923520 | tf_op jit(solution)/shard_map/rskgd,lkd->rkgsl/dot_general | solution.py:24
  96.9 7.5 %fusion.5 = (f32[32,4,16,2]{0,2,3,1:T(8,128)S(1)}, f32[4,1024,32,2,16]{1,2,4,3,0:T(8,128)}) fusion(pred[32,1024]{1,0:T(8,128)(4,1)S(1)} %get-tuple-element.54, bf16[1024,4,128,1,1]{0,2,4,3,1:T(8,128)(2,1)S(1)} %bitcast.190, bf16[32,2,4,16,128]{4,3,2,1,0:T(8,128)(2,1)S(1)} %reshape.272), kind=kOutput, calls=%fused_computation.19 | convolution fusion | flops 1086320640 | bytes 18923520 | tf_op jit(solution)/shard_map/rskgd,lkd->rkgsl/dot_general | solution.py:24
  105.1 2.6 fusion.56
  107.8 8.0 %fusion.3 = f32[32,4,16,2]{0,2,3,1:T(8,128)S(1)} fusion(f32[4,1024,32,2,16]{1,2,4,3,0:T(8,128)} %get-tuple-element.49, f32[32,4,16,2]{0,2,3,1:T(8,128)S(1)} %get-tuple-element.31, pred[32,1024]{1,0:T(8,128)(4,1)S(1)} %get-tuple-element.52), kind=kLoop, calls=%fused_computation.17 | loop fusion | flops 16773120 | bytes 16842752 | tf_op jit(solution)/shard_map/reduce_sum | solution.py:39
  116.0 1.9 fusion.60
  117.9 92.9 %all-to-all-done = bf16[32,32,4096]{2,1,0:T(8,128)(2,1)} async-done(((bf16[32,32,4096]{2,1,0:T(8,128)(2,1)}), bf16[32,32,4096]{2,1,0:T(8,128)(2,1)}, u32[]{:S(2)}, u32[]{:S(2)}) %all-to-all-start) | async-done | bytes 8388640 | tf_op jit(solution)/shard_map/all_to_all | solution.py:96
  210.7 11.0 %fusion.17 = f32[1024,768]{1,0:T(8,128)S(1)} fusion(bf16[1024,4096]{1,0:T(8,128)(2,1)} %bitcast.47, bf16[1,4096,768]{2,1,0:T(8,128)(2,1)} %param.22), kind=kOutput, calls=%fused_computation.32 | convolution fusion | flops 6442450944 | bytes 17825792 | tf_op jit(solution)/shard_map/dot_general | solution.py:100
  221.8 11.4 %multiply_convert_fusion = bf16[1024,768]{1,0:T(8,128)(2,1)S(1)} fusion(f32[1024,768]{1,0:T(8,128)S(1)} %fusion.17, bf16[1024,4096]{1,0:T(8,128)(2,1)} %bitcast.47, bf16[1,4096,768]{2,1,0:T(8,128)(2,1)} %param.21), kind=kOutput, calls=%fused_computation.38 | convolution fusion | flops 6447169536 | bytes 19398656 | tf_op jit(solution)/shard_map/dot_general | solution.py:99
  233.2 9.1 %convolution_convert_fusion = bf16[1024,4096]{1,0:T(8,128)(2,1)} fusion(bf16[1024,768]{1,0:T(8,128)(2,1)S(1)} %multiply_convert_fusion, bf16[1,768,4096]{2,1,0:T(8,128)(2,1)S(1)} %bitcast.203), kind=kOutput, calls=%fused_computation.30 | convolution fusion | flops 6446645248 | bytes 16252928 | tf_op jit(solution)/shard_map/dot_general | solution.py:102
  242.3 3.8 all-to-all-start.1
  246.1 9.1 %fusion.23 = bf16[32,2,4,16,128]{4,0,1,3,2:T(8,128)(2,1)S(1)} fusion(f32[32,4,16,2,128]{4,2,3,1,0:T(8,128)} %fusion.60, bf16[1024,4,128,1,1]{0,2,4,3,1:T(8,128)(2,1)S(1)} %bitcast.197, f32[4,1024,32,2,16]{1,2,4,3,0:T(8,128)} %get-tuple-element.49, f32[32,4,16,2]{0,2,3,1:T(8,128)S(1)} %add.72, f32[32,4,16,2]{0,2,3,1:T(8,128)S(1)} %get-tuple-element.31, ...), kind=kOutput, calls=%fused_computation.40 | convolution fusion | flops 1095761920 | bytes 21037056 | tf_op jit(solution)/shard_map/rkgsl,lkd->rskgd/dot_general | solution.py:42
  255.2 0.7 copy.340
  255.9 0.5 convert_element_type.94
  256.4 1.0 copy.322
  257.5 8.0 %fusion.2 = f32[32,4,16,2]{0,2,3,1:T(8,128)S(1)} fusion(f32[4,1024,32,2,16]{1,2,4,3,0:T(8,128)} %get-tuple-element.47, f32[32,4,16,2]{0,2,3,1:T(8,128)S(1)} %get-tuple-element.32, pred[32,1024]{1,0:T(8,128)(4,1)S(1)} %get-tuple-element.53), kind=kLoop, calls=%fused_computation.16 | loop fusion | flops 16773120 | bytes 16842752 | tf_op jit(solution)/shard_map/reduce_sum | solution.py:39
  265.7 0.6 fusion.59
  266.3 8.7 %fusion.24 = bf16[32,2,4,16,128]{4,0,1,3,2:T(8,128)(2,1)S(1)} fusion(f32[32,4,16,2,128]{4,2,3,1,0:T(8,128)S(1)} %fusion.59, bf16[1024,4,128,1,1]{0,2,4,3,1:T(8,128)(2,1)S(1)} %bitcast.196, f32[4,1024,32,2,16]{1,2,4,3,0:T(8,128)} %get-tuple-element.47, f32[32,4,16,2]{0,2,3,1:T(8,128)} %copy-done.18, f32[32,4,16,2]{0,2,3,1:T(8,128)S(1)} %get-tuple-element.32, ...), kind=kOutput, calls=%fused_computation.42 | convolution fusion | flops 1095761920 | bytes 21037056 | tf_op jit(solution)/shard_map/rkgsl,lkd->rskgd/dot_general | solution.py:42
  275.0 0.7 copy.328
  275.6 0.5 convert_element_type.90
  276.1 1.0 copy.310
  277.2 8.0 %fusion.1 = f32[32,4,16,2]{0,2,3,1:T(8,128)S(1)} fusion(f32[4,1024,32,2,16]{1,2,4,3,0:T(8,128)} %get-tuple-element.51, f32[32,4,16,2]{0,2,3,1:T(8,128)S(1)} %get-tuple-element.30, pred[32,1024]{1,0:T(8,128)(4,1)S(1)} %get-tuple-element.54), kind=kLoop, calls=%fused_computation.15 | loop fusion | flops 16773120 | bytes 16842752 | tf_op jit(solution)/shard_map/reduce_sum | solution.py:39
  285.3 0.6 fusion.58
  285.9 9.2 %fusion.25 = bf16[32,2,4,16,128]{4,0,1,3,2:T(8,128)(2,1)S(1)} fusion(f32[32,4,16,2,128]{4,2,3,1,0:T(8,128)S(1)} %fusion.58, bf16[1024,4,128,1,1]{0,2,4,3,1:T(8,128)(2,1)} %bitcast.195, f32[4,1024,32,2,16]{1,2,4,3,0:T(8,128)} %get-tuple-element.51, f32[32,4,16,2]{0,2,3,1:T(8,128)} %copy-done.19, f32[32,4,16,2]{0,2,3,1:T(8,128)S(1)} %get-tuple-element.30, ...), kind=kOutput, calls=%fused_computation.44 | convolution fusion | flops 1095761920 | bytes 21037056 | tf_op jit(solution)/shard_map/rkgsl,lkd->rskgd/dot_general | solution.py:42
  295.2 1.7 copy.316
  296.8 1.5 convert_element_type.86
  298.5 8.0 %fusion = f32[32,4,16,2]{0,2,3,1:T(8,128)S(1)} fusion(f32[4,1024,32,2,16]{1,2,4,3,0:T(8,128)} %get-tuple-element.43, f32[32,4,16,2]{0,2,3,1:T(8,128)S(1)} %copy-done.8, pred[32,1024]{1,0:T(8,128)(4,1)S(1)} %copy-done.2), kind=kLoop, calls=%fused_computation.14 | loop fusion | flops 16773120 | bytes 16842752 | tf_op jit(solution)/shard_map/reduce_sum | solution.py:39
  306.5 0.7 copy.300
  307.2 1.6 fusion.57
  308.8 8.8 %fusion.26 = bf16[32,2,4,16,128]{4,0,1,3,2:T(8,128)(2,1)S(1)} fusion(f32[32,4,16,2,128]{4,2,3,1,0:T(8,128)S(1)} %fusion.57, bf16[1024,4,128,1,1]{0,2,4,3,1:T(8,128)(2,1)} %bitcast.194, f32[4,1024,32,2,16]{1,2,4,3,0:T(8,128)} %get-tuple-element.43, f32[32,4,16,2]{0,2,3,1:T(8,128)S(1)} %add.66, f32[32,4,16,2]{0,2,3,1:T(8,128)S(1)} %copy-done.8, ...), kind=kOutput, calls=%fused_computation.46 | convolution fusion | flops 1095761920 | bytes 21037056 | tf_op jit(solution)/shard_map/rkgsl,lkd->rskgd/dot_general | solution.py:42
  317.6 1.6 copy.304
  319.3 2.4 convert_element_type.82
  321.7 1.5 select_select_fusion
  323.2 2.1 copy.347
  325.3 107.0 %all-to-all-done.1 = bf16[32,32,4096]{2,1,0:T(8,128)(2,1)} async-done(((bf16[32,32,4096]{2,1,0:T(8,128)(2,1)}), bf16[32,32,4096]{2,1,0:T(8,128)(2,1)}, u32[]{:S(2)}, u32[]{:S(2)}) %all-to-all-start.1) | async-done | bytes 8388640 | tf_op jit(solution)/shard_map/all_to_all | solution.py:103
  432.3 9.4 %convert_reduce_fusion = f32[16,32,4096]{2,1,0:T(8,128)} fusion(bf16[32,32,4096]{2,1,0:T(8,128)(2,1)} %all-to-all-done.1), kind=kLoop, calls=%fused_computation.1 | loop fusion | flops 6291456 | bytes 16777216 | tf_op jit(solution)/shard_map/reduce_sum | solution.py:110
  441.6 7.9 %convolution_convert_fusion.2 = bf16[32,4096]{1,0:T(8,128)(2,1)} fusion(f32[32,512]{1,0:T(8,128)S(1)} %copy-done.14, f32[512,4096]{1,0:T(8,128)} %bitcast.183), kind=kOutput, calls=%fused_computation.37 | convolution fusion | flops 805437440 | bytes 8716288 | tf_op jit(solution)/shard_map/dot_general | solution.py:112
  (118 shorter events, 3.4 us)
Async XLA Ops:
  8.9 2.1 copy-start.24
  8.9 2.5 copy-start.26
  8.9 2.5 copy-start.3
  17.2 8.2 %copy-start.4 = (bf16[32,2,8192]{2,1,0:T(2,128)(2,1)S(1)}, bf16[32,2,8192]{2,1,0:T(2,128)(2,1)}, u32[]{:S(2)}) copy-start(bf16[32,2,8192]{2,1,0:T(2,128)(2,1)} %param.12) | copy-start | bytes 3145732
  17.2 9.1 %copy-start.20 = (bf16[32,2,1024]{2,1,0:T(2,128)(2,1)S(1)}, bf16[32,2,1024]{2,1,0:T(2,128)(2,1)}, u32[]{:S(2)}) copy-start(bf16[32,2,1024]{2,1,0:T(2,128)(2,1)} %param.13) | copy-start | bytes 393220
  17.2 193.5 %all-to-all-start = ((bf16[32,32,4096]{2,1,0:T(8,128)(2,1)}), bf16[32,32,4096]{2,1,0:T(8,128)(2,1)}, u32[]{:S(2)}, u32[]{:S(2)}) async-start(bf16[32,32,4096]{2,1,0:T(8,128)(2,1)} %bitcast.182), calls=%async_computation | async-start | bytes 16777216 | tf_op jit(solution)/shard_map/all_to_all | solution.py:96
  24.7 5.1 %slice-start = ((bf16[32,2,1024]{2,1,0:T(2,128)(2,1)}), bf16[32,2,512]{2,1,0:T(2,128)(2,1)S(1)}, s32[]{:S(2)}) async-start(bf16[32,2,1024]{2,1,0:T(2,128)(2,1)} %param.13), calls=%async_computation.3 | async-start | bytes 131072 | tf_op jit(solution)/shard_map/slice | solution.py:20
  24.7 5.8 %copy-start.25 = (f32[32,8]{0,1:T(8,128)S(1)}, f32[32,8]{0,1:T(8,128)}, u32[]{:S(2)}) copy-start(f32[32,8]{0,1:T(8,128)} %param.20) | copy-start | bytes 3076
  24.7 5.9 %copy-start.27 = (s32[4]{0:T(128)S(1)}, s32[4]{0:T(128)}, u32[]{:S(2)}) copy-start(s32[4]{0:T(128)} %param.15) | copy-start | bytes 52
  24.7 9.9 %copy-start.36 = (s32[32]{0:T(128)S(1)}, s32[32]{0:T(128)}, u32[]{:S(2)}) copy-start(s32[32]{0:T(128)} %param.16) | copy-start | bytes 388
  24.7 23.4 %all-gather.2.cloned.1.call-start = ((), (), s32[]{:S(2)}) async-start(), calls=%async_computation.2 | async-start | bytes 12582912 | tf_op jit(solution)/shard_map/all_gather | solution.py:74
  34.6 0.5 copy-start.28
  34.6 0.6 copy-start.30
  34.7 19.1 %copy-start.32 = (pred[32]{0:T(512)(128)(4,1)}, pred[32]{0:T(512)(128)(4,1)S(1)}, u32[]{:S(2)}) copy-start(pred[32]{0:T(512)(128)(4,1)S(1)} %get-tuple-element.36) | copy-start | bytes 100
  34.7 19.1 %copy-start.34 = (pred[32]{0:T(512)(128)(4,1)}, pred[32]{0:T(512)(128)(4,1)S(1)}, u32[]{:S(2)}) copy-start(pred[32]{0:T(512)(128)(4,1)S(1)} %get-tuple-element.37) | copy-start | bytes 100
  34.8 40.1 %copy-start.1 = (pred[32,1024]{1,0:T(8,128)(4,1)}, pred[32,1024]{1,0:T(8,128)(4,1)S(1)}, u32[]{:S(2)}) copy-start(pred[32,1024]{1,0:T(8,128)(4,1)S(1)} %get-tuple-element.55) | copy-start | bytes 98308
  67.0 5.5 %copy-start = (bf16[1,1024,1024]{1,2,0:T(8,128)(2,1)S(1)}, bf16[1,1024,1024]{1,2,0:T(8,128)(2,1)}, u32[]{:S(2)}) copy-start(bf16[1,1024,1024]{1,2,0:T(8,128)(2,1)} %copy.393) | copy-start | bytes 6291460
  96.9 8.2 %copy-start.15 = (f32[32,4,16,2,2]{2,4,3,1,0:T(2,128)S(1)}, f32[32,4,16,2,2]{2,4,3,1,0:T(2,128)}, u32[]{:S(2)}) copy-start(f32[32,4,16,2,2]{2,4,3,1,0:T(2,128)} %get-tuple-element.45) | copy-start | bytes 98308
  104.5 11.3 %copy-start.7 = (f32[32,4,16,2]{0,2,3,1:T(8,128)}, f32[32,4,16,2]{0,2,3,1:T(8,128)S(1)}, u32[]{:S(2)}) copy-start(f32[32,4,16,2]{0,2,3,1:T(8,128)S(1)} %get-tuple-element.33) | copy-start | bytes 49156
  104.7 11.2 %copy-start.9 = (f32[32,4,16,2]{2,3,1,0:T(2,128)}, f32[32,4,16,2]{2,3,1,0:T(2,128)S(1)}, u32[]{:S(2)}) copy-start(f32[32,4,16,2]{2,3,1,0:T(2,128)S(1)} %copy.296) | copy-start | bytes 49156
  104.9 10.9 %copy-start.12 = (f32[32,4,16,2]{2,3,1,0:T(2,128)}, f32[32,4,16,2]{2,3,1,0:T(2,128)S(1)}, u32[]{:S(2)}) copy-start(f32[32,4,16,2]{2,3,1,0:T(2,128)S(1)} %copy.321) | copy-start | bytes 49156
  107.8 8.2 %copy-start.21 = (bf16[32,2,4,128]{3,2,1,0:T(4,128)(2,1)S(1)}, bf16[32,2,4,128]{3,2,1,0:T(4,128)(2,1)}, u32[]{:S(2)}) copy-start(bf16[32,2,4,128]{3,2,1,0:T(4,128)(2,1)} %reshape.313) | copy-start | bytes 196612
  210.7 22.4 %slice-start.1 = ((s8[6291456]{0:T(1024)(128)(4,1)}), s8[4194304]{0:T(1024)(128)(4,1)S(1)}, s32[]{:S(2)}) async-start(s8[6291456]{0:T(1024)(128)(4,1)} %bitcast.202), calls=%async_computation.4 | async-start | bytes 8388608
  221.8 11.4 %slice-start.2 = ((s8[6291456]{0:T(1024)(128)(4,1)}), s8[2097152]{0:T(1024)(128)(4,1)S(1)}, s32[]{:S(2)}) async-start(s8[6291456]{0:T(1024)(128)(4,1)} %bitcast.202), calls=%async_computation.5 | async-start | bytes 4194304
  242.3 3.8 copy-start.6
  242.3 190.0 %all-to-all-start.1 = ((bf16[32,32,4096]{2,1,0:T(8,128)(2,1)}), bf16[32,32,4096]{2,1,0:T(8,128)(2,1)}, u32[]{:S(2)}, u32[]{:S(2)}) async-start(bf16[32,32,4096]{2,1,0:T(8,128)(2,1)} %bitcast.185), calls=%async_computation.1 | async-start | bytes 16777216 | tf_op jit(solution)/shard_map/all_to_all | solution.py:103
  257.4 8.2 %copy-start.13 = (f32[32,4,16,2]{2,3,1,0:T(2,128)S(1)}, f32[32,4,16,2]{2,3,1,0:T(2,128)}, u32[]{:S(2)}) copy-start(f32[32,4,16,2]{2,3,1,0:T(2,128)} %copy-done.12) | copy-start | bytes 49156
  257.4 8.3 %copy-start.16 = (f32[32,4,16,2,2]{2,4,3,1,0:T(2,128)S(1)}, f32[32,4,16,2,2]{2,4,3,1,0:T(2,128)}, u32[]{:S(2)}) copy-start(f32[32,4,16,2,2]{2,4,3,1,0:T(2,128)} %get-tuple-element.45) | copy-start | bytes 98308
  257.4 8.2 %copy-start.22 = (bf16[32,2,4,128]{3,2,1,0:T(4,128)(2,1)S(1)}, bf16[32,2,4,128]{3,2,1,0:T(4,128)(2,1)}, u32[]{:S(2)}) copy-start(bf16[32,2,4,128]{3,2,1,0:T(4,128)(2,1)} %reshape.313) | copy-start | bytes 196612
  257.5 8.8 %copy-start.5 = (bf16[1024,512]{0,1:T(8,128)(2,1)S(1)}, bf16[1024,512]{0,1:T(8,128)(2,1)}, u32[]{:S(2)}) copy-start(bf16[1024,512]{0,1:T(8,128)(2,1)} %get-tuple-element.24) | copy-start | bytes 3145732
  265.5 0.7 copy-start.18
  277.1 8.2 %copy-start.17 = (f32[32,4,16,2,2]{2,4,3,1,0:T(2,128)S(1)}, f32[32,4,16,2,2]{2,4,3,1,0:T(2,128)}, u32[]{:S(2)}) copy-start(f32[32,4,16,2,2]{2,4,3,1,0:T(2,128)} %get-tuple-element.45) | copy-start | bytes 98308
  277.2 8.2 %copy-start.23 = (bf16[32,2,4,128]{3,2,1,0:T(4,128)(2,1)S(1)}, bf16[32,2,4,128]{3,2,1,0:T(4,128)(2,1)}, u32[]{:S(2)}) copy-start(bf16[32,2,4,128]{3,2,1,0:T(4,128)(2,1)} %reshape.313) | copy-start | bytes 196612
  285.2 0.7 copy-start.19
  285.9 12.4 %copy-start.11 = (f32[32,4,16,2]{2,3,1,0:T(2,128)S(1)}, f32[32,4,16,2]{2,3,1,0:T(2,128)}, u32[]{:S(2)}) copy-start(f32[32,4,16,2]{2,3,1,0:T(2,128)} %get-tuple-element.17) | copy-start | bytes 49156
  285.9 12.5 %copy-start.2 = (pred[32,1024]{1,0:T(8,128)(4,1)S(1)}, pred[32,1024]{1,0:T(8,128)(4,1)}, u32[]{:S(2)}) copy-start(pred[32,1024]{1,0:T(8,128)(4,1)} %copy-done.1) | copy-start | bytes 98308
  285.9 12.5 %copy-start.8 = (f32[32,4,16,2]{0,2,3,1:T(8,128)S(1)}, f32[32,4,16,2]{0,2,3,1:T(8,128)}, u32[]{:S(2)}) copy-start(f32[32,4,16,2]{0,2,3,1:T(8,128)} %copy-done.7) | copy-start | bytes 49156
  298.5 8.7 %copy-start.10 = (f32[32,4,16,2]{2,3,1,0:T(2,128)S(1)}, f32[32,4,16,2]{2,3,1,0:T(2,128)}, u32[]{:S(2)}) copy-start(f32[32,4,16,2]{2,3,1,0:T(2,128)} %copy-done.9) | copy-start | bytes 49156
  308.8 12.9 %copy-start.29 = (pred[32]{0:T(512)(128)(4,1)S(1)}, pred[32]{0:T(512)(128)(4,1)}, u32[]{:S(2)}) copy-start(pred[32]{0:T(512)(128)(4,1)} %copy-done.28) | copy-start | bytes 100
  308.8 12.9 %copy-start.31 = (pred[32]{0:T(512)(128)(4,1)S(1)}, pred[32]{0:T(512)(128)(4,1)}, u32[]{:S(2)}) copy-start(pred[32]{0:T(512)(128)(4,1)} %copy-done.30) | copy-start | bytes 100
  308.8 12.9 %copy-start.33 = (pred[32]{0:T(512)(128)(4,1)S(1)}, pred[32]{0:T(512)(128)(4,1)}, u32[]{:S(2)}) copy-start(pred[32]{0:T(512)(128)(4,1)} %copy-done.32) | copy-start | bytes 100
  308.8 12.9 %copy-start.35 = (pred[32]{0:T(512)(128)(4,1)S(1)}, pred[32]{0:T(512)(128)(4,1)}, u32[]{:S(2)}) copy-start(pred[32]{0:T(512)(128)(4,1)} %copy-done.34) | copy-start | bytes 100
  325.3 116.4 %copy-start.14 = (f32[32,512]{1,0:T(8,128)S(1)}, f32[32,512]{1,0:T(8,128)}, u32[]{:S(2)}) copy-start(f32[32,512]{1,0:T(8,128)} %select_reduce_fusion) | copy-start | bytes 196612
Sparse Core Ops, SparseCore 0:
  27.1 21.0 all-gather.1
where the time goes:
time: 460 us; the launch traced here: 457 us
  waiting for transfers between devices  213 us (46%)
  matrix products  114 us (25%)
  local copies, waits for them, and re-layouts  51.9 us (11%)
  other arithmetic  51 us (11%)
  between operations  15 us (3%)
  starting transfers between devices  11.8 us (3%)
    all_to_all x1, waiting for transfers between devices, on_device(): lax.all_to_all(partial_out.reshape(sources, slots, cols), ('ep', 'fan'),...  107 us
    all_to_all x1, waiting for transfers between devices, on_device(): lax.all_to_all(doubled, ('ep', 'fan'), split_axis=0, concat_axis=0, tiled...  92.9 us
    dot_general x4, matrix products, attend_block(): jnp.einsum('rkgsl,lkd->rskgd', cache_weights, value_rows, preferred_eleme...  35.8 us
    reduce_sum x5, other arithmetic, attend_block(): denominator = jnp.sum(cache_exp, axis=-1) + jnp.sum(own_exp, axis=-1)  34.6 us
    dot_general x4, matrix products, attend_block(): jnp.einsum('rskgd,lkd->rkgsl', query_heads, key_rows, preferred_element_t...  29.6 us
    unnamed x83, local copies, waits for them, and re-layouts  15.9 us
    all_gather x1, waiting for transfers between devices, on_device(): all_caches = lax.all_gather(prompt_kv, 'fan', axis=0, tiled=True)  12.8 us
    dot_general x1, matrix products, on_device(): gate_out = jnp.dot(flat_rows, w_gate[0], preferred_element_type=jnp.float32)  11.4 us
  transfers between devices with their start and end apart: 3, of which 3 were waited for; matrix products, arithmetic and copies ran while one was open for 35% of the time, Pallas kernels for 0%

commit v1 on v0

--- a/solution.py
+++ b/solution.py
@@ -7,7 +7,6 @@
 KVH = 4
 HD = 128
 STEPS = 2
-CAP = 32
 
 
 def attend_block(query_block, own_block, cache, length, matches):
@@ -74,44 +73,23 @@
     all_caches = lax.all_gather(prompt_kv, "fan", axis=0, tiled=True)
     context = attend_all(queries, new_kv, sample_prompt, all_caches, prompt_lens)
     experts = lax.axis_size("ep")
-    fan_count = lax.axis_size("fan")
-    width = hidden.shape[1]
     hidden32 = hidden.astype(jnp.float32)
     meansq = jnp.mean(hidden32 * hidden32, axis=-1, keepdims=True)
     normed = (hidden32 * lax.rsqrt(meansq + 1e-06) * norm_gain.astype(jnp.float32)).astype(
         jnp.bfloat16
     )
     route_weights = jax.nn.softmax(route_logits, axis=-1)
-    chosen = (route_ids[:, :, None] == jnp.arange(experts, dtype=jnp.int32)).astype(jnp.int32)
-    per_token = jnp.sum(chosen, axis=1)
-    earlier = jnp.cumsum(per_token, axis=0) - per_token
-    slot_index = jnp.take_along_axis(earlier, route_ids, axis=1)
-    target = route_ids * CAP + slot_index
-    matched = target[:, :, None] == jnp.arange(experts * CAP, dtype=jnp.int32)
-    dispatch = jnp.any(matched, axis=1).astype(jnp.bfloat16)
+    matched = route_ids[:, :, None] == jnp.arange(experts, dtype=jnp.int32)
     combine = jnp.sum(jnp.where(matched, route_weights[:, :, None], 0.0), axis=1)
-    outgoing = jnp.dot(dispatch.T, normed, preferred_element_type=jnp.float32).astype(jnp.bfloat16)
-    outgoing = outgoing.reshape(experts, CAP, width)
-    doubled = jnp.repeat(outgoing, fan_count, axis=0)
-    arrived = lax.all_to_all(doubled, ("ep", "fan"), split_axis=0, concat_axis=0, tiled=True)
-    sources, slots, cols = arrived.shape
-    flat_rows = arrived.reshape(sources * slots, cols)
-    gate_out = jnp.dot(flat_rows, w_gate[0], preferred_element_type=jnp.float32)
-    up_out = jnp.dot(flat_rows, w_up[0], preferred_element_type=jnp.float32)
+    tokens = lax.all_gather(normed, ("ep", "fan"), axis=0, tiled=True)
+    all_combine = lax.all_gather(combine, ("ep", "fan"), axis=0, tiled=True)
+    column = lax.dynamic_slice_in_dim(all_combine, lax.axis_index("ep"), 1, axis=1)
+    gate_out = jnp.dot(tokens, w_gate[0], preferred_element_type=jnp.float32)
+    up_out = jnp.dot(tokens, w_up[0], preferred_element_type=jnp.float32)
     units = (jax.nn.silu(gate_out) * up_out).astype(jnp.bfloat16)
-    partial_out = jnp.dot(units, w_down[0], preferred_element_type=jnp.float32).astype(jnp.bfloat16)
-    answers = lax.all_to_all(
-        partial_out.reshape(sources, slots, cols),
-        ("ep", "fan"),
-        split_axis=0,
-        concat_axis=0,
-        tiled=True,
-    )
-    summed = jnp.sum(answers.reshape(experts, fan_count, CAP, width).astype(jnp.float32), axis=1)
-    summed = summed.reshape(experts * CAP, width)
-    expert_out = jnp.dot(
-        combine, summed, precision=lax.Precision.HIGHEST, preferred_element_type=jnp.float32
-    )
+    partial_out = jnp.dot(units, w_down[0], preferred_element_type=jnp.float32)
+    weighted = (partial_out * column).astype(jnp.bfloat16)
+    expert_out = lax.psum_scatter(weighted, ("ep", "fan"), scatter_dimension=0, tiled=True)
     return (context, expert_out.astype(jnp.bfloat16))
 
 

time: 460 us -> 323 us (0.70)
  waiting for transfers between devices: 213 us -> 65.4 us
  blocking collectives: 0 us -> 44.4 us
  starting transfers between devices: 11.8 us -> 0.12 us
  matrix products: 114 us -> 105 us
  other arithmetic: 51 us -> 43 us
    all_to_all x2 -> x0, waiting for transfers between devices: 200 us -> none  [the longest x1 107 us: on_device(): lax.all_to_all(partial_out.reshape(sources, slots, cols), ('ep', 'fan'),...]
    reduce_scatter x0 -> x1, waiting for transfers between devices: none -> 64.6 us  [on_device(): lax.psum_scatter(weighted, ('ep', 'fan'), scatter_dimension=0, tiled=True)]
    all_gather x0 -> x1, blocking collectives: none -> 44.4 us  [on_device(): all_combine = lax.all_gather(combine, ('ep', 'fan'), axis=0, tiled=True)]
    all_gather x1, waiting for transfers between devices: 12.8 us -> 0.02 us  [on_device(): all_caches = lax.all_gather(prompt_kv, 'fan', axis=0, tiled=True)]
    all_to_all x2 -> x0, starting transfers between devices: 11.2 us -> none  [the longest x1 7.43 us: on_device(): lax.all_to_all(doubled, ('ep', 'fan'), split_axis=0, concat_axis=0, tiled...]
    dot_general x5 -> x3, matrix products: 40.7 us -> 30.4 us  [the longest x1 11 us: on_device(): up_out = jnp.dot(tokens, w_up[0], preferred_element_type=jnp.float32)]
    reduce_sum x2 -> x0, other arithmetic: 10.1 us -> none  [the longest x1 9.37 us: on_device(): jnp.sum(answers.reshape(experts, fan_count, CAP, width).astype(jnp.float3...]
    unnamed x83 -> x76, local copies, waits for them, and re-layouts: 15.9 us -> 17.4 us
  transfers between devices with their start and end apart: 3 -> 3, of which waited for: 3 -> 1; matrix products, arithmetic and copies ran while one was open for 35% -> 51% of each run, Pallas kernels for 0% -> 0%
where the time goes in v1:
time: 323 us; the launch traced here: 320 us
  matrix products  105 us (33%)
  waiting for transfers between devices  65.4 us (20%)
  local copies, waits for them, and re-layouts  47.9 us (15%)
  blocking collectives  44.4 us (14%)
  other arithmetic  43 us (13%)
  between operations  14.6 us (5%)
    reduce_scatter x1, waiting for transfers between devices, on_device(): lax.psum_scatter(weighted, ('ep', 'fan'), scatter_dimension=0, tiled=True)  64.6 us
    all_gather x1, blocking collectives, on_device(): all_combine = lax.all_gather(combine, ('ep', 'fan'), axis=0, tiled=True)  44.4 us
    dot_general x4, matrix products, attend_block(): jnp.einsum('rkgsl,lkd->rskgd', cache_weights, value_rows, preferred_eleme...  35.8 us
    reduce_sum x5, other arithmetic, attend_block(): denominator = jnp.sum(cache_exp, axis=-1) + jnp.sum(own_exp, axis=-1)  35 us
    dot_general x4, matrix products, attend_block(): jnp.einsum('rskgd,lkd->rkgsl', query_heads, key_rows, preferred_element_t...  29.9 us
    unnamed x76, local copies, waits for them, and re-layouts  17.4 us
    dot_general x1, matrix products, on_device(): up_out = jnp.dot(tokens, w_up[0], preferred_element_type=jnp.float32)  11 us
    dot_general x1, matrix products, on_device(): gate_out = jnp.dot(tokens, w_gate[0], preferred_element_type=jnp.float32)  9.94 us
  transfers between devices with their start and end apart: 3, of which 1 were waited for; matrix products, arithmetic and copies ran while one was open for 51% of the time, Pallas kernels for 0%

profile of v1, /device:TPU:0, one launch (start us, length us, event | category | flops | bytes accessed | tf_op | source)
XLA Modules:
  0.0 320.2 jit_solution(4825514016132348767)
XLA Ops:
  7.3 0.7 all-gather.4.cloned.1.call-update
  8.0 0.7 convert_element_type.80
  8.7 1.1 fusion.46
  9.8 1.8 fusion.48
  11.7 1.9 reshape.244
  13.6 4.2 %fusion.80 = (f32[32,4,16,2]{2,3,1,0:T(2,128)S(1)}, f32[32,4,16,2,2]{2,4,3,1,0:T(2,128)}) fusion(bf16[32,2,4,16,128]{4,3,2,1,0:T(8,128)(2,1)S(1)} %reshape.244, bf16[32,2,1024]{2,1,0:T(2,128)(2,1)} %param.13, pred[2,2]{1,0:T(4,128)(4,1)S(1)} %iota_compare_fusion.5), kind=kOutput, calls=%fused_computation.118 | convolution fusion | flops 2117632 | bytes 1163268 | tf_op jit(solution)/shard_map/rskgd,rjkd->rkgsj/dot_general | solution.py:27
  17.8 0.7 reshape.269
  18.6 44.4 %all-gather = f32[32,32,16]{1,2,0:T(8,128)S(1)} all-gather(f32[1,32,16]{1,2,0:T(8,128)S(1)} %bitcast.187), channel_id=1, replica_groups=mesh['parts'=1,'ep'=16,'fan'=2] {'ep','fan'}, dimensions={0}, use_global_device_ids=true | all-gather | bytes 67584 | tf_op jit(solution)/shard_map/all_gather | solution.py:85
  63.1 0.1 reshape.255
  63.3 0.7 fusion.79
  63.9 0.6 iota_compare_fusion.3
  64.6 0.6 iota_compare_fusion.4
  65.2 0.6 iota_compare_fusion.1
  65.9 0.7 iota_compare_fusion.2
  66.8 0.4 copy-done.22
  67.3 5.7 %fusion.73 = (bf16[1,1024,1024]{2,1,0:T(8,128)(2,1)}, bf16[1,1024,1024]{2,1,0:T(8,128)(2,1)}, bf16[1,1024,1024]{2,1,0:T(8,128)(2,1)}, bf16[1,1024,1024]{2,1,0:T(8,128)(2,1)S(1)}) fusion(bf16[4,1024,1024]{2,1,0:T(8,128)(2,1)} %all-gather.4.cloned.1.call-done), kind=kLoop, calls=%fused_computation.111 | loop fusion | bytes 16777216 | tf_op jit(solution)/shard_map/slice | solution.py:54
  73.0 4.0 %copy.364 = bf16[1,1024,1024]{1,2,0:T(8,128)(2,1)} copy(bf16[1,1024,1024]{2,1,0:T(8,128)(2,1)} %get-tuple-element.20) | data formatting | bytes 4194304
  77.0 3.9 %copy.366 = bf16[1,1024,1024]{1,2,0:T(8,128)(2,1)} copy(bf16[1,1024,1024]{2,1,0:T(8,128)(2,1)} %get-tuple-element.19) | data formatting | bytes 4194304
  80.9 2.5 copy.367
  83.4 3.0 copy.365
  86.5 2.8 fusion.77
  89.3 2.8 fusion.75
  92.1 1.2 fusion.74
  93.3 1.1 fusion.76
  94.5 7.5 %fusion.4 = (f32[32,4,16,2]{0,2,3,1:T(8,128)S(1)}, f32[4,1024,32,2,16]{1,2,4,3,0:T(8,128)}) fusion(pred[32,1024]{1,0:T(8,128)(4,1)S(1)} %get-tuple-element.55, bf16[1024,4,128,1,1]{0,2,4,3,1:T(8,128)(2,1)S(1)} %bitcast.177, bf16[32,2,4,16,128]{4,3,2,1,0:T(8,128)(2,1)S(1)} %reshape.244), kind=kOutput, calls=%fused_computation.17 | convolution fusion | flops 1086320640 | bytes 18923520 | tf_op jit(solution)/shard_map/rskgd,lkd->rkgsl/dot_general | solution.py:23
  101.9 7.4 %fusion.6 = (f32[32,4,16,2]{0,2,3,1:T(8,128)S(1)}, f32[4,1024,32,2,16]{1,2,4,3,0:T(8,128)}) fusion(pred[32,1024]{1,0:T(8,128)(4,1)S(1)} %get-tuple-element.53, bf16[1024,4,128,1,1]{0,2,4,3,1:T(8,128)(2,1)S(1)} %bitcast.178, bf16[32,2,4,16,128]{4,3,2,1,0:T(8,128)(2,1)S(1)} %reshape.244), kind=kOutput, calls=%fused_computation.19 | convolution fusion | flops 1086320640 | bytes 18923520 | tf_op jit(solution)/shard_map/rskgd,lkd->rkgsl/dot_general | solution.py:23
  109.4 7.5 %fusion.7 = (f32[32,4,16,2]{0,2,3,1:T(8,128)S(1)}, f32[4,1024,32,2,16]{1,2,4,3,0:T(8,128)}) fusion(pred[32,1024]{1,0:T(8,128)(4,1)S(1)} %get-tuple-element.52, bf16[1024,4,128,1,1]{0,2,4,3,1:T(8,128)(2,1)S(1)} %bitcast.176, bf16[32,2,4,16,128]{4,3,2,1,0:T(8,128)(2,1)S(1)} %reshape.244), kind=kOutput, calls=%fused_computation.20 | convolution fusion | flops 1086320640 | bytes 18923520 | tf_op jit(solution)/shard_map/rskgd,lkd->rkgsl/dot_general | solution.py:23
  116.9 7.5 %fusion.5 = (f32[32,4,16,2]{0,2,3,1:T(8,128)S(1)}, f32[4,1024,32,2,16]{1,2,4,3,0:T(8,128)}) fusion(pred[32,1024]{1,0:T(8,128)(4,1)S(1)} %get-tuple-element.54, bf16[1024,4,128,1,1]{0,2,4,3,1:T(8,128)(2,1)S(1)} %bitcast.175, bf16[32,2,4,16,128]{4,3,2,1,0:T(8,128)(2,1)S(1)} %reshape.244), kind=kOutput, calls=%fused_computation.18 | convolution fusion | flops 1086320640 | bytes 18923520 | tf_op jit(solution)/shard_map/rskgd,lkd->rkgsl/dot_general | solution.py:23
  124.4 0.1 copy.275
  124.6 0.1 copy.288
  124.7 0.1 copy.300
  124.9 0.1 copy.312
  125.0 2.6 fusion.52
  127.8 8.0 %fusion.3 = f32[32,4,16,2]{0,2,3,1:T(8,128)S(1)} fusion(f32[4,1024,32,2,16]{1,2,4,3,0:T(8,128)} %get-tuple-element.49, f32[32,4,16,2]{0,2,3,1:T(8,128)S(1)} %get-tuple-element.31, pred[32,1024]{1,0:T(8,128)(4,1)S(1)} %get-tuple-element.52), kind=kLoop, calls=%fused_computation.16 | loop fusion | flops 16773120 | bytes 16842752 | tf_op jit(solution)/shard_map/reduce_sum | solution.py:38
  135.8 0.1 copy.316
  135.9 1.9 fusion.56
  137.8 11.0 %fusion.17 = f32[1024,768]{1,0:T(8,128)S(1)} fusion(bf16[1024,4096]{1,0:T(8,128)(2,1)} %all-gather.6.cloned.1.call-done, bf16[1,4096,768]{2,1,0:T(8,128)(2,1)} %param.22), kind=kOutput, calls=%fused_computation.30 | convolution fusion | flops 6442450944 | bytes 17825792 | tf_op jit(solution)/shard_map/dot_general | solution.py:88
  148.9 9.9 %multiply_convert_fusion.1 = bf16[1024,768]{1,0:T(8,128)(2,1)S(1)} fusion(f32[1024,768]{1,0:T(8,128)S(1)} %fusion.17, bf16[1024,4096]{1,0:T(8,128)(2,1)S(1)} %copy-done.32, bf16[1,4096,768]{2,1,0:T(8,128)(2,1)} %param.21), kind=kOutput, calls=%fused_computation.34 | convolution fusion | flops 6447169536 | bytes 19398656 | tf_op jit(solution)/shard_map/dot_general | solution.py:87
  158.9 9.4 %multiply_convert_fusion = bf16[1024,4096]{1,0:T(8,128)(2,1)} fusion(f32[1024]{0:T(1024)S(1)} %bitcast.188, bf16[1024,768]{1,0:T(8,128)(2,1)S(1)} %multiply_convert_fusion.1, bf16[1,768,4096]{2,1,0:T(8,128)(2,1)S(1)} %bitcast.190), kind=kOutput, calls=%fused_computation.4 | convolution fusion | flops 6450839552 | bytes 16257024 | tf_op jit(solution)/shard_map/dot_general | solution.py:90
  168.3 1.2 copy-done.4
  169.5 9.3 %fusion.23 = bf16[32,2,4,16,128]{4,0,1,3,2:T(8,128)(2,1)S(1)} fusion(f32[32,4,16,2,128]{4,2,3,1,0:T(8,128)} %fusion.56, bf16[1024,4,128,1,1]{0,2,4,3,1:T(8,128)(2,1)S(1)} %bitcast.182, f32[4,1024,32,2,16]{1,2,4,3,0:T(8,128)} %get-tuple-element.49, f32[32,4,16,2]{0,2,3,1:T(8,128)S(1)} %add.66, f32[32,4,16,2]{0,2,3,1:T(8,128)S(1)} %get-tuple-element.31, ...), kind=kOutput, calls=%fused_computation.36 | convolution fusion | flops 1095761920 | bytes 21037056 | tf_op jit(solution)/shard_map/rkgsl,lkd->rskgd/dot_general | solution.py:41
  178.8 0.7 copy.319
  179.5 0.5 convert_element_type.78
  180.0 1.0 copy.301
  181.0 8.1 %fusion.2 = f32[32,4,16,2]{0,2,3,1:T(8,128)S(1)} fusion(f32[4,1024,32,2,16]{1,2,4,3,0:T(8,128)} %get-tuple-element.47, f32[32,4,16,2]{0,2,3,1:T(8,128)S(1)} %get-tuple-element.32, pred[32,1024]{1,0:T(8,128)(4,1)S(1)} %get-tuple-element.53), kind=kLoop, calls=%fused_computation.15 | loop fusion | flops 16773120 | bytes 16842752 | tf_op jit(solution)/shard_map/reduce_sum | solution.py:38
  189.3 0.6 fusion.55
  189.9 8.7 %fusion.24 = bf16[32,2,4,16,128]{4,0,1,3,2:T(8,128)(2,1)S(1)} fusion(f32[32,4,16,2,128]{4,2,3,1,0:T(8,128)S(1)} %fusion.55, bf16[1024,4,128,1,1]{0,2,4,3,1:T(8,128)(2,1)S(1)} %bitcast.181, f32[4,1024,32,2,16]{1,2,4,3,0:T(8,128)} %get-tuple-element.47, f32[32,4,16,2]{0,2,3,1:T(8,128)} %copy-done.15, f32[32,4,16,2]{0,2,3,1:T(8,128)S(1)} %get-tuple-element.32, ...), kind=kOutput, calls=%fused_computation.38 | convolution fusion | flops 1095761920 | bytes 21037056 | tf_op jit(solution)/shard_map/rkgsl,lkd->rskgd/dot_general | solution.py:41
  198.6 0.7 copy.307
  199.2 0.5 convert_element_type.74
  199.8 1.0 copy.289
  200.8 8.2 %fusion.1 = f32[32,4,16,2]{0,2,3,1:T(8,128)S(1)} fusion(f32[4,1024,32,2,16]{1,2,4,3,0:T(8,128)} %get-tuple-element.51, f32[32,4,16,2]{0,2,3,1:T(8,128)S(1)} %get-tuple-element.30, pred[32,1024]{1,0:T(8,128)(4,1)S(1)} %get-tuple-element.54), kind=kLoop, calls=%fused_computation.14 | loop fusion | flops 16773120 | bytes 16842752 | tf_op jit(solution)/shard_map/reduce_sum | solution.py:38
  209.1 0.6 fusion.54
  209.7 8.9 %fusion.25 = bf16[32,2,4,16,128]{4,0,1,3,2:T(8,128)(2,1)S(1)} fusion(f32[32,4,16,2,128]{4,2,3,1,0:T(8,128)S(1)} %fusion.54, bf16[1024,4,128,1,1]{0,2,4,3,1:T(8,128)(2,1)} %bitcast.180, f32[4,1024,32,2,16]{1,2,4,3,0:T(8,128)} %get-tuple-element.51, f32[32,4,16,2]{0,2,3,1:T(8,128)} %copy-done.16, f32[32,4,16,2]{0,2,3,1:T(8,128)S(1)} %get-tuple-element.30, ...), kind=kOutput, calls=%fused_computation.40 | convolution fusion | flops 1095761920 | bytes 21037056 | tf_op jit(solution)/shard_map/rkgsl,lkd->rskgd/dot_general | solution.py:41
  218.6 1.7 copy.295
  220.3 1.5 convert_element_type.70
  221.9 8.1 %fusion = f32[32,4,16,2]{0,2,3,1:T(8,128)S(1)} fusion(f32[4,1024,32,2,16]{1,2,4,3,0:T(8,128)} %get-tuple-element.43, f32[32,4,16,2]{0,2,3,1:T(8,128)S(1)} %copy-done.6, pred[32,1024]{1,0:T(8,128)(4,1)S(1)} %copy-done.2), kind=kLoop, calls=%fused_computation.13 | loop fusion | flops 16773120 | bytes 16842752 | tf_op jit(solution)/shard_map/reduce_sum | solution.py:38
  230.1 0.8 copy.279
  230.8 1.6 fusion.53
  232.5 8.9 %fusion.26 = bf16[32,2,4,16,128]{4,0,1,3,2:T(8,128)(2,1)S(1)} fusion(f32[32,4,16,2,128]{4,2,3,1,0:T(8,128)S(1)} %fusion.53, bf16[1024,4,128,1,1]{0,2,4,3,1:T(8,128)(2,1)} %bitcast.179, f32[4,1024,32,2,16]{1,2,4,3,0:T(8,128)} %get-tuple-element.43, f32[32,4,16,2]{0,2,3,1:T(8,128)S(1)} %add.60, f32[32,4,16,2]{0,2,3,1:T(8,128)S(1)} %copy-done.6, ...), kind=kOutput, calls=%fused_computation.42 | convolution fusion | flops 1095761920 | bytes 21037056 | tf_op jit(solution)/shard_map/rkgsl,lkd->rskgd/dot_general | solution.py:41
  241.4 1.6 copy.283
  243.0 2.3 convert_element_type.66
  245.3 1.5 select_select_fusion
  246.8 2.1 copy.321
  248.9 64.6 %reduce-scatter.2.cloned.1.call-done = bf16[32,4096]{1,0:T(8,128)(2,1)} async-done(((bf16[1024,4096]{1,0:T(8,128)(2,1)}), bf16[32,4096]{1,0:T(8,128)(2,1)}) %reduce-scatter.2.cloned.1.call-update) | async-done | bytes 262160 | tf_op jit(solution)/shard_map/reduce_scatter | solution.py:92
  (99 shorter events, 1.4 us)
Async XLA Ops:
  7.2 10.7 %slice-start = ((bf16[32,2,1024]{2,1,0:T(2,128)(2,1)}), bf16[32,2,512]{2,1,0:T(2,128)(2,1)S(1)}, s32[]{:S(2)}) async-start(bf16[32,2,1024]{2,1,0:T(2,128)(2,1)} %param.13), calls=%async_computation.4 | async-start | bytes 131072 | tf_op jit(solution)/shard_map/slice | solution.py:19
  7.2 11.4 %copy-start.20 = (f32[32,8]{0,1:T(8,128)S(1)}, f32[32,8]{0,1:T(8,128)}, u32[]{:S(2)}) copy-start(f32[32,8]{0,1:T(8,128)} %param.20) | copy-start | bytes 3076
  7.2 11.4 %copy-start.30 = (s32[32,8]{0,1:T(8,128)S(1)}, s32[32,8]{0,1:T(8,128)}, u32[]{:S(2)}) copy-start(s32[32,8]{0,1:T(8,128)} %param.19) | copy-start | bytes 3076
  7.2 56.1 %copy-start.21 = (s32[4]{0:T(128)S(1)}, s32[4]{0:T(128)}, u32[]{:S(2)}) copy-start(s32[4]{0:T(128)} %param.15) | copy-start | bytes 52
  7.2 59.4 %copy-start.31 = (s32[32]{0:T(128)S(1)}, s32[32]{0:T(128)}, u32[]{:S(2)}) copy-start(s32[32]{0:T(128)} %param.16) | copy-start | bytes 388
  7.2 60.1 %all-gather.4.cloned.1.call-start = ((), (), s32[]{:S(2)}) async-start(), calls=%async_computation.1 | async-start | bytes 12582912 | tf_op jit(solution)/shard_map/all_gather | solution.py:73
  8.0 129.9 %all-gather.6.cloned.1.call-start = ((), (), s32[]{:S(2)}) async-start(), calls=%async_computation.2 | async-start | bytes 8650752 | tf_op jit(solution)/shard_map/all_gather | solution.py:84
  11.6 301.9 %reduce-scatter.2.cloned.1.call-start = ((), (), s32[]{:S(2)}) async-start(), calls=%async_computation.3 | async-start | bytes 8650752 | tf_op jit(solution)/shard_map/reduce_scatter | solution.py:92
  66.6 0.6 copy-start.22
  66.6 0.6 copy-start.24
  66.6 6.4 %copy-start.26 = (pred[32]{0:T(512)(128)(4,1)}, pred[32]{0:T(512)(128)(4,1)S(1)}, u32[]{:S(2)}) copy-start(pred[32]{0:T(512)(128)(4,1)S(1)} %get-tuple-element.36) | copy-start | bytes 100
  66.6 6.4 %copy-start.28 = (pred[32]{0:T(512)(128)(4,1)}, pred[32]{0:T(512)(128)(4,1)S(1)}, u32[]{:S(2)}) copy-start(pred[32]{0:T(512)(128)(4,1)S(1)} %get-tuple-element.37) | copy-start | bytes 100
  66.7 27.7 %copy-start.1 = (pred[32,1024]{1,0:T(8,128)(4,1)}, pred[32,1024]{1,0:T(8,128)(4,1)S(1)}, u32[]{:S(2)}) copy-start(pred[32,1024]{1,0:T(8,128)(4,1)S(1)} %get-tuple-element.55) | copy-start | bytes 98308
  86.5 5.6 %copy-start = (bf16[1,1024,1024]{1,2,0:T(8,128)(2,1)S(1)}, bf16[1,1024,1024]{1,2,0:T(8,128)(2,1)}, u32[]{:S(2)}) copy-start(bf16[1,1024,1024]{1,2,0:T(8,128)(2,1)} %copy.367) | copy-start | bytes 6291460
  116.9 8.2 %copy-start.12 = (f32[32,4,16,2,2]{2,4,3,1,0:T(2,128)S(1)}, f32[32,4,16,2,2]{2,4,3,1,0:T(2,128)}, u32[]{:S(2)}) copy-start(f32[32,4,16,2,2]{2,4,3,1,0:T(2,128)} %get-tuple-element.45) | copy-start | bytes 98308
  124.4 11.3 %copy-start.5 = (f32[32,4,16,2]{0,2,3,1:T(8,128)}, f32[32,4,16,2]{0,2,3,1:T(8,128)S(1)}, u32[]{:S(2)}) copy-start(f32[32,4,16,2]{0,2,3,1:T(8,128)S(1)} %get-tuple-element.33) | copy-start | bytes 49156
  124.6 11.2 %copy-start.7 = (f32[32,4,16,2]{2,3,1,0:T(2,128)}, f32[32,4,16,2]{2,3,1,0:T(2,128)S(1)}, u32[]{:S(2)}) copy-start(f32[32,4,16,2]{2,3,1,0:T(2,128)S(1)} %copy.275) | copy-start | bytes 49156
  124.9 10.9 %copy-start.10 = (f32[32,4,16,2]{2,3,1,0:T(2,128)}, f32[32,4,16,2]{2,3,1,0:T(2,128)S(1)}, u32[]{:S(2)}) copy-start(f32[32,4,16,2]{2,3,1,0:T(2,128)S(1)} %copy.300) | copy-start | bytes 49156
  127.8 8.2 %copy-start.17 = (bf16[32,2,4,128]{3,2,1,0:T(4,128)(2,1)S(1)}, bf16[32,2,4,128]{3,2,1,0:T(4,128)(2,1)}, u32[]{:S(2)}) copy-start(bf16[32,2,4,128]{3,2,1,0:T(4,128)(2,1)} %reshape.269) | copy-start | bytes 196612
  137.8 11.1 %copy-start.32 = (bf16[1024,4096]{1,0:T(8,128)(2,1)S(1)}, bf16[1024,4096]{1,0:T(8,128)(2,1)}, u32[]{:S(2)}) copy-start(bf16[1024,4096]{1,0:T(8,128)(2,1)} %all-gather.6.cloned.1.call-done) | copy-start | bytes 25165828
  137.8 21.0 %slice-start.1 = ((s8[6291456]{0:T(1024)(128)(4,1)}), s8[4194304]{0:T(1024)(128)(4,1)S(1)}, s32[]{:S(2)}) async-start(s8[6291456]{0:T(1024)(128)(4,1)} %bitcast.189), calls=%async_computation.5 | async-start | bytes 8388608
  148.9 10.0 %slice-start.2 = ((s8[6291456]{0:T(1024)(128)(4,1)}), s8[2097152]{0:T(1024)(128)(4,1)S(1)}, s32[]{:S(2)}) async-start(s8[6291456]{0:T(1024)(128)(4,1)} %bitcast.189), calls=%async_computation.6 | async-start | bytes 4194304
  168.3 1.2 copy-start.4
  181.0 8.3 %copy-start.11 = (f32[32,4,16,2]{2,3,1,0:T(2,128)S(1)}, f32[32,4,16,2]{2,3,1,0:T(2,128)}, u32[]{:S(2)}) copy-start(f32[32,4,16,2]{2,3,1,0:T(2,128)} %copy-done.10) | copy-start | bytes 49156
  181.0 8.3 %copy-start.13 = (f32[32,4,16,2,2]{2,4,3,1,0:T(2,128)S(1)}, f32[32,4,16,2,2]{2,4,3,1,0:T(2,128)}, u32[]{:S(2)}) copy-start(f32[32,4,16,2,2]{2,4,3,1,0:T(2,128)} %get-tuple-element.45) | copy-start | bytes 98308
  181.0 8.3 %copy-start.18 = (bf16[32,2,4,128]{3,2,1,0:T(4,128)(2,1)S(1)}, bf16[32,2,4,128]{3,2,1,0:T(4,128)(2,1)}, u32[]{:S(2)}) copy-start(bf16[32,2,4,128]{3,2,1,0:T(4,128)(2,1)} %reshape.269) | copy-start | bytes 196612
  181.0 8.9 %copy-start.3 = (bf16[1024,512]{0,1:T(8,128)(2,1)S(1)}, bf16[1024,512]{0,1:T(8,128)(2,1)}, u32[]{:S(2)}) copy-start(bf16[1024,512]{0,1:T(8,128)(2,1)} %get-tuple-element.24) | copy-start | bytes 3145732
  189.1 0.8 copy-start.15
  200.7 8.4 %copy-start.14 = (f32[32,4,16,2,2]{2,4,3,1,0:T(2,128)S(1)}, f32[32,4,16,2,2]{2,4,3,1,0:T(2,128)}, u32[]{:S(2)}) copy-start(f32[32,4,16,2,2]{2,4,3,1,0:T(2,128)} %get-tuple-element.45) | copy-start | bytes 98308
  200.8 8.4 %copy-start.19 = (bf16[32,2,4,128]{3,2,1,0:T(4,128)(2,1)S(1)}, bf16[32,2,4,128]{3,2,1,0:T(4,128)(2,1)}, u32[]{:S(2)}) copy-start(bf16[32,2,4,128]{3,2,1,0:T(4,128)(2,1)} %reshape.269) | copy-start | bytes 196612
  209.0 0.7 copy-start.16
  209.7 12.1 %copy-start.9 = (f32[32,4,16,2]{2,3,1,0:T(2,128)S(1)}, f32[32,4,16,2]{2,3,1,0:T(2,128)}, u32[]{:S(2)}) copy-start(f32[32,4,16,2]{2,3,1,0:T(2,128)} %get-tuple-element.17) | copy-start | bytes 49156
  209.7 12.2 %copy-start.2 = (pred[32,1024]{1,0:T(8,128)(4,1)S(1)}, pred[32,1024]{1,0:T(8,128)(4,1)}, u32[]{:S(2)}) copy-start(pred[32,1024]{1,0:T(8,128)(4,1)} %copy-done.1) | copy-start | bytes 98308
  209.7 12.2 %copy-start.6 = (f32[32,4,16,2]{0,2,3,1:T(8,128)S(1)}, f32[32,4,16,2]{0,2,3,1:T(8,128)}, u32[]{:S(2)}) copy-start(f32[32,4,16,2]{0,2,3,1:T(8,128)} %copy-done.5) | copy-start | bytes 49156
  221.9 8.9 %copy-start.8 = (f32[32,4,16,2]{2,3,1,0:T(2,128)S(1)}, f32[32,4,16,2]{2,3,1,0:T(2,128)}, u32[]{:S(2)}) copy-start(f32[32,4,16,2]{2,3,1,0:T(2,128)} %copy-done.7) | copy-start | bytes 49156
  232.4 12.9 %copy-start.23 = (pred[32]{0:T(512)(128)(4,1)S(1)}, pred[32]{0:T(512)(128)(4,1)}, u32[]{:S(2)}) copy-start(pred[32]{0:T(512)(128)(4,1)} %copy-done.22) | copy-start | bytes 100
  232.4 12.9 %copy-start.25 = (pred[32]{0:T(512)(128)(4,1)S(1)}, pred[32]{0:T(512)(128)(4,1)}, u32[]{:S(2)}) copy-start(pred[32]{0:T(512)(128)(4,1)} %copy-done.24) | copy-start | bytes 100
  232.4 12.9 %copy-start.27 = (pred[32]{0:T(512)(128)(4,1)S(1)}, pred[32]{0:T(512)(128)(4,1)}, u32[]{:S(2)}) copy-start(pred[32]{0:T(512)(128)(4,1)} %copy-done.26) | copy-start | bytes 100
  232.4 12.9 %copy-start.29 = (pred[32]{0:T(512)(128)(4,1)S(1)}, pred[32]{0:T(512)(128)(4,1)}, u32[]{:S(2)}) copy-start(pred[32]{0:T(512)(128)(4,1)} %copy-done.28) | copy-start | bytes 100
Sparse Core Ops, SparseCore 0:
  9.6 22.6 all-gather.3
  35.7 78.7 all-gather.5
  168.4 145.0 reduce-scatter.1

commit v2 on v1

v2 whole, which is shorter than its diff:
```python
import functools

import jax
import jax.numpy as jnp
from jax import lax
from jax.experimental import pallas as pl
from jax.experimental.pallas import tpu as pltpu
from jax.sharding import PartitionSpec as P

KVH = 4
HD = 128
STEPS = 2
SAMP = 16
TOP = 8
GROUP = SAMP * STEPS
LANES = 128
LOG2E = 1.4426950408889634
MIB = 1 << 20


def dot(a, b, contract=((1,), (0,))):
    return lax.dot_general(a, b, (contract, ((), ())), preferred_element_type=jnp.float32)


def cost(flops, moved):
    return pl.CostEstimate(flops=int(flops), bytes_accessed=int(moved), transcendentals=0)


def norm_kernel(hidden_ref, gain_ref, ids_ref, logits_ref, out_ref):
    rows, width = hidden_ref.shape
    hidden = hidden_ref[...].astype(jnp.float32)
    meansq = jnp.mean(hidden * hidden, axis=-1, keepdims=True)
    gain = gain_ref[...].astype(jnp.float32)
    out_ref[:, :width] = (hidden * lax.rsqrt(meansq + 1e-06) * gain).astype(jnp.bfloat16)
    logits = logits_ref[...]
    raised = jnp.exp(logits - jnp.max(logits, axis=0, keepdims=True))
    weights = raised / jnp.sum(raised, axis=0, keepdims=True)
    ids = ids_ref[...]
    number = lax.broadcasted_iota(jnp.int32, (LANES, rows), 0)
    total = jnp.zeros((LANES, rows), jnp.float32)
    for choice in range(TOP):
        picked = (number % 16) == ids[choice : choice + 1, :]
        total = total + jnp.where(picked, weights[choice : choice + 1, :], 0.0)
    high = total.astype(jnp.bfloat16).astype(jnp.float32)
    middle = (total - high).astype(jnp.bfloat16).astype(jnp.float32)
    low = total - high - middle
    piece = number // 16
    parts = jnp.where(
        piece == 0, high, jnp.where(piece == 1, middle, jnp.where(piece == 2, low, 0.0))
    ).astype(jnp.bfloat16)
    first = lax.broadcasted_iota(jnp.int32, (LANES, LANES), 0)
    second = lax.broadcasted_iota(jnp.int32, (LANES, LANES), 1)
    identity = jnp.where(first == second, 1.0, 0.0).astype(jnp.bfloat16)
    out_ref[:, width:] = dot(parts, identity, ((0,), (0,))).astype(jnp.bfloat16)


def norm_message(hidden, gain, ids, logits):
    rows, width = hidden.shape
    return pl.pallas_call(
        norm_kernel,
        out_shape=jax.ShapeDtypeStruct((rows, width + LANES), jnp.bfloat16),
        cost_estimate=cost(1e6, rows * width * 4),
        name="norm_message",
    )(hidden, gain.reshape(1, width), ids.T, logits.T)


def rank_rows(match, rows):
    first = lax.broadcasted_iota(jnp.int32, (rows, rows), 0)
    second = lax.broadcasted_iota(jnp.int32, (rows, rows), 1)
    below = jnp.where(second < first, 1.0, 0.0).astype(jnp.bfloat16)
    return dot(below, match)


def attend_kernel(
    local, lens_ref, q_mine, q_other, k_mine, k_other, v_mine, v_other, n_mine, n_other,
    key_ref, value_ref, out_ref
):
    number = lax.axis_index("fan") * 2 + local
    length = lens_ref[number]
    prompts = jnp.concatenate([n_mine[...], n_other[...]], axis=0).astype(jnp.float32)
    chosen = prompts == number.astype(jnp.float32)
    match = jnp.where(chosen, 1.0, 0.0).astype(jnp.bfloat16)
    rank = rank_rows(match, LANES)
    lane = lax.broadcasted_iota(jnp.int32, (LANES, LANES), 1)
    select = jnp.where(chosen & (rank == lane.astype(jnp.float32)), 1.0, 0.0).astype(jnp.bfloat16)

    def pick(mine, other):
        both = jnp.concatenate([mine[...], other[...]], axis=0)
        return dot(select, both, ((0,), (0,))).astype(jnp.bfloat16)

    queries = pick(q_mine, q_other)[:GROUP]
    own_keys = pick(k_mine, k_other)
    own_values = pick(v_mine, v_other)
    keys, values = key_ref[0], value_ref[0]
    span = keys.shape[0]
    factor = HD**-0.5 * LOG2E
    usable = lax.broadcasted_iota(jnp.int32, (1, span), 1) < length
    row = lax.broadcasted_iota(jnp.int32, (LANES, LANES), 0) % GROUP
    causal = (row // STEPS == lane // STEPS) & (lane <= row)
    heads = queries.shape[1] // HD
    together = LANES // GROUP
    for base in range(0, heads, together):
        block = jnp.concatenate(
            [queries[:, (base + i) * HD : (base + i + 1) * HD] for i in range(together)], axis=0
        )
        scores = jnp.where(usable, dot(block, keys, ((1,), (1,))), -1e30)
        own = jnp.where(causal, dot(block, own_keys, ((1,), (1,))), -1e30)
        highest = jnp.maximum(
            jnp.max(scores, axis=-1, keepdims=True), jnp.max(own, axis=-1, keepdims=True)
        )
        raised = jnp.exp2((scores - highest) * factor)
        own_raised = jnp.exp2((own - highest) * factor)
        total = jnp.sum(raised, axis=-1, keepdims=True) + jnp.sum(
            own_raised, axis=-1, keepdims=True
        )
        mixed = dot(raised.astype(jnp.bfloat16), values)
        mixed = mixed + dot(own_raised.astype(jnp.bfloat16), own_values)
        mixed = (mixed / total).astype(jnp.bfloat16)
        for i in range(together):
            out_ref[:, (base + i) * HD : (base + i + 1) * HD] = mixed[i * GROUP : (i + 1) * GROUP]


def attend(local, lens, mine, other, cache):
    rows = mine.shape[0]
    span = cache.shape[1]
    q_width = mine.shape[1] - 2 * KVH * HD - LANES
    head = q_width // KVH
    first = q_width // HD

    def column(at):
        return pl.BlockSpec((rows, HD), at)

    q_spec = pl.BlockSpec((rows, head), lambda k: (0, k))
    k_spec = column(lambda k: (0, first + k))
    v_spec = column(lambda k: (0, first + KVH + k))
    n_spec = column(lambda k: (0, first + 2 * KVH))
    return pl.pallas_call(
        functools.partial(attend_kernel, local),
        grid=(KVH,),
        out_shape=jax.ShapeDtypeStruct((GROUP, q_width), jnp.bfloat16),
        in_specs=[pl.BlockSpec(memory_space=pltpu.SMEM)]
        + [q_spec, q_spec, k_spec, k_spec, v_spec, v_spec, n_spec, n_spec]
        + [
            pl.BlockSpec((1, span, HD), lambda k: (local, 0, k)),
            pl.BlockSpec((1, span, HD), lambda k: (local, 0, KVH + k)),
        ],
        out_specs=pl.BlockSpec((GROUP, head), lambda k: (0, k)),
        compiler_params=pltpu.CompilerParams(vmem_limit_bytes=32 * MIB),
        cost_estimate=cost(5e9, 5 * MIB),
        name="attend",
    )(lens, mine, other, mine, other, mine, other, mine, other, cache, cache)


def place_kernel(n_mine, mine_0, mine_1, other_0, other_1, out_ref):
    rows = out_ref.shape[0]
    fan = lax.axis_index("fan")
    prompts = n_mine[...].astype(jnp.float32)
    lane = lax.broadcasted_iota(jnp.int32, (rows, LANES), 1).astype(jnp.float32)
    every = jnp.ones((rows, rows), jnp.bfloat16)
    place = jnp.zeros((rows, LANES), jnp.float32)
    for side in range(2):
        for local in range(2):
            number = (fan if side == 0 else 1 - fan) * 2 + local
            chosen = prompts == number.astype(jnp.float32)
            match = jnp.where(chosen, 1.0, 0.0).astype(jnp.bfloat16)
            rank = rank_rows(match, rows)
            if side == 1:
                rank = rank + (GROUP - dot(every, match))
            here = chosen & (rank + (side * 2 + local) * GROUP == lane)
            place = jnp.where(here, 1.0, place)
    stacked = jnp.concatenate([mine_0[...], mine_1[...], other_0[...], other_1[...]], axis=0)
    out_ref[...] = dot(place.astype(jnp.bfloat16), stacked).astype(jnp.bfloat16)


def place_context(message, mine, other):
    rows = message.shape[0]
    q_width = mine[0].shape[1]
    width = q_width // 4
    marks = message.shape[1] // LANES - 1
    block = pl.BlockSpec((GROUP, width), lambda k: (0, k))
    return pl.pallas_call(
        place_kernel,
        grid=(q_width // width,),
        out_shape=jax.ShapeDtypeStruct((rows, q_width), jnp.bfloat16),
        in_specs=[pl.BlockSpec((rows, LANES), lambda k: (0, marks)), block, block, block, block],
        out_specs=pl.BlockSpec((rows, width), lambda k: (0, k)),
        cost_estimate=cost(1e8, 3 * MIB),
        name="place_context",
    )(message, *mine, *other)


def expert_kernel(pieces, *refs):
    xs, (gate, up, down) = refs[:pieces], refs[pieces : pieces + 3]
    keep, send, other = refs[pieces + 3 : pieces + 6]
    x, w_gate, w_up, w_down, units, x_sem, g_sem, u_sem, d_sem = refs[pieces + 6 :]
    width, hidden = gate.shape
    piece_rows = xs[0].shape[0]
    step = 256
    deep = 1024
    copies = []
    for i in range(pieces):
        copies.append(
            pltpu.make_async_copy(
                xs[i], x.at[pl.ds(i * piece_rows, piece_rows)], x_sem.at[i]
            )
        )
    gates, ups, downs = [], [], []
    for i in range(hidden // step):
        at = pl.ds(i * step, step)
        gates.append(pltpu.make_async_copy(gate.at[:, at], w_gate.at[:, at], g_sem.at[i]))
        ups.append(pltpu.make_async_copy(up.at[:, at], w_up.at[:, at], u_sem.at[i]))
    for i in range(width // deep):
        at = pl.ds(i * deep, deep)
        downs.append(pltpu.make_async_copy(down.at[:, at], w_down.at[:, at], d_sem.at[i]))
    for copy in copies:
        copy.start()
    for i in range(hidden // step):
        gates[i].start()
        ups[i].start()
    for copy in downs:
        copy.start()
    for copy in copies:
        copy.wait()
    for i in range(hidden // step):
        at = slice(i * step, (i + 1) * step)
        gates[i].wait()
        opened = dot(x[:, :width], w_gate[:, at])
        ups[i].wait()
        raised = dot(x[:, :width], w_up[:, at])
        units[:, at] = (opened * jax.nn.sigmoid(opened) * raised).astype(jnp.bfloat16)
    marks = x[:, width:].astype(jnp.float32)
    lane = lax.broadcasted_iota(jnp.int32, marks.shape, 1)
    mine = (lane % 16 == lax.axis_index("ep")) & (lane < 48)
    weight = jnp.sum(jnp.where(mine, marks, 0.0), axis=1, keepdims=True)
    half = pieces // 2 * piece_rows
    near = half // 2
    for i in range(width // deep):
        downs[i].wait()
        at = slice(i * deep, (i + 1) * deep)
        result = (dot(units[...], w_down[:, at]) * weight).astype(jnp.bfloat16)
        keep[:, at] = result[:near]
        send[:, at] = result[near:half]
        other[:, at] = result[half:]


def expert_chunk(pieces, gate, up, down):
    count = len(pieces)
    piece_rows, message = pieces[0].shape
    width, hidden = gate.shape
    rows = count * piece_rows
    anywhere = pl.BlockSpec(memory_space=pl.ANY)
    whole = pl.BlockSpec(memory_space=pltpu.VMEM)
    return pl.pallas_call(
        functools.partial(expert_kernel, count),
        out_shape=(
            jax.ShapeDtypeStruct((rows // 4, width), jnp.bfloat16),
            jax.ShapeDtypeStruct((rows // 4, width), jnp.bfloat16),
            jax.ShapeDtypeStruct((rows // 2, width), jnp.bfloat16),
        ),
        in_specs=[anywhere] * (count + 3),
        out_specs=(whole, whole, whole),
        scratch_shapes=[
            pltpu.VMEM((rows, message), jnp.bfloat16),
            pltpu.VMEM((width, hidden), jnp.bfloat16),
            pltpu.VMEM((width, hidden), jnp.bfloat16),
            pltpu.VMEM((hidden, width), jnp.bfloat16),
            pltpu.VMEM((rows, hidden), jnp.bfloat16),
            pltpu.SemaphoreType.DMA((count,)),
            pltpu.SemaphoreType.DMA((hidden // 256,)),
            pltpu.SemaphoreType.DMA((hidden // 256,)),
            pltpu.SemaphoreType.DMA((width // 1024,)),
        ],
        compiler_params=pltpu.CompilerParams(vmem_limit_bytes=40 * MIB),
        cost_estimate=cost(6 * rows * width * hidden, 6 * width * hidden),
        name="expert_chunk",
    )(*pieces, gate, up, down)


def on_device(
    queries,
    new_kv,
    prompt_kv,
    prompt_lens,
    sample_prompt,
    hidden,
    norm_gain,
    route_ids,
    route_logits,
    w_gate,
    w_up,
    w_down,
):
    chips = lax.axis_size("ep")
    layers = chips // 4
    count, _, q_width = queries.shape
    rows = count * STEPS

    def swap(value, by_fan):
        pairs = [
            ((e * 2 + f), ((e ^ by_fan[f]) * 2 + f)) for e in range(chips) for f in range(2)
        ]
        return lax.ppermute(value, ("ep", "fan"), pairs)

    def near(value):
        return swap(value, (1, 2))

    def cross(value):
        return swap(value, (2, 1))

    def far(value, layer):
        return swap(value, (4 * layer, 4 * layer))

    def beside(value):
        return lax.ppermute(value, "fan", [(0, 1), (1, 0)])

    token = norm_message(hidden, norm_gain, route_ids, route_logits)
    arrived = [token] + [far(token, layer) for layer in range(1, layers)]

    marks = jnp.broadcast_to(sample_prompt.astype(jnp.bfloat16)[:, None, None], (count, STEPS, LANES))
    mine = jnp.concatenate([queries, new_kv, marks], axis=2).reshape(rows, -1)
    other = beside(mine)
    context_mine = [attend(local, prompt_lens, mine, other, prompt_kv) for local in range(2)]
    context_other = [beside(value) for value in context_mine]
    context = place_context(mine, context_mine, context_other).reshape(count, STEPS, q_width)

    parts = []
    for layer in range(layers):
        own = arrived[layer]
        first = near(own)
        pieces = [own, first, cross(own), cross(first)]
        pieces = pieces + [beside(piece) for piece in pieces]
        keep, send, away = expert_chunk(pieces, w_gate[0], w_up[0], w_down[0])
        back = beside(away).astype(jnp.float32)
        half = send.shape[0]
        single = half // 2
        there = (send.astype(jnp.float32) + back[half:]).astype(jnp.bfloat16)
        turned = cross(there).astype(jnp.float32)
        held = keep.astype(jnp.float32) + back[:half] + turned
        last = near(held[single:].astype(jnp.bfloat16)).astype(jnp.float32)
        reached = held[:single] + last
        if layer:
            reached = far(reached.astype(jnp.bfloat16), layer).astype(jnp.float32)
        parts.append(reached)
    expert_out = functools.reduce(jnp.add, parts).astype(jnp.bfloat16)
    return (context, expert_out)


def solution(mesh):
    placed = (
        P(("parts", "ep", "fan"), None, None),
        P(("parts", "ep", "fan"), None, None),
        P(("parts", "ep", "fan"), None, None),
        P(("parts", "ep")),
        P(("parts", "ep", "fan")),
        P(("parts", "ep", "fan"), None),
        P(),
        P(("parts", "ep", "fan"), None),
        P(("parts", "ep", "fan"), None),
        P("ep", None, "fan"),
        P("ep", None, "fan"),
        P("ep", "fan", None),
    )
    return jax.shard_map(
        on_device,
        mesh=mesh,
        in_specs=placed,
        out_specs=(P(("parts", "ep", "fan"), None, None), P(("parts", "ep", "fan"), None)),
        check_vma=False,
    )
```

time: 323 us -> 200 us (0.62)
  matrix products: 105 us -> 0 us
  Pallas kernels: 0 us -> 71.6 us
  blocking collectives: 44.4 us -> 0 us
  starting transfers between devices: 0.12 us -> 40.6 us
  other arithmetic: 43 us -> 12.4 us
  local copies, waits for them, and re-layouts: 47.9 us -> 18.2 us
  between operations: 14.6 us -> 1.08 us
  waiting for transfers between devices: 65.4 us -> 54 us
    dot_general x16 -> x0, matrix products: 105 us -> none  [the longest x4 35.8 us: attend_block(): jnp.einsum('rkgsl,lkd->rskgd', cache_weights, value_rows, preferred_eleme...]
    pallas_call x0 -> x8, Pallas kernels: none -> 71.6 us  [the longest x4 45.3 us: expert_chunk(): pl.pallas_call(functools.partial(expert_kernel, count), out_shape=(jax.Sh...]
    reduce_scatter x1 -> x0, waiting for transfers between devices: 64.6 us -> none  [on_device(): lax.psum_scatter(weighted, ('ep', 'fan'), scatter_dimension=0, tiled=True)]
    ppermute x0 -> x49, waiting for transfers between devices: none -> 54 us  [the longest x26 54 us: swap(): return lax.ppermute(value, ('ep', 'fan'), pairs)]
    all_gather x1 -> x0, blocking collectives: 44.4 us -> none  [on_device(): all_combine = lax.all_gather(combine, ('ep', 'fan'), axis=0, tiled=True)]
    ppermute x0 -> x49, starting transfers between devices: none -> 40.6 us  [the longest x26 36.2 us: swap(): return lax.ppermute(value, ('ep', 'fan'), pairs)]
    reduce_sum x8 -> x0, other arithmetic: 36.1 us -> none  [the longest x5 35 us: attend_block(): denominator = jnp.sum(cache_exp, axis=-1) + jnp.sum(own_exp, axis=-1)]
    slice x8 -> x4, local copies, waits for them, and re-layouts: 14.4 us -> 0.8 us  [on_device(): last = near(held[single:].astype(jnp.bfloat16)).astype(jnp.float32)]
  transfers between devices with their start and end apart: 3 -> 49, of which waited for: 1 -> 12; matrix products, arithmetic and copies ran while one was open for 51% -> 8% of each run, Pallas kernels for 0% -> 35%
where the time goes in v2:
time: 200 us; the launch traced here: 198 us
  Pallas kernels  71.6 us (36%)
  waiting for transfers between devices  54 us (27%)
  starting transfers between devices  40.6 us (20%)
  local copies, waits for them, and re-layouts  18.2 us (9%)
  other arithmetic  12.4 us (6%)
    ppermute x26, waiting for transfers between devices, swap(): return lax.ppermute(value, ('ep', 'fan'), pairs)  54 us
    pallas_call x4, Pallas kernels, expert_chunk(): pl.pallas_call(functools.partial(expert_kernel, count), out_shape=(jax.Sh...  45.3 us
    ppermute x26, starting transfers between devices, swap(): return lax.ppermute(value, ('ep', 'fan'), pairs)  36.2 us
    pallas_call x2, Pallas kernels, attend(): pl.pallas_call(functools.partial(attend_kernel, local), grid=(KVH,), out_...  20 us
    unnamed x52, local copies, waits for them, and re-layouts  11.9 us
    convert_element_type x4, other arithmetic, on_device(): back = beside(away).astype(jnp.float32)  4.48 us
    ppermute x23, starting transfers between devices, beside(): return lax.ppermute(value, 'fan', [(0, 1), (1, 0)])  4.4 us
    pallas_call x1, Pallas kernels, place_context(): pl.pallas_call(place_kernel, grid=(q_width // width,), out_shape=jax.Shap...  4.36 us
  transfers between devices with their start and end apart: 49, of which 12 were waited for; matrix products, arithmetic and copies ran while one was open for 8% of the time, Pallas kernels for 35%

profile of v2, /device:TPU:0, one launch (start us, length us, event | category | flops | bytes accessed | tf_op | source)
XLA Modules:
  0.0 197.9 jit_solution(13806575573921501233)
XLA Ops:
  0.6 1.3 reshape.16.gain_ref
  1.9 1.9 norm_message.1.refs_0_
  3.9 3.0 %collective-permute-start.13 = (bf16[32,4224]{1,0:T(8,128)(2,1)}, bf16[32,4224]{1,0:T(8,128)(2,1)S(1)}, u32[]{:S(2)}, u32[]{:S(2)}) collective-permute-start(bf16[32,4224]{1,0:T(8,128)(2,1)} %norm_message.1.refs_0_), channel_id=1, source_target_pairs={{0,8},{1,9},{2,10},{3,11},{4,12},{5,13},{6,14},{7,15},{8,0},{9,1},... | collective-permute-start | bytes 811016 | tf_op jit(solution)/shard_map/ppermute | solution.py:302
  6.9 2.6 %collective-permute-start.25 = (bf16[32,4224]{1,0:T(8,128)(2,1)}, bf16[32,4224]{1,0:T(8,128)(2,1)S(1)}, u32[]{:S(2)}, u32[]{:S(2)}) collective-permute-start(bf16[32,4224]{1,0:T(8,128)(2,1)} %norm_message.1.refs_0_), channel_id=1, source_target_pairs={{0,16},{1,17},{2,18},{3,19},{4,20},{5,21},{6,22},{7,23},{8,24},{9,... | collective-permute-start | bytes 811016 | tf_op jit(solution)/shard_map/ppermute | solution.py:302
  9.5 1.7 collective-permute-start.3
  11.2 1.5 collective-permute-start.4
  12.7 5.9 %collective-permute-done.13.refs_0_ = bf16[32,4224]{1,0:T(8,128)(2,1)S(1)} collective-permute-done((bf16[32,4224]{1,0:T(8,128)(2,1)}, bf16[32,4224]{1,0:T(8,128)(2,1)S(1)}, u32[]{:S(2)}, u32[]{:S(2)}) %collective-permute-start.13) | collective-permute-done | bytes 270368 | tf_op jit(solution)/shard_map/ppermute | solution.py:302
  18.6 10.4 %collective-permute-done.25.refs_0_ = bf16[32,4224]{1,0:T(8,128)(2,1)S(1)} collective-permute-done((bf16[32,4224]{1,0:T(8,128)(2,1)}, bf16[32,4224]{1,0:T(8,128)(2,1)S(1)}, u32[]{:S(2)}, u32[]{:S(2)}) %collective-permute-start.25) | collective-permute-done | bytes 270368 | tf_op jit(solution)/shard_map/ppermute | solution.py:302
  29.0 1.5 collective-permute-start.14
  30.5 1.5 collective-permute-start.15
  32.0 0.7 copy-done.7
  33.2 0.7 copy-done.15
  34.5 1.1 collective-permute-done.14.refs_1_
  35.5 0.7 copy-done.5
  36.3 1.9 collective-permute-done.15.refs_2_
  38.2 2.6 %collective-permute-start.5 = (bf16[32,4224]{1,0:T(8,128)(2,1)}, bf16[32,4224]{1,0:T(8,128)(2,1)}, u32[]{:S(2)}, u32[]{:S(2)}) collective-permute-start(bf16[32,4224]{1,0:T(8,128)(2,1)} %collective-permute-done.3.refs_1_), channel_id=1, source_target_pairs={{0,4},{1,3},{2,6},{3,1},{4,0},{5,7},{6,2},{7,5},{8,12},{9,11},{10,... | collective-permute-start | bytes 811016 | tf_op jit(solution)/shard_map/ppermute | solution.py:302
  40.7 0.7 convert_element_type.100
  41.4 0.7 copy-done.13
  42.1 0.5 collective-permute-start.38
  42.8 0.7 copy-done.11
  43.5 1.6 collective-permute-start.16
  45.1 1.7 collective-permute-done.5.refs_3_
  46.8 3.2 %pad_maximum_fusion = bf16[32,2,9344]{2,1,0:T(2,128)(2,1)} fusion(bf16[32,2,128]{2,1,0:T(2,128)(2,1)S(1)} %broadcast_in_dim.2, bf16[32,2,1024]{2,1,0:T(2,128)(2,1)} %param.13, bf16[32,2,8192]{2,1,0:T(2,128)(2,1)} %param.12), kind=kLoop, calls=%fused_computation | loop fusion | flops 3588096 | bytes 2392064 | tf_op jit(solution)/shard_map/concatenate | solution.py:320
  50.0 1.5 reshape.14.q_mine.k_mine.v_mine.n_mine
  51.6 2.5 %collective-permute-start.39 = (bf16[32,4224]{1,0:T(8,128)(2,1)}, bf16[32,4224]{1,0:T(8,128)(2,1)S(1)}, u32[]{:S(2)}, u32[]{:S(2)}) collective-permute-start(bf16[32,4224]{1,0:T(8,128)(2,1)} %collective-permute-done.37.refs_0_), channel_id=1, source_target_pairs={{0,4},{1,3},{2,6},{3,1},{4,0},{5,7},{6,2},{7,5},{8,12},{9,11},{10,... | collective-permute-start | bytes 811016 | tf_op jit(solution)/shard_map/ppermute | solution.py:302
  55.0 2.8 %copy-done = bf16[1,4096,768]{2,1,0:T(8,128)(2,1)S(1)} copy-done((bf16[1,4096,768]{2,1,0:T(8,128)(2,1)S(1)}, bf16[1,4096,768]{2,1,0:T(8,128)(2,1)}, u32[]{:S(2)}) %copy-start) | copy-done | bytes 6291480
  57.8 1.0 copy-done.2
  58.7 1.0 copy-done.16
  59.7 11.4 %expert_chunk.4 = (bf16[64,4096]{1,0:T(8,128)(2,1)S(1)}, bf16[64,4096]{1,0:T(8,128)(2,1)S(1)}, bf16[128,4096]{1,0:T(8,128)(2,1)S(1)}) custom-call(bf16[32,4224]{1,0:T(8,128)(2,1)S(1)} %copy-done.2, bf16[32,4224]{1,0:T(8,128)(2,1)} %collective-permute-done.3.refs_1_, bf16[32,4224]{1,0:T(8,128)(2,1)} %collective-permute-done.4.refs_2_, ...), custom_call_target="tpu_custom_call" | custom-call | flops 4831838208 | bytes 18874368 | tf_op jit(solution)/shard_map/expert_chunk/pallas_call | solution.py:253
  71.1 1.0 copy-done.18
  73.1 1.7 collective-permute-start.40
  74.8 11.0 %expert_chunk.5 = (bf16[64,4096]{1,0:T(8,128)(2,1)S(1)}, bf16[64,4096]{1,0:T(8,128)(2,1)S(1)}, bf16[128,4096]{1,0:T(8,128)(2,1)S(1)}) custom-call(bf16[32,4224]{1,0:T(8,128)(2,1)S(1)} %copy-done.8, bf16[32,4224]{1,0:T(8,128)(2,1)} %collective-permute-done.14.refs_1_, bf16[32,4224]{1,0:T(8,128)(2,1)} %collective-permute-done.15.refs_2_, ...), custom_call_target="tpu_custom_call" | custom-call | flops 4831838208 | bytes 18874368 | tf_op jit(solution)/shard_map/expert_chunk/pallas_call | solution.py:253
  85.9 0.6 collective-permute-start.41
  87.0 11.8 %expert_chunk.6 = (bf16[64,4096]{1,0:T(8,128)(2,1)S(1)}, bf16[64,4096]{1,0:T(8,128)(2,1)S(1)}, bf16[128,4096]{1,0:T(8,128)(2,1)}) custom-call(bf16[32,4224]{1,0:T(8,128)(2,1)S(1)} %copy-done.6, bf16[32,4224]{1,0:T(8,128)(2,1)} %collective-permute-done.26.refs_1_, bf16[32,4224]{1,0:T(8,128)(2,1)S(1)} %copy-done.10, ...), custom_call_target="tpu_custom_call" | custom-call | flops 4831838208 | bytes 18874368 | tf_op jit(solution)/shard_map/expert_chunk/pallas_call | solution.py:253
  99.9 11.1 %expert_chunk.7 = (bf16[64,4096]{1,0:T(8,128)(2,1)S(1)}, bf16[64,4096]{1,0:T(8,128)(2,1)S(1)}, bf16[128,4096]{1,0:T(8,128)(2,1)S(1)}) custom-call(bf16[32,4224]{1,0:T(8,128)(2,1)} %collective-permute-done.37.refs_0_, bf16[32,4224]{1,0:T(8,128)(2,1)} %collective-permute-done.38.refs_1_, bf16[32,4224]{1,0:T(8,128)(2,1)S(1)} %collective-permute-done.39.refs_2_, ...), custom_call_target="tpu_custom_call" | custom-call | flops 4831838208 | bytes 18874368 | tf_op jit(solution)/shard_map/expert_chunk/pallas_call | solution.py:253
  111.2 9.9 %attend.3.mine_1 = bf16[32,8192]{1,0:T(8,128)(2,1)S(1)} custom-call(s32[4]{0:T(128)S(1)} %copy-done.20, bf16[64,9344]{1,0:T(8,128)(2,1)S(1)} %reshape.14.q_mine.k_mine.v_mine.n_mine, bf16[64,9344]{1,0:T(8,128)(2,1)S(1)} %collective-permute-done.q_other.k_other.v_other.n_other, bf16[64,9344]{1,0:T(8,128)(2,1)S(1)} %reshape.14.q_mine.k_mine.v_mine.n_mine, ...), custom_call_target="tpu_custom_call" | custom-call | flops 5000000000 | bytes 5242880 | tf_op jit(solution)/shard_map/attend/pallas_call | solution.py:137
  121.6 10.1 %attend.2.mine_0 = bf16[32,8192]{1,0:T(8,128)(2,1)S(1)} custom-call(s32[4]{0:T(128)S(1)} %copy-done.20, bf16[64,9344]{1,0:T(8,128)(2,1)S(1)} %reshape.14.q_mine.k_mine.v_mine.n_mine, bf16[64,9344]{1,0:T(8,128)(2,1)S(1)} %collective-permute-done.q_other.k_other.v_other.n_other, bf16[64,9344]{1,0:T(8,128)(2,1)S(1)} %reshape.14.q_mine.k_mine.v_mine.n_mine, ...), custom_call_target="tpu_custom_call" | custom-call | flops 5000000000 | bytes 5242880 | tf_op jit(solution)/shard_map/attend/pallas_call | solution.py:137
  131.8 1.0 copy-done.21
  132.8 1.4 convert_element_type.102
  134.8 1.4 convert_element_type.108
  136.3 1.8 collective-permute-start.22
  138.1 1.4 convert_element_type.116
  140.4 3.3 %collective-permute-done.11 = bf16[64,4096]{1,0:T(8,128)(2,1)S(1)} collective-permute-done((bf16[64,4096]{1,0:T(8,128)(2,1)S(1)}, bf16[64,4096]{1,0:T(8,128)(2,1)S(1)}, u32[]{:S(2)}, u32[]{:S(2)}) %collective-permute-start.11) | collective-permute-done | bytes 524320 | tf_op jit(solution)/shard_map/ppermute | solution.py:302
  144.1 0.7 slice.133
  144.8 4.4 %collective-permute-done.22 = bf16[64,4096]{1,0:T(8,128)(2,1)S(1)} collective-permute-done((bf16[64,4096]{1,0:T(8,128)(2,1)S(1)}, bf16[64,4096]{1,0:T(8,128)(2,1)S(1)}, u32[]{:S(2)}, u32[]{:S(2)}) %collective-permute-start.22) | collective-permute-done | bytes 524320 | tf_op jit(solution)/shard_map/ppermute | solution.py:302
  149.3 0.5 collective-permute-start.12
  150.0 7.7 %collective-permute-done.34 = bf16[64,4096]{1,0:T(8,128)(2,1)S(1)} collective-permute-done((bf16[64,4096]{1,0:T(8,128)(2,1)S(1)}, bf16[64,4096]{1,0:T(8,128)(2,1)S(1)}, u32[]{:S(2)}, u32[]{:S(2)}) %collective-permute-start.34) | collective-permute-done | bytes 524320 | tf_op jit(solution)/shard_map/ppermute | solution.py:302
  157.7 0.5 collective-permute-start.23
  158.4 7.7 %collective-permute-done.46 = bf16[64,4096]{1,0:T(8,128)(2,1)S(1)} collective-permute-done((bf16[64,4096]{1,0:T(8,128)(2,1)S(1)}, bf16[64,4096]{1,0:T(8,128)(2,1)S(1)}, u32[]{:S(2)}, u32[]{:S(2)}) %collective-permute-start.46) | collective-permute-done | bytes 524320 | tf_op jit(solution)/shard_map/ppermute | solution.py:302
  166.1 0.5 collective-permute-start.35
  166.9 1.5 collective-permute-start.47
  168.4 0.8 fusion.10
  169.2 3.3 %collective-permute-done.35 = bf16[32,4096]{1,0:T(8,128)(2,1)S(1)} collective-permute-done((bf16[32,4096]{1,0:T(8,128)(2,1)S(1)}, bf16[32,4096]{1,0:T(8,128)(2,1)S(1)}, u32[]{:S(2)}, u32[]{:S(2)}) %collective-permute-start.35) | collective-permute-done | bytes 262176 | tf_op jit(solution)/shard_map/ppermute | solution.py:302
  172.5 3.6 %collective-permute-start.24 = (bf16[32,4096]{1,0:T(8,128)(2,1)}, bf16[32,4096]{1,0:T(8,128)(2,1)S(1)}, u32[]{:S(2)}, u32[]{:S(2)}) collective-permute-start(bf16[32,4096]{1,0:T(8,128)(2,1)} %fusion.10), channel_id=1, source_target_pairs={{0,8},{1,9},{2,10},{3,11},{4,12},{5,13},{6,14},{7,15},{8,0},{9,1},... | collective-permute-start | bytes 786440 | tf_op jit(solution)/shard_map/ppermute | solution.py:302
  176.1 0.8 fusion.9
  176.8 3.0 %collective-permute-start.36 = (bf16[32,4096]{1,0:T(8,128)(2,1)}, bf16[32,4096]{1,0:T(8,128)(2,1)S(1)}, u32[]{:S(2)}, u32[]{:S(2)}) collective-permute-start(bf16[32,4096]{1,0:T(8,128)(2,1)} %fusion.9), channel_id=1, source_target_pairs={{0,16},{1,17},{2,18},{3,19},{4,20},{5,21},{6,22},{7,23},{8,24},{9,... | collective-permute-start | bytes 786440 | tf_op jit(solution)/shard_map/ppermute | solution.py:302
  179.9 0.7 fusion.8
  180.6 0.8 copy-done.22
  181.5 1.4 collective-permute-start.48
  182.8 0.8 copy-done.23
  183.6 4.4 %place_context.1 = bf16[64,8192]{1,0:T(8,128)(2,1)} custom-call(bf16[64,9344]{1,0:T(8,128)(2,1)} %copy-done.1, bf16[32,8192]{1,0:T(8,128)(2,1)} %copy-done.4, bf16[32,8192]{1,0:T(8,128)(2,1)} %copy-done.3, bf16[32,8192]{1,0:T(8,128)(2,1)} %copy-done.23, bf16[32,8192]{1,0:T(8,128)(2,1)} %copy-done.22), custom_call_target="tpu_custom_call" | custom-call | flops 100000000 | bytes 3145728 | tf_op jit(solution)/shard_map/place_context/pallas_call | solution.py:181
  188.0 2.5 %reshape.15 = bf16[32,2,8192]{2,1,0:T(2,128)(2,1)} reshape(bf16[64,8192]{1,0:T(8,128)(2,1)} %place_context.1) | data formatting | bytes 2097152 | tf_op jit(solution)/shard_map/reshape | solution.py:324
  190.5 6.5 %collective-permute-done.36 = bf16[32,4096]{1,0:T(8,128)(2,1)S(1)} collective-permute-done((bf16[32,4096]{1,0:T(8,128)(2,1)}, bf16[32,4096]{1,0:T(8,128)(2,1)S(1)}, u32[]{:S(2)}, u32[]{:S(2)}) %collective-permute-start.36) | collective-permute-done | bytes 262176 | tf_op jit(solution)/shard_map/ppermute | solution.py:302
  197.0 0.9 fusion.14
  (121 shorter events, 7.9 us)
Async XLA Ops:
  3.9 14.7 %collective-permute-start.13 = (bf16[32,4224]{1,0:T(8,128)(2,1)}, bf16[32,4224]{1,0:T(8,128)(2,1)S(1)}, u32[]{:S(2)}, u32[]{:S(2)}) collective-permute-start(bf16[32,4224]{1,0:T(8,128)(2,1)} %norm_message.1.refs_0_), channel_id=1, source_target_pairs={{0,8},{1,9},{2,10},{3,11},{4,12},{5,13},{6,14},{7,15},{8,0},{9,1},... | collective-permute-start | bytes 811016 | tf_op jit(solution)/shard_map/ppermute | solution.py:302
  6.9 22.1 %collective-permute-start.25 = (bf16[32,4224]{1,0:T(8,128)(2,1)}, bf16[32,4224]{1,0:T(8,128)(2,1)S(1)}, u32[]{:S(2)}, u32[]{:S(2)}) collective-permute-start(bf16[32,4224]{1,0:T(8,128)(2,1)} %norm_message.1.refs_0_), channel_id=1, source_target_pairs={{0,16},{1,17},{2,18},{3,19},{4,20},{5,21},{6,22},{7,23},{8,24},{9,... | collective-permute-start | bytes 811016 | tf_op jit(solution)/shard_map/ppermute | solution.py:302
  9.5 21.0 %collective-permute-start.37 = (bf16[32,4224]{1,0:T(8,128)(2,1)}, bf16[32,4224]{1,0:T(8,128)(2,1)}, u32[]{:S(2)}, u32[]{:S(2)}) collective-permute-start(bf16[32,4224]{1,0:T(8,128)(2,1)} %norm_message.1.refs_0_), channel_id=1, source_target_pairs={{0,24},{1,25},{2,26},{3,27},{4,28},{5,29},{6,30},{7,31},{8,16},{9,... | collective-permute-start | bytes 811016 | tf_op jit(solution)/shard_map/ppermute | solution.py:302
  9.5 22.5 %collective-permute-start.3 = (bf16[32,4224]{1,0:T(8,128)(2,1)}, bf16[32,4224]{1,0:T(8,128)(2,1)}, u32[]{:S(2)}, u32[]{:S(2)}) collective-permute-start(bf16[32,4224]{1,0:T(8,128)(2,1)} %norm_message.1.refs_0_), channel_id=1, source_target_pairs={{0,2},{1,5},{2,0},{3,7},{4,6},{5,1},{6,4},{7,3},{8,10},{9,13},{10,... | collective-permute-start | bytes 811016 | tf_op jit(solution)/shard_map/ppermute | solution.py:302
  11.2 21.5 %collective-permute-start.4 = (bf16[32,4224]{1,0:T(8,128)(2,1)}, bf16[32,4224]{1,0:T(8,128)(2,1)}, u32[]{:S(2)}, u32[]{:S(2)}) collective-permute-start(bf16[32,4224]{1,0:T(8,128)(2,1)} %norm_message.1.refs_0_), channel_id=1, source_target_pairs={{0,4},{1,3},{2,6},{3,1},{4,0},{5,7},{6,2},{7,5},{8,12},{9,11},{10,... | collective-permute-start | bytes 811016 | tf_op jit(solution)/shard_map/ppermute | solution.py:302
  18.6 14.7 %collective-permute-start.6 = (bf16[32,4224]{1,0:T(8,128)(2,1)}, bf16[32,4224]{1,0:T(8,128)(2,1)S(1)}, u32[]{:S(2)}, u32[]{:S(2)}) collective-permute-start(bf16[32,4224]{1,0:T(8,128)(2,1)} %norm_message.1.refs_0_), channel_id=1, source_target_pairs={{0,1},{1,0},{2,3},{3,2},{4,5},{5,4},{6,7},{7,6},{8,9},{9,8},{10,11... | collective-permute-start | bytes 811016 | tf_op jit(solution)/shard_map/ppermute | solution.py:314
  29.0 6.6 %collective-permute-start.14 = (bf16[32,4224]{1,0:T(8,128)(2,1)S(1)}, bf16[32,4224]{1,0:T(8,128)(2,1)}, u32[]{:S(2)}, u32[]{:S(2)}) collective-permute-start(bf16[32,4224]{1,0:T(8,128)(2,1)S(1)} %collective-permute-done.13.refs_0_), channel_id=1, source_target_pairs={{0,2},{1,5},{2,0},{3,7},{4,6},{5,1},{6,4},{7,3},{8,10},{9,13},{10,... | collective-permute-start | bytes 811016 | tf_op jit(solution)/shard_map/ppermute | solution.py:302
  30.5 7.7 %collective-permute-start.15 = (bf16[32,4224]{1,0:T(8,128)(2,1)S(1)}, bf16[32,4224]{1,0:T(8,128)(2,1)}, u32[]{:S(2)}, u32[]{:S(2)}) collective-permute-start(bf16[32,4224]{1,0:T(8,128)(2,1)S(1)} %collective-permute-done.13.refs_0_), channel_id=1, source_target_pairs={{0,4},{1,3},{2,6},{3,1},{4,0},{5,7},{6,2},{7,5},{8,12},{9,11},{10,... | collective-permute-start | bytes 811016 | tf_op jit(solution)/shard_map/ppermute | solution.py:302
  32.0 9.4 %collective-permute-start.17 = (bf16[32,4224]{1,0:T(8,128)(2,1)S(1)}, bf16[32,4224]{1,0:T(8,128)(2,1)S(1)}, u32[]{:S(2)}, u32[]{:S(2)}) collective-permute-start(bf16[32,4224]{1,0:T(8,128)(2,1)S(1)} %collective-permute-done.13.refs_0_), channel_id=1, source_target_pairs={{0,1},{1,0},{2,3},{3,2},{4,5},{5,4},{6,7},{7,6},{8,9},{9,8},{10,11... | collective-permute-start | bytes 811016 | tf_op jit(solution)/shard_map/ppermute | solution.py:314
  32.7 9.4 %collective-permute-start.26 = (bf16[32,4224]{1,0:T(8,128)(2,1)S(1)}, bf16[32,4224]{1,0:T(8,128)(2,1)}, u32[]{:S(2)}, u32[]{:S(2)}) collective-permute-start(bf16[32,4224]{1,0:T(8,128)(2,1)S(1)} %collective-permute-done.25.refs_0_), channel_id=1, source_target_pairs={{0,2},{1,5},{2,0},{3,7},{4,6},{5,1},{6,4},{7,3},{8,10},{9,13},{10,... | collective-permute-start | bytes 811016 | tf_op jit(solution)/shard_map/ppermute | solution.py:302
  33.9 8.8 %collective-permute-start.27 = (bf16[32,4224]{1,0:T(8,128)(2,1)S(1)}, bf16[32,4224]{1,0:T(8,128)(2,1)S(1)}, u32[]{:S(2)}, u32[]{:S(2)}) collective-permute-start(bf16[32,4224]{1,0:T(8,128)(2,1)S(1)} %collective-permute-done.25.refs_0_), channel_id=1, source_target_pairs={{0,4},{1,3},{2,6},{3,1},{4,0},{5,7},{6,2},{7,5},{8,12},{9,11},{10,... | collective-permute-start | bytes 811016 | tf_op jit(solution)/shard_map/ppermute | solution.py:302
  35.5 7.2 %collective-permute-start.29 = (bf16[32,4224]{1,0:T(8,128)(2,1)S(1)}, bf16[32,4224]{1,0:T(8,128)(2,1)S(1)}, u32[]{:S(2)}, u32[]{:S(2)}) collective-permute-start(bf16[32,4224]{1,0:T(8,128)(2,1)S(1)} %collective-permute-done.25.refs_0_), channel_id=1, source_target_pairs={{0,1},{1,0},{2,3},{3,2},{4,5},{5,4},{6,7},{7,6},{8,9},{9,8},{10,11... | collective-permute-start | bytes 811016 | tf_op jit(solution)/shard_map/ppermute | solution.py:314
  38.2 8.6 %collective-permute-start.5 = (bf16[32,4224]{1,0:T(8,128)(2,1)}, bf16[32,4224]{1,0:T(8,128)(2,1)}, u32[]{:S(2)}, u32[]{:S(2)}) collective-permute-start(bf16[32,4224]{1,0:T(8,128)(2,1)} %collective-permute-done.3.refs_1_), channel_id=1, source_target_pairs={{0,4},{1,3},{2,6},{3,1},{4,0},{5,7},{6,2},{7,5},{8,12},{9,11},{10,... | collective-permute-start | bytes 811016 | tf_op jit(solution)/shard_map/ppermute | solution.py:302
  42.1 12.0 %collective-permute-start.7 = (bf16[32,4224]{1,0:T(8,128)(2,1)}, bf16[32,4224]{1,0:T(8,128)(2,1)}, u32[]{:S(2)}, u32[]{:S(2)}) collective-permute-start(bf16[32,4224]{1,0:T(8,128)(2,1)} %collective-permute-done.3.refs_1_), channel_id=1, source_target_pairs={{0,1},{1,0},{2,3},{3,2},{4,5},{5,4},{6,7},{7,6},{8,9},{9,8},{10,11... | collective-permute-start | bytes 811016 | tf_op jit(solution)/shard_map/ppermute | solution.py:314
  42.1 9.5 %collective-permute-start.38 = (bf16[32,4224]{1,0:T(8,128)(2,1)}, bf16[32,4224]{1,0:T(8,128)(2,1)}, u32[]{:S(2)}, u32[]{:S(2)}) collective-permute-start(bf16[32,4224]{1,0:T(8,128)(2,1)} %collective-permute-done.37.refs_0_), channel_id=1, source_target_pairs={{0,2},{1,5},{2,0},{3,7},{4,6},{5,1},{6,4},{7,3},{8,10},{9,13},{10,... | collective-permute-start | bytes 811016 | tf_op jit(solution)/shard_map/ppermute | solution.py:302
  42.7 4.0 %copy-start.9 = (bf16[32,4224]{1,0:T(8,128)(2,1)}, bf16[32,4224]{1,0:T(8,128)(2,1)S(1)}, u32[]{:S(2)}) copy-start(bf16[32,4224]{1,0:T(8,128)(2,1)S(1)} %collective-permute-done.27.refs_2_) | copy-start | bytes 811012
  42.7 11.4 %collective-permute-start.8 = (bf16[32,4224]{1,0:T(8,128)(2,1)}, bf16[32,4224]{1,0:T(8,128)(2,1)}, u32[]{:S(2)}, u32[]{:S(2)}) collective-permute-start(bf16[32,4224]{1,0:T(8,128)(2,1)} %collective-permute-done.4.refs_2_), channel_id=1, source_target_pairs={{0,1},{1,0},{2,3},{3,2},{4,5},{5,4},{6,7},{7,6},{8,9},{9,8},{10,11... | collective-permute-start | bytes 811016 | tf_op jit(solution)/shard_map/ppermute | solution.py:314
  43.5 11.1 %collective-permute-start.16 = (bf16[32,4224]{1,0:T(8,128)(2,1)}, bf16[32,4224]{1,0:T(8,128)(2,1)}, u32[]{:S(2)}, u32[]{:S(2)}) collective-permute-start(bf16[32,4224]{1,0:T(8,128)(2,1)} %collective-permute-done.14.refs_1_), channel_id=1, source_target_pairs={{0,4},{1,3},{2,6},{3,1},{4,0},{5,7},{6,2},{7,5},{8,12},{9,11},{10,... | collective-permute-start | bytes 811016 | tf_op jit(solution)/shard_map/ppermute | solution.py:302
  46.7 8.2 %collective-permute-start.9 = (bf16[32,4224]{1,0:T(8,128)(2,1)}, bf16[32,4224]{1,0:T(8,128)(2,1)}, u32[]{:S(2)}, u32[]{:S(2)}) collective-permute-start(bf16[32,4224]{1,0:T(8,128)(2,1)} %collective-permute-done.5.refs_3_), channel_id=1, source_target_pairs={{0,1},{1,0},{2,3},{3,2},{4,5},{5,4},{6,7},{7,6},{8,9},{9,8},{10,11... | collective-permute-start | bytes 811016 | tf_op jit(solution)/shard_map/ppermute | solution.py:314
  46.8 28.0 %slice-start = ((s8[6291456]{0:T(1024)(128)(4,1)}), s8[2097152]{0:T(1024)(128)(4,1)S(1)}, s32[]{:S(2)}) async-start(s8[6291456]{0:T(1024)(128)(4,1)} %bitcast.6), calls=%async_computation | async-start | bytes 4194304
  51.6 70.0 %copy-start.1 = (bf16[64,9344]{1,0:T(8,128)(2,1)}, bf16[64,9344]{1,0:T(8,128)(2,1)S(1)}, u32[]{:S(2)}) copy-start(bf16[64,9344]{1,0:T(8,128)(2,1)S(1)} %reshape.14.q_mine.k_mine.v_mine.n_mine) | copy-start | bytes 3588100
  51.6 20.5 %collective-permute-start.39 = (bf16[32,4224]{1,0:T(8,128)(2,1)}, bf16[32,4224]{1,0:T(8,128)(2,1)S(1)}, u32[]{:S(2)}, u32[]{:S(2)}) collective-permute-start(bf16[32,4224]{1,0:T(8,128)(2,1)} %collective-permute-done.37.refs_0_), channel_id=1, source_target_pairs={{0,4},{1,3},{2,6},{3,1},{4,0},{5,7},{6,2},{7,5},{8,12},{9,11},{10,... | collective-permute-start | bytes 811016 | tf_op jit(solution)/shard_map/ppermute | solution.py:302
  54.1 18.4 %collective-permute-start.18 = (bf16[32,4224]{1,0:T(8,128)(2,1)}, bf16[32,4224]{1,0:T(8,128)(2,1)S(1)}, u32[]{:S(2)}, u32[]{:S(2)}) collective-permute-start(bf16[32,4224]{1,0:T(8,128)(2,1)} %collective-permute-done.14.refs_1_), channel_id=1, source_target_pairs={{0,1},{1,0},{2,3},{3,2},{4,5},{5,4},{6,7},{7,6},{8,9},{9,8},{10,11... | collective-permute-start | bytes 811016 | tf_op jit(solution)/shard_map/ppermute | solution.py:314
  54.1 18.5 %collective-permute-start.19 = (bf16[32,4224]{1,0:T(8,128)(2,1)}, bf16[32,4224]{1,0:T(8,128)(2,1)S(1)}, u32[]{:S(2)}, u32[]{:S(2)}) collective-permute-start(bf16[32,4224]{1,0:T(8,128)(2,1)} %collective-permute-done.15.refs_2_), channel_id=1, source_target_pairs={{0,1},{1,0},{2,3},{3,2},{4,5},{5,4},{6,7},{7,6},{8,9},{9,8},{10,11... | collective-permute-start | bytes 811016 | tf_op jit(solution)/shard_map/ppermute | solution.py:314
  54.6 18.4 %collective-permute-start.28 = (bf16[32,4224]{1,0:T(8,128)(2,1)}, bf16[32,4224]{1,0:T(8,128)(2,1)S(1)}, u32[]{:S(2)}, u32[]{:S(2)}) collective-permute-start(bf16[32,4224]{1,0:T(8,128)(2,1)} %collective-permute-done.26.refs_1_), channel_id=1, source_target_pairs={{0,4},{1,3},{2,6},{3,1},{4,0},{5,7},{6,2},{7,5},{8,12},{9,11},{10,... | collective-permute-start | bytes 811016 | tf_op jit(solution)/shard_map/ppermute | solution.py:302
  55.0 19.8 %collective-permute-start.20 = (bf16[32,4224]{1,0:T(8,128)(2,1)}, bf16[32,4224]{1,0:T(8,128)(2,1)S(1)}, u32[]{:S(2)}, u32[]{:S(2)}) collective-permute-start(bf16[32,4224]{1,0:T(8,128)(2,1)} %collective-permute-done.16.refs_3_), channel_id=1, source_target_pairs={{0,1},{1,0},{2,3},{3,2},{4,5},{5,4},{6,7},{7,6},{8,9},{9,8},{10,11... | collective-permute-start | bytes 811016 | tf_op jit(solution)/shard_map/ppermute | solution.py:314
  55.0 2.8 %copy-start = (bf16[1,4096,768]{2,1,0:T(8,128)(2,1)S(1)}, bf16[1,4096,768]{2,1,0:T(8,128)(2,1)}, u32[]{:S(2)}) copy-start(bf16[1,4096,768]{2,1,0:T(8,128)(2,1)} %param.21) | copy-start | bytes 18874372
  59.7 13.0 %copy-start.10 = (bf16[32,4224]{1,0:T(8,128)(2,1)S(1)}, bf16[32,4224]{1,0:T(8,128)(2,1)}, u32[]{:S(2)}) copy-start(bf16[32,4224]{1,0:T(8,128)(2,1)} %copy-done.9) | copy-start | bytes 811012
  59.7 15.1 %slice-start.1 = ((s8[6291456]{0:T(1024)(128)(4,1)}), s8[4194304]{0:T(1024)(128)(4,1)S(1)}, s32[]{:S(2)}) async-start(s8[6291456]{0:T(1024)(128)(4,1)} %bitcast.6), calls=%async_computation.1 | async-start | bytes 8388608
  59.7 15.1 %copy-start.8 = (bf16[32,4224]{1,0:T(8,128)(2,1)S(1)}, bf16[32,4224]{1,0:T(8,128)(2,1)}, u32[]{:S(2)}) copy-start(bf16[32,4224]{1,0:T(8,128)(2,1)} %copy-done.7) | copy-start | bytes 811012
  59.7 15.1 %copy-start.14 = (bf16[32,4224]{1,0:T(8,128)(2,1)S(1)}, bf16[32,4224]{1,0:T(8,128)(2,1)}, u32[]{:S(2)}) copy-start(bf16[32,4224]{1,0:T(8,128)(2,1)} %copy-done.13) | copy-start | bytes 811012
  72.0 15.0 %copy-start.6 = (bf16[32,4224]{1,0:T(8,128)(2,1)S(1)}, bf16[32,4224]{1,0:T(8,128)(2,1)}, u32[]{:S(2)}) copy-start(bf16[32,4224]{1,0:T(8,128)(2,1)} %copy-done.5) | copy-start | bytes 811012
  72.1 15.0 %copy-start.12 = (bf16[32,4224]{1,0:T(8,128)(2,1)S(1)}, bf16[32,4224]{1,0:T(8,128)(2,1)}, u32[]{:S(2)}) copy-start(bf16[32,4224]{1,0:T(8,128)(2,1)} %copy-done.11) | copy-start | bytes 811012
  72.1 39.1 %collective-permute-start = (bf16[64,9344]{1,0:T(8,128)(2,1)S(1)}, bf16[64,9344]{1,0:T(8,128)(2,1)S(1)}, u32[]{:S(2)}, u32[]{:S(2)}) collective-permute-start(bf16[64,9344]{1,0:T(8,128)(2,1)S(1)} %reshape.14.q_mine.k_mine.v_mine.n_mine), channel_id=1, source_target_pairs={{0,1},{1,0},{2,3},{3,2},{4,5},{5,4},{6,7},{7,6},{8,9},{9,8},{10,11... | collective-permute-start | bytes 3588104 | tf_op jit(solution)/shard_map/ppermute | solution.py:314
  72.6 13.3 %collective-permute-start.30 = (bf16[32,4224]{1,0:T(8,128)(2,1)}, bf16[32,4224]{1,0:T(8,128)(2,1)S(1)}, u32[]{:S(2)}, u32[]{:S(2)}) collective-permute-start(bf16[32,4224]{1,0:T(8,128)(2,1)} %collective-permute-done.26.refs_1_), channel_id=1, source_target_pairs={{0,1},{1,0},{2,3},{3,2},{4,5},{5,4},{6,7},{7,6},{8,9},{9,8},{10,11... | collective-permute-start | bytes 811016 | tf_op jit(solution)/shard_map/ppermute | solution.py:314
  72.7 13.8 %collective-permute-start.31 = (bf16[32,4224]{1,0:T(8,128)(2,1)S(1)}, bf16[32,4224]{1,0:T(8,128)(2,1)S(1)}, u32[]{:S(2)}, u32[]{:S(2)}) collective-permute-start(bf16[32,4224]{1,0:T(8,128)(2,1)S(1)} %copy-done.10), channel_id=1, source_target_pairs={{0,1},{1,0},{2,3},{3,2},{4,5},{5,4},{6,7},{7,6},{8,9},{9,8},{10,11... | collective-permute-start | bytes 811016 | tf_op jit(solution)/shard_map/ppermute | solution.py:314
  73.1 13.4 %collective-permute-start.40 = (bf16[32,4224]{1,0:T(8,128)(2,1)}, bf16[32,4224]{1,0:T(8,128)(2,1)S(1)}, u32[]{:S(2)}, u32[]{:S(2)}) collective-permute-start(bf16[32,4224]{1,0:T(8,128)(2,1)} %collective-permute-done.38.refs_1_), channel_id=1, source_target_pairs={{0,4},{1,3},{2,6},{3,1},{4,0},{5,7},{6,2},{7,5},{8,12},{9,11},{10,... | collective-permute-start | bytes 811016 | tf_op jit(solution)/shard_map/ppermute | solution.py:302
  74.8 12.2 %collective-permute-start.32 = (bf16[32,4224]{1,0:T(8,128)(2,1)S(1)}, bf16[32,4224]{1,0:T(8,128)(2,1)S(1)}, u32[]{:S(2)}, u32[]{:S(2)}) collective-permute-start(bf16[32,4224]{1,0:T(8,128)(2,1)S(1)} %collective-permute-done.28.refs_3_), channel_id=1, source_target_pairs={{0,1},{1,0},{2,3},{3,2},{4,5},{5,4},{6,7},{7,6},{8,9},{9,8},{10,11... | collective-permute-start | bytes 811016 | tf_op jit(solution)/shard_map/ppermute | solution.py:314
  85.9 13.0 %copy-start.19 = (bf16[128,4096]{1,0:T(8,128)(2,1)S(1)}, bf16[128,4096]{1,0:T(8,128)(2,1)}, u32[]{:S(2)}) copy-start(bf16[128,4096]{1,0:T(8,128)(2,1)} %copy-done.18) | copy-start | bytes 3145732
  85.9 13.0 %collective-permute-start.41 = (bf16[32,4224]{1,0:T(8,128)(2,1)}, bf16[32,4224]{1,0:T(8,128)(2,1)S(1)}, u32[]{:S(2)}, u32[]{:S(2)}) collective-permute-start(bf16[32,4224]{1,0:T(8,128)(2,1)} %collective-permute-done.37.refs_0_), channel_id=1, source_target_pairs={{0,1},{1,0},{2,3},{3,2},{4,5},{5,4},{6,7},{7,6},{8,9},{9,8},{10,11... | collective-permute-start | bytes 811016 | tf_op jit(solution)/shard_map/ppermute | solution.py:314
  86.4 13.0 %collective-permute-start.42 = (bf16[32,4224]{1,0:T(8,128)(2,1)}, bf16[32,4224]{1,0:T(8,128)(2,1)S(1)}, u32[]{:S(2)}, u32[]{:S(2)}) collective-permute-start(bf16[32,4224]{1,0:T(8,128)(2,1)} %collective-permute-done.38.refs_1_), channel_id=1, source_target_pairs={{0,1},{1,0},{2,3},{3,2},{4,5},{5,4},{6,7},{7,6},{8,9},{9,8},{10,11... | collective-permute-start | bytes 811016 | tf_op jit(solution)/shard_map/ppermute | solution.py:314
  86.5 13.0 %collective-permute-start.43 = (bf16[32,4224]{1,0:T(8,128)(2,1)S(1)}, bf16[32,4224]{1,0:T(8,128)(2,1)S(1)}, u32[]{:S(2)}, u32[]{:S(2)}) collective-permute-start(bf16[32,4224]{1,0:T(8,128)(2,1)S(1)} %collective-permute-done.39.refs_2_), channel_id=1, source_target_pairs={{0,1},{1,0},{2,3},{3,2},{4,5},{5,4},{6,7},{7,6},{8,9},{9,8},{10,11... | collective-permute-start | bytes 811016 | tf_op jit(solution)/shard_map/ppermute | solution.py:314
  86.9 13.0 %collective-permute-start.44 = (bf16[32,4224]{1,0:T(8,128)(2,1)S(1)}, bf16[32,4224]{1,0:T(8,128)(2,1)S(1)}, u32[]{:S(2)}, u32[]{:S(2)}) collective-permute-start(bf16[32,4224]{1,0:T(8,128)(2,1)S(1)} %collective-permute-done.40.refs_3_), channel_id=1, source_target_pairs={{0,1},{1,0},{2,3},{3,2},{4,5},{5,4},{6,7},{7,6},{8,9},{9,8},{10,11... | collective-permute-start | bytes 811016 | tf_op jit(solution)/shard_map/ppermute | solution.py:314
  98.9 32.8 %collective-permute-start.10 = (bf16[128,4096]{1,0:T(8,128)(2,1)S(1)}, bf16[128,4096]{1,0:T(8,128)(2,1)S(1)}, u32[]{:S(2)}, u32[]{:S(2)}) collective-permute-start(bf16[128,4096]{1,0:T(8,128)(2,1)S(1)} %copy-done.19), channel_id=1, source_target_pairs={{0,1},{1,0},{2,3},{3,2},{4,5},{5,4},{6,7},{7,6},{8,9},{9,8},{10,11... | collective-permute-start | bytes 3145736 | tf_op jit(solution)/shard_map/ppermute | solution.py:314
  99.4 35.0 %collective-permute-start.21 = (bf16[128,4096]{1,0:T(8,128)(2,1)S(1)}, bf16[128,4096]{1,0:T(8,128)(2,1)}, u32[]{:S(2)}, u32[]{:S(2)}) collective-permute-start(bf16[128,4096]{1,0:T(8,128)(2,1)S(1)} %get-tuple-element.18), channel_id=1, source_target_pairs={{0,1},{1,0},{2,3},{3,2},{4,5},{5,4},{6,7},{7,6},{8,9},{9,8},{10,11... | collective-permute-start | bytes 3145736 | tf_op jit(solution)/shard_map/ppermute | solution.py:314
  99.5 11.7 %copy-start.17 = (bf16[2,1024,1024]{2,1,0:T(8,128)(2,1)S(1)}, bf16[2,1024,1024]{2,1,0:T(8,128)(2,1)}, u32[]{:S(2)}) copy-start(bf16[2,1024,1024]{2,1,0:T(8,128)(2,1)} %value_ref.3) | copy-start | bytes 12582916
  99.5 11.7 %copy-start.20 = (s32[4]{0:T(128)S(1)}, s32[4]{0:T(128)}, u32[]{:S(2)}) copy-start(s32[4]{0:T(128)} %lens_ref.3) | copy-start | bytes 52
  99.5 36.9 %collective-permute-start.33 = (bf16[128,4096]{1,0:T(8,128)(2,1)}, bf16[128,4096]{1,0:T(8,128)(2,1)}, u32[]{:S(2)}, u32[]{:S(2)}) collective-permute-start(bf16[128,4096]{1,0:T(8,128)(2,1)} %get-tuple-element.21), channel_id=1, source_target_pairs={{0,1},{1,0},{2,3},{3,2},{4,5},{5,4},{6,7},{7,6},{8,9},{9,8},{10,11... | collective-permute-start | bytes 3145736 | tf_op jit(solution)/shard_map/ppermute | solution.py:314
  111.0 28.6 %collective-permute-start.45 = (bf16[128,4096]{1,0:T(8,128)(2,1)S(1)}, bf16[128,4096]{1,0:T(8,128)(2,1)S(1)}, u32[]{:S(2)}, u32[]{:S(2)}) collective-permute-start(bf16[128,4096]{1,0:T(8,128)(2,1)S(1)} %get-tuple-element.24), channel_id=1, source_target_pairs={{0,1},{1,0},{2,3},{3,2},{4,5},{5,4},{6,7},{7,6},{8,9},{9,8},{10,11... | collective-permute-start | bytes 3145736 | tf_op jit(solution)/shard_map/ppermute | solution.py:314
  121.1 10.6 %copy-start.3 = (bf16[32,8192]{1,0:T(8,128)(2,1)}, bf16[32,8192]{1,0:T(8,128)(2,1)S(1)}, u32[]{:S(2)}) copy-start(bf16[32,8192]{1,0:T(8,128)(2,1)S(1)} %attend.3.mine_1) | copy-start | bytes 1572868
  121.1 59.5 %collective-permute-start.2 = (bf16[32,8192]{1,0:T(8,128)(2,1)S(1)}, bf16[32,8192]{1,0:T(8,128)(2,1)S(1)}, u32[]{:S(2)}, u32[]{:S(2)}) collective-permute-start(bf16[32,8192]{1,0:T(8,128)(2,1)S(1)} %attend.3.mine_1), channel_id=1, source_target_pairs={{0,1},{1,0},{2,3},{3,2},{4,5},{5,4},{6,7},{7,6},{8,9},{9,8},{10,11... | collective-permute-start | bytes 1572872 | tf_op jit(solution)/shard_map/ppermute | solution.py:314
  131.7 2.7 %copy-start.4 = (bf16[32,8192]{1,0:T(8,128)(2,1)}, bf16[32,8192]{1,0:T(8,128)(2,1)S(1)}, u32[]{:S(2)}) copy-start(bf16[32,8192]{1,0:T(8,128)(2,1)S(1)} %attend.2.mine_0) | copy-start | bytes 1572868
  132.8 50.1 %collective-permute-start.1 = (bf16[32,8192]{1,0:T(8,128)(2,1)S(1)}, bf16[32,8192]{1,0:T(8,128)(2,1)S(1)}, u32[]{:S(2)}, u32[]{:S(2)}) collective-permute-start(bf16[32,8192]{1,0:T(8,128)(2,1)S(1)} %attend.2.mine_0), channel_id=1, source_target_pairs={{0,1},{1,0},{2,3},{3,2},{4,5},{5,4},{6,7},{7,6},{8,9},{9,8},{10,11... | collective-permute-start | bytes 1572872 | tf_op jit(solution)/shard_map/ppermute | solution.py:314
  134.4 9.2 %collective-permute-start.11 = (bf16[64,4096]{1,0:T(8,128)(2,1)S(1)}, bf16[64,4096]{1,0:T(8,128)(2,1)S(1)}, u32[]{:S(2)}, u32[]{:S(2)}) collective-permute-start(bf16[64,4096]{1,0:T(8,128)(2,1)S(1)} %fusion.6), channel_id=1, source_target_pairs={{0,4},{1,3},{2,6},{3,1},{4,0},{5,7},{6,2},{7,5},{8,12},{9,11},{10,... | collective-permute-start | bytes 1572872 | tf_op jit(solution)/shard_map/ppermute | solution.py:302
  136.3 12.9 %collective-permute-start.22 = (bf16[64,4096]{1,0:T(8,128)(2,1)S(1)}, bf16[64,4096]{1,0:T(8,128)(2,1)S(1)}, u32[]{:S(2)}, u32[]{:S(2)}) collective-permute-start(bf16[64,4096]{1,0:T(8,128)(2,1)S(1)} %fusion.4), channel_id=1, source_target_pairs={{0,4},{1,3},{2,6},{3,1},{4,0},{5,7},{6,2},{7,5},{8,12},{9,11},{10,... | collective-permute-start | bytes 1572872 | tf_op jit(solution)/shard_map/ppermute | solution.py:302
  139.7 18.0 %collective-permute-start.34 = (bf16[64,4096]{1,0:T(8,128)(2,1)S(1)}, bf16[64,4096]{1,0:T(8,128)(2,1)S(1)}, u32[]{:S(2)}, u32[]{:S(2)}) collective-permute-start(bf16[64,4096]{1,0:T(8,128)(2,1)S(1)} %fusion.2), channel_id=1, source_target_pairs={{0,4},{1,3},{2,6},{3,1},{4,0},{5,7},{6,2},{7,5},{8,12},{9,11},{10,... | collective-permute-start | bytes 1572872 | tf_op jit(solution)/shard_map/ppermute | solution.py:302
  143.7 22.5 %collective-permute-start.46 = (bf16[64,4096]{1,0:T(8,128)(2,1)S(1)}, bf16[64,4096]{1,0:T(8,128)(2,1)S(1)}, u32[]{:S(2)}, u32[]{:S(2)}) collective-permute-start(bf16[64,4096]{1,0:T(8,128)(2,1)S(1)} %fusion), channel_id=1, source_target_pairs={{0,4},{1,3},{2,6},{3,1},{4,0},{5,7},{6,2},{7,5},{8,12},{9,11},{10,... | collective-permute-start | bytes 1572872 | tf_op jit(solution)/shard_map/ppermute | solution.py:302
  149.3 41.2 %collective-permute-start.12 = (bf16[32,4096]{1,0:T(8,128)(2,1)}, bf16[32,4096]{1,0:T(8,128)(2,1)S(1)}, u32[]{:S(2)}, u32[]{:S(2)}) collective-permute-start(bf16[32,4096]{1,0:T(8,128)(2,1)} %slice.133), channel_id=1, source_target_pairs={{0,2},{1,5},{2,0},{3,7},{4,6},{5,1},{6,4},{7,3},{8,10},{9,13},{10,... | collective-permute-start | bytes 786440 | tf_op jit(solution)/shard_map/ppermute | solution.py:302
  157.7 9.2 %collective-permute-start.23 = (bf16[32,4096]{1,0:T(8,128)(2,1)S(1)}, bf16[32,4096]{1,0:T(8,128)(2,1)S(1)}, u32[]{:S(2)}, u32[]{:S(2)}) collective-permute-start(bf16[32,4096]{1,0:T(8,128)(2,1)S(1)} %slice.132), channel_id=1, source_target_pairs={{0,2},{1,5},{2,0},{3,7},{4,6},{5,1},{6,4},{7,3},{8,10},{9,13},{10,... | collective-permute-start | bytes 786440 | tf_op jit(solution)/shard_map/ppermute | solution.py:302
  166.1 6.4 %collective-permute-start.35 = (bf16[32,4096]{1,0:T(8,128)(2,1)S(1)}, bf16[32,4096]{1,0:T(8,128)(2,1)S(1)}, u32[]{:S(2)}, u32[]{:S(2)}) collective-permute-start(bf16[32,4096]{1,0:T(8,128)(2,1)S(1)} %slice.131), channel_id=1, source_target_pairs={{0,2},{1,5},{2,0},{3,7},{4,6},{5,1},{6,4},{7,3},{8,10},{9,13},{10,... | collective-permute-start | bytes 786440 | tf_op jit(solution)/shard_map/ppermute | solution.py:302
  166.9 10.0 %collective-permute-start.47 = (bf16[32,4096]{1,0:T(8,128)(2,1)S(1)}, bf16[32,4096]{1,0:T(8,128)(2,1)S(1)}, u32[]{:S(2)}, u32[]{:S(2)}) collective-permute-start(bf16[32,4096]{1,0:T(8,128)(2,1)S(1)} %slice.130), channel_id=1, source_target_pairs={{0,2},{1,5},{2,0},{3,7},{4,6},{5,1},{6,4},{7,3},{8,10},{9,13},{10,... | collective-permute-start | bytes 786440 | tf_op jit(solution)/shard_map/ppermute | solution.py:302
  172.5 18.0 %collective-permute-start.24 = (bf16[32,4096]{1,0:T(8,128)(2,1)}, bf16[32,4096]{1,0:T(8,128)(2,1)S(1)}, u32[]{:S(2)}, u32[]{:S(2)}) collective-permute-start(bf16[32,4096]{1,0:T(8,128)(2,1)} %fusion.10), channel_id=1, source_target_pairs={{0,8},{1,9},{2,10},{3,11},{4,12},{5,13},{6,14},{7,15},{8,0},{9,1},... | collective-permute-start | bytes 786440 | tf_op jit(solution)/shard_map/ppermute | solution.py:302
  176.8 20.2 %collective-permute-start.36 = (bf16[32,4096]{1,0:T(8,128)(2,1)}, bf16[32,4096]{1,0:T(8,128)(2,1)S(1)}, u32[]{:S(2)}, u32[]{:S(2)}) collective-permute-start(bf16[32,4096]{1,0:T(8,128)(2,1)} %fusion.9), channel_id=1, source_target_pairs={{0,16},{1,17},{2,18},{3,19},{4,20},{5,21},{6,22},{7,23},{8,24},{9,... | collective-permute-start | bytes 786440 | tf_op jit(solution)/shard_map/ppermute | solution.py:302
  181.5 15.6 %collective-permute-start.48 = (bf16[32,4096]{1,0:T(8,128)(2,1)}, bf16[32,4096]{1,0:T(8,128)(2,1)S(1)}, u32[]{:S(2)}, u32[]{:S(2)}) collective-permute-start(bf16[32,4096]{1,0:T(8,128)(2,1)} %fusion.8), channel_id=1, source_target_pairs={{0,24},{1,25},{2,26},{3,27},{4,28},{5,29},{6,30},{7,31},{8,16},{9,... | collective-permute-start | bytes 786440 | tf_op jit(solution)/shard_map/ppermute | solution.py:302
  (11 other events, 9.1 us)

commit v3 on v2

--- a/solution.py
+++ b/solution.py
@@ -14,6 +14,7 @@
 TOP = 8
 GROUP = SAMP * STEPS
 LANES = 128
+BAND = 64
 LOG2E = 1.4426950408889634
 MIB = 1 << 20
 
@@ -73,8 +74,9 @@
 
 def attend_kernel(
     local, lens_ref, q_mine, q_other, k_mine, k_other, v_mine, v_other, n_mine, n_other,
-    key_ref, value_ref, out_ref
+    key_ref, value_ref, *refs
 ):
+    out_ref, q_ref, score_ref, weight_ref, total_ref = refs[-5:]
     number = lax.axis_index("fan") * 2 + local
     length = lens_ref[number]
     prompts = jnp.concatenate([n_mine[...], n_other[...]], axis=0).astype(jnp.float32)
@@ -89,22 +91,20 @@
         return dot(select, both, ((0,), (0,))).astype(jnp.bfloat16)
 
     queries = pick(q_mine, q_other)[:GROUP]
-    own_keys = pick(k_mine, k_other)
-    own_values = pick(v_mine, v_other)
-    keys, values = key_ref[0], value_ref[0]
-    span = keys.shape[0]
+    span = key_ref.shape[1]
     factor = HD**-0.5 * LOG2E
+    heads = queries.shape[1] // HD
+    for head in range(heads):
+        q_ref[head * GROUP : (head + 1) * GROUP] = queries[:, head * HD : (head + 1) * HD]
+    score_ref[:, :span] = dot(q_ref[...], key_ref[0], ((1,), (1,)))
+    score_ref[:, span:] = dot(q_ref[...], pick(k_mine, k_other), ((1,), (1,)))
     usable = lax.broadcasted_iota(jnp.int32, (1, span), 1) < length
     row = lax.broadcasted_iota(jnp.int32, (LANES, LANES), 0) % GROUP
     causal = (row // STEPS == lane // STEPS) & (lane <= row)
-    heads = queries.shape[1] // HD
-    together = LANES // GROUP
-    for base in range(0, heads, together):
-        block = jnp.concatenate(
-            [queries[:, (base + i) * HD : (base + i + 1) * HD] for i in range(together)], axis=0
-        )
-        scores = jnp.where(usable, dot(block, keys, ((1,), (1,))), -1e30)
-        own = jnp.where(causal, dot(block, own_keys, ((1,), (1,))), -1e30)
+    for base in range(0, heads * GROUP, BAND):
+        at = slice(base, base + BAND)
+        scores = jnp.where(usable, score_ref[at, :span], -1e30)
+        own = jnp.where(causal[:BAND], score_ref[at, span:], -1e30)
         highest = jnp.maximum(
             jnp.max(scores, axis=-1, keepdims=True), jnp.max(own, axis=-1, keepdims=True)
         )
@@ -113,27 +113,29 @@
         total = jnp.sum(raised, axis=-1, keepdims=True) + jnp.sum(
             own_raised, axis=-1, keepdims=True
         )
-        mixed = dot(raised.astype(jnp.bfloat16), values)
-        mixed = mixed + dot(own_raised.astype(jnp.bfloat16), own_values)
-        mixed = (mixed / total).astype(jnp.bfloat16)
-        for i in range(together):
-            out_ref[:, (base + i) * HD : (base + i + 1) * HD] = mixed[i * GROUP : (i + 1) * GROUP]
-
-
-def attend(local, lens, mine, other, cache):
-    rows = mine.shape[0]
+        weight_ref[at, :span] = raised.astype(jnp.bfloat16)
+        weight_ref[at, span:] = own_raised.astype(jnp.bfloat16)
+        total_ref[at] = jnp.broadcast_to(1.0 / total, (BAND, HD))
+    mixed = dot(weight_ref[:, :span], value_ref[0])
+    mixed = mixed + dot(weight_ref[:, span:], pick(v_mine, v_other))
+    mixed = (mixed * total_ref[...]).astype(jnp.bfloat16)
+    for head in range(heads):
+        out_ref[:, head * HD : (head + 1) * HD] = mixed[head * GROUP : (head + 1) * GROUP]
+
+
+def attend(local, lens, queries, own, cache, after):
+    rows, q_width = queries[0].shape
     span = cache.shape[1]
-    q_width = mine.shape[1] - 2 * KVH * HD - LANES
     head = q_width // KVH
-    first = q_width // HD
+    band = head // HD * GROUP
 
     def column(at):
         return pl.BlockSpec((rows, HD), at)
 
     q_spec = pl.BlockSpec((rows, head), lambda k: (0, k))
-    k_spec = column(lambda k: (0, first + k))
-    v_spec = column(lambda k: (0, first + KVH + k))
-    n_spec = column(lambda k: (0, first + 2 * KVH))
+    k_spec = column(lambda k: (0, k))
+    v_spec = column(lambda k: (0, KVH + k))
+    n_spec = column(lambda k: (0, 2 * KVH))
     return pl.pallas_call(
         functools.partial(attend_kernel, local),
         grid=(KVH,),
@@ -143,12 +145,19 @@
         + [
             pl.BlockSpec((1, span, HD), lambda k: (local, 0, k)),
             pl.BlockSpec((1, span, HD), lambda k: (local, 0, KVH + k)),
+        ]
+        + [pl.BlockSpec(memory_space=pl.ANY)] * len(after),
+        out_specs=pl.BlockSpec((GROUP, head), lambda k: (0, k)),
+        scratch_shapes=[
+            pltpu.VMEM((band, HD), jnp.bfloat16),
+            pltpu.VMEM((band, span + LANES), jnp.float32),
+            pltpu.VMEM((band, span + LANES), jnp.bfloat16),
+            pltpu.VMEM((band, HD), jnp.float32),
         ],
-        out_specs=pl.BlockSpec((GROUP, head), lambda k: (0, k)),
-        compiler_params=pltpu.CompilerParams(vmem_limit_bytes=32 * MIB),
+        compiler_params=pltpu.CompilerParams(vmem_limit_bytes=24 * MIB),
         cost_estimate=cost(5e9, 5 * MIB),
         name="attend",
-    )(lens, mine, other, mine, other, mine, other, mine, other, cache, cache)
+    )(lens, *queries, *own, *own, *own, cache, cache, *after)
 
 
 def place_kernel(n_mine, mine_0, mine_1, other_0, other_1, out_ref):
@@ -191,8 +200,8 @@
 
 def expert_kernel(pieces, *refs):
     xs, (gate, up, down) = refs[:pieces], refs[pieces : pieces + 3]
-    keep, send, other = refs[pieces + 3 : pieces + 6]
-    x, w_gate, w_up, w_down, units, x_sem, g_sem, u_sem, d_sem = refs[pieces + 6 :]
+    keep, send, other = refs[-12:-9]
+    x, w_gate, w_up, w_down, units, x_sem, g_sem, u_sem, d_sem = refs[-9:]
     width, hidden = gate.shape
     piece_rows = xs[0].shape[0]
     step = 256
@@ -243,12 +252,13 @@
         other[:, at] = result[half:]
 
 
-def expert_chunk(pieces, gate, up, down):
+def expert_chunk(pieces, gate, up, down, after):
     count = len(pieces)
     piece_rows, message = pieces[0].shape
     width, hidden = gate.shape
     rows = count * piece_rows
     anywhere = pl.BlockSpec(memory_space=pl.ANY)
+    stored = pl.BlockSpec(memory_space=pltpu.HBM)
     whole = pl.BlockSpec(memory_space=pltpu.VMEM)
     return pl.pallas_call(
         functools.partial(expert_kernel, count),
@@ -257,7 +267,7 @@
             jax.ShapeDtypeStruct((rows // 4, width), jnp.bfloat16),
             jax.ShapeDtypeStruct((rows // 2, width), jnp.bfloat16),
         ),
-        in_specs=[anywhere] * (count + 3),
+        in_specs=[stored] * (count + 3) + [anywhere] * len(after),
         out_specs=(whole, whole, whole),
         scratch_shapes=[
             pltpu.VMEM((rows, message), jnp.bfloat16),
@@ -273,7 +283,7 @@
         compiler_params=pltpu.CompilerParams(vmem_limit_bytes=40 * MIB),
         cost_estimate=cost(6 * rows * width * hidden, 6 * width * hidden),
         name="expert_chunk",
-    )(*pieces, gate, up, down)
+    )(*pieces, gate, up, down, *after)
 
 
 def on_device(
@@ -291,7 +301,6 @@
     w_down,
 ):
     chips = lax.axis_size("ep")
-    layers = chips // 4
     count, _, q_width = queries.shape
     rows = count * STEPS
 
@@ -314,34 +323,72 @@
         return lax.ppermute(value, "fan", [(0, 1), (1, 0)])
 
     token = norm_message(hidden, norm_gain, route_ids, route_logits)
-    arrived = [token] + [far(token, layer) for layer in range(1, layers)]
-
-    marks = jnp.broadcast_to(sample_prompt.astype(jnp.bfloat16)[:, None, None], (count, STEPS, LANES))
-    mine = jnp.concatenate([queries, new_kv, marks], axis=2).reshape(rows, -1)
-    other = beside(mine)
-    context_mine = [attend(local, prompt_lens, mine, other, prompt_kv) for local in range(2)]
-    context_other = [beside(value) for value in context_mine]
-    context = place_context(mine, context_mine, context_other).reshape(count, STEPS, q_width)
-
-    parts = []
-    for layer in range(layers):
+    opposite = far(token, 2)
+    arrived = {0: token, 1: far(token, 1), 2: opposite, 3: far(opposite, 1)}
+    pieces = {}
+    for layer in (0, 1, 3, 2):
         own = arrived[layer]
         first = near(own)
-        pieces = [own, first, cross(own), cross(first)]
-        pieces = pieces + [beside(piece) for piece in pieces]
-        keep, send, away = expert_chunk(pieces, w_gate[0], w_up[0], w_down[0])
-        back = beside(away).astype(jnp.float32)
+        four = [own, first, cross(own), cross(first)]
+        pieces[layer] = four + [beside(piece) for piece in four]
+
+    marks = jnp.broadcast_to(sample_prompt.astype(jnp.bfloat16)[:, None, None], (count, STEPS, LANES))
+    q_mine = queries.reshape(rows, q_width)
+    own_mine = jnp.concatenate([new_kv, marks], axis=2).reshape(rows, -1)
+    q_both = (q_mine, beside(q_mine))
+    own_both = (own_mine, beside(own_mine))
+
+    def expert(layer, *after):
+        return expert_chunk(pieces[layer], w_gate[0], w_up[0], w_down[0], after)
+
+    def add_cores(result):
+        keep, send, away = result
+        back = beside(away)
         half = send.shape[0]
+        there = (send.astype(jnp.float32) + back[half:].astype(jnp.float32)).astype(jnp.bfloat16)
+        return keep, back, there
+
+    def add_cross(keep, back, there):
+        half = keep.shape[0]
         single = half // 2
-        there = (send.astype(jnp.float32) + back[half:]).astype(jnp.bfloat16)
         turned = cross(there).astype(jnp.float32)
-        held = keep.astype(jnp.float32) + back[:half] + turned
-        last = near(held[single:].astype(jnp.bfloat16)).astype(jnp.float32)
-        reached = held[:single] + last
-        if layer:
-            reached = far(reached.astype(jnp.bfloat16), layer).astype(jnp.float32)
-        parts.append(reached)
-    expert_out = functools.reduce(jnp.add, parts).astype(jnp.bfloat16)
+        held = keep.astype(jnp.float32) + back[:half].astype(jnp.float32) + turned
+        return held[:single], held[single:].astype(jnp.bfloat16)
+
+    def add_near(held, passed):
+        return held + near(passed).astype(jnp.float32)
+
+    def add_far(total, layer):
+        return far(total.astype(jnp.bfloat16), layer).astype(jnp.float32)
+
+    context_0 = attend(0, prompt_lens, q_both, own_both, prompt_kv, ())
+    result_1 = expert(1, context_0, *pieces[0][1:4], *pieces[3][1:3])
+    result_3 = expert(3, result_1[0], *pieces[2][1:4])
+    cores_1 = add_cores(result_1)
+    result_2 = expert(2, result_3[0], cores_1[2])
+    cores_3 = add_cores(result_3)
+    cross_1 = add_cross(*cores_1)
+    result_0 = expert(0, result_2[0], cores_3[2], cross_1[1])
+    cores_2 = add_cores(result_2)
+    cross_3 = add_cross(*cores_3)
+    near_1 = add_near(*cross_1)
+    far_1 = add_far(near_1, 1)
+    context_1 = attend(
+        1, prompt_lens, q_both, own_both, prompt_kv, (result_0[0], cores_2[2], cross_3[1])
+    )
+    cores_0 = add_cores(result_0)
+    cross_2 = add_cross(*cores_2)
+    near_3 = add_near(*cross_3)
+    far_3 = add_far(near_3, 1)
+    cross_0 = add_cross(*cores_0)
+    near_2 = add_near(*cross_2)
+    far_2 = add_far(near_2 + far_3, 2)
+    near_0 = add_near(*cross_0)
+    expert_out = (near_0 + far_1 + far_2).astype(jnp.bfloat16)
+
+    context_mine = [context_0, context_1]
+    context_other = [beside(value) for value in context_mine]
+    context = place_context(own_mine, context_mine, context_other).reshape(count, STEPS, q_width)
     return (context, expert_out)
 
 

time: 200 us -> 173 us (0.86)
  waiting for transfers between devices: 54 us -> 46.1 us
  local copies, waits for them, and re-layouts: 18.2 us -> 11.3 us
  Pallas kernels: 71.6 us -> 66.8 us
  other arithmetic: 12.4 us -> 8.75 us
  starting transfers between devices: 40.6 us -> 38.2 us
    ppermute x26, waiting for transfers between devices: 54 us -> 45.2 us  [swap(): return lax.ppermute(value, ('ep', 'fan'), pairs)]
    unnamed x52 -> x30, local copies, waits for them, and re-layouts: 11.9 us -> 5.73 us
    convert_element_type x12 -> x8, other arithmetic: 7.98 us -> 4.28 us  [the longest x1 1.85 us: on_device(): expert_out = (near_0 + far_1 + far_2).astype(jnp.bfloat16)]
    ppermute x26, starting transfers between devices: 36.2 us -> 33.3 us  [swap(): return lax.ppermute(value, ('ep', 'fan'), pairs)]
    pallas_call x2, Pallas kernels: 20 us -> 17.4 us  [attend(): pl.pallas_call(functools.partial(attend_kernel, local), grid=(KVH,), out_...]
    pallas_call x4, Pallas kernels: 45.3 us -> 43.1 us  [expert_chunk(): pl.pallas_call(functools.partial(expert_kernel, count), out_shape=(jax.Sh...]
    add x4, other arithmetic: 0.56 us -> 2.78 us  [add_cross(): held = keep.astype(jnp.float32) + back[:half].astype(jnp.float32) + turned]
    concatenate x1, other arithmetic: 3.15 us -> 1.04 us  [on_device(): own_mine = jnp.concatenate([new_kv, marks], axis=2).reshape(rows, -1)]
  transfers between devices with their start and end apart: 49 -> 50, of which waited for: 12 -> 11; matrix products, arithmetic and copies ran while one was open for 8% -> 6% of each run, Pallas kernels for 35% -> 39%
where the time goes in v3:
time: 173 us; the launch traced here: 172 us
  Pallas kernels  66.8 us (39%)
  waiting for transfers between devices  46.1 us (27%)
  starting transfers between devices  38.2 us (22%)
  local copies, waits for them, and re-layouts  11.3 us (7%)
  other arithmetic  8.75 us (5%)
    ppermute x26, waiting for transfers between devices, swap(): return lax.ppermute(value, ('ep', 'fan'), pairs)  45.2 us
    pallas_call x4, Pallas kernels, expert_chunk(): pl.pallas_call(functools.partial(expert_kernel, count), out_shape=(jax.Sh...  43.1 us
    ppermute x26, starting transfers between devices, swap(): return lax.ppermute(value, ('ep', 'fan'), pairs)  33.3 us
    pallas_call x2, Pallas kernels, attend(): pl.pallas_call(functools.partial(attend_kernel, local), grid=(KVH,), out_...  17.4 us
    unnamed x30, local copies, waits for them, and re-layouts  5.73 us
    ppermute x24, starting transfers between devices, beside(): return lax.ppermute(value, 'fan', [(0, 1), (1, 0)])  4.83 us
    pallas_call x1, Pallas kernels, place_context(): pl.pallas_call(place_kernel, grid=(q_width // width,), out_shape=jax.Shap...  4.35 us
  transfers between devices with their start and end apart: 50, of which 11 were waited for; matrix products, arithmetic and copies ran while one was open for 6% of the time, Pallas kernels for 39%

profile of v3, /device:TPU:0, one launch (start us, length us, event | category | flops | bytes accessed | tf_op | source)
XLA Modules:
  0.0 172.1 jit_solution(5770474657640082196)
XLA Ops:
  0.6 1.5 reshape.18.q_mine
  2.1 0.5 collective-permute-start
  2.6 1.3 reshape.19.gain_ref
  3.9 1.9 %norm_message.1.refs_0_ = bf16[32,4224]{1,0:T(8,128)(2,1)} custom-call(bf16[32,4096]{1,0:T(8,128)(2,1)} %hidden_ref.1, bf16[1,4096]{1,0:T(2,128)(2,1)} %reshape.19.gain_ref, s32[8,32]{1,0:T(8,128)} %bitcast.19, f32[8,32]{1,0:T(8,128)} %bitcast.20), custom_call_target="tpu_custom_call" | custom-call | flops 1000000 | bytes 524288 | tf_op jit(solution)/shard_map/norm_message/pallas_call | solution.py:60
  5.8 3.6 %collective-permute-start.9 = (bf16[32,4224]{1,0:T(8,128)(2,1)}, bf16[32,4224]{1,0:T(8,128)(2,1)}, u32[]{:S(2)}, u32[]{:S(2)}) collective-permute-start(bf16[32,4224]{1,0:T(8,128)(2,1)} %norm_message.1.refs_0_), channel_id=1, source_target_pairs={{0,16},{1,17},{2,18},{3,19},{4,20},{5,21},{6,22},{7,23},{8,24},{9,... | collective-permute-start | bytes 811016 | tf_op jit(solution)/shard_map/ppermute | solution.py:311
  9.5 1.6 collective-permute-start.25
  11.1 0.7 convert_element_type.112
  11.8 1.0 pad_maximum_fusion
  13.1 1.6 collective-permute-start.2
  14.6 1.5 collective-permute-start.3
  16.1 6.7 %collective-permute-done.9.refs_0_ = bf16[32,4224]{1,0:T(8,128)(2,1)} collective-permute-done((bf16[32,4224]{1,0:T(8,128)(2,1)}, bf16[32,4224]{1,0:T(8,128)(2,1)}, u32[]{:S(2)}, u32[]{:S(2)}) %collective-permute-start.9) | collective-permute-done | bytes 270368 | tf_op jit(solution)/shard_map/ppermute | solution.py:311
  22.8 0.6 collective-permute-start.17
  23.4 1.5 collective-permute-start.26
  24.9 1.5 collective-permute-start.4
  26.4 0.5 collective-permute-start.27
  26.9 4.3 %collective-permute-done.17.refs_0_ = bf16[32,4224]{1,0:T(8,128)(2,1)S(1)} collective-permute-done((bf16[32,4224]{1,0:T(8,128)(2,1)}, bf16[32,4224]{1,0:T(8,128)(2,1)S(1)}, u32[]{:S(2)}, u32[]{:S(2)}) %collective-permute-start.17) | collective-permute-done | bytes 270368 | tf_op jit(solution)/shard_map/ppermute | solution.py:311
  31.2 1.8 %collective-permute-done.26.refs_1_ = bf16[32,4224]{1,0:T(8,128)(2,1)S(1)} collective-permute-done((bf16[32,4224]{1,0:T(8,128)(2,1)}, bf16[32,4224]{1,0:T(8,128)(2,1)S(1)}, u32[]{:S(2)}, u32[]{:S(2)}) %collective-permute-start.26) | collective-permute-done | bytes 270368 | tf_op jit(solution)/shard_map/ppermute | solution.py:311
  33.0 1.5 collective-permute-start.28
  34.5 1.5 collective-permute-start.18
  36.0 0.5 collective-permute-start.19
  36.8 4.4 %collective-permute-done.28.refs_3_ = bf16[32,4224]{1,0:T(8,128)(2,1)S(1)} collective-permute-done((bf16[32,4224]{1,0:T(8,128)(2,1)S(1)}, bf16[32,4224]{1,0:T(8,128)(2,1)S(1)}, u32[]{:S(2)}, u32[]{:S(2)}) %collective-permute-start.28) | collective-permute-done | bytes 270368 | tf_op jit(solution)/shard_map/ppermute | solution.py:311
  41.2 0.5 collective-permute-start.32
  41.7 1.2 copy-done.3
  42.9 2.2 %copy-done.7 = bf16[2,1024,1024]{2,1,0:T(8,128)(2,1)S(1)} copy-done((bf16[2,1024,1024]{2,1,0:T(8,128)(2,1)S(1)}, bf16[2,1024,1024]{2,1,0:T(8,128)(2,1)}, u32[]{:S(2)}) %copy-start.7) | copy-done | bytes 4194328
  45.1 0.7 copy-done.9
  45.8 8.7 %attend.2.refs_11_.mine_0 = bf16[32,8192]{1,0:T(8,128)(2,1)S(1)} custom-call(s32[4]{0:T(128)S(1)} %copy-done.9, bf16[64,8192]{1,0:T(8,128)(2,1)S(1)} %copy-done.3, bf16[64,8192]{1,0:T(8,128)(2,1)} %collective-permute-done.q_other, bf16[64,1152]{1,0:T(8,128)(2,1)S(1)} %reshape.17.k_mine.v_mine.n_mine, ...), custom_call_target="tpu_custom_call" | custom-call | flops 5000000000 | bytes 5242880 | tf_op jit(solution)/shard_map/attend/pallas_call | solution.py:139
  54.5 1.6 collective-permute-start.10
  56.1 10.8 %expert_chunk.4 = (bf16[64,4096]{1,0:T(8,128)(2,1)S(1)}, bf16[64,4096]{1,0:T(8,128)(2,1)S(1)}, bf16[128,4096]{1,0:T(8,128)(2,1)S(1)}) custom-call(bf16[32,4224]{1,0:T(8,128)(2,1)} %collective-permute-done.25.refs_0_, bf16[32,4224]{1,0:T(8,128)(2,1)S(1)} %collective-permute-done.26.refs_1_, bf16[32,4224]{1,0:T(8,128)(2,1)S(1)} %collective-permute-done.27.refs_2_, ...), custom_call_target="tpu_custom_call" | custom-call | flops 4831838208 | bytes 18874368 | tf_op jit(solution)/shard_map/expert_chunk/pallas_call | solution.py:263
  67.0 0.9 collective-permute-start.11
  67.9 1.2 collective-permute-start.12
  69.1 0.8 collective-permute-start.20
  69.9 3.8 %collective-permute-done.11.refs_13_.refs_2_ = bf16[32,4224]{1,0:T(8,128)(2,1)S(1)} collective-permute-done((bf16[32,4224]{1,0:T(8,128)(2,1)}, bf16[32,4224]{1,0:T(8,128)(2,1)S(1)}, u32[]{:S(2)}, u32[]{:S(2)}) %collective-permute-start.11) | collective-permute-done | bytes 270368 | tf_op jit(solution)/shard_map/ppermute | solution.py:311
  73.8 2.9 %collective-permute-done.12.refs_14_.refs_3_ = bf16[32,4224]{1,0:T(8,128)(2,1)S(1)} collective-permute-done((bf16[32,4224]{1,0:T(8,128)(2,1)S(1)}, bf16[32,4224]{1,0:T(8,128)(2,1)S(1)}, u32[]{:S(2)}, u32[]{:S(2)}) %collective-permute-start.12) | collective-permute-done | bytes 270368 | tf_op jit(solution)/shard_map/ppermute | solution.py:311
  76.7 2.9 %collective-permute-done.20.refs_3_ = bf16[32,4224]{1,0:T(8,128)(2,1)S(1)} collective-permute-done((bf16[32,4224]{1,0:T(8,128)(2,1)S(1)}, bf16[32,4224]{1,0:T(8,128)(2,1)S(1)}, u32[]{:S(2)}, u32[]{:S(2)}) %collective-permute-start.20) | collective-permute-done | bytes 270368 | tf_op jit(solution)/shard_map/ppermute | solution.py:311
  79.6 0.5 collective-permute-start.13
  80.6 0.8 collective-permute-done.24.refs_7_
  81.5 10.7 %expert_chunk.5 = (bf16[64,4096]{1,0:T(8,128)(2,1)S(1)}, bf16[64,4096]{1,0:T(8,128)(2,1)S(1)}, bf16[128,4096]{1,0:T(8,128)(2,1)S(1)}) custom-call(bf16[32,4224]{1,0:T(8,128)(2,1)S(1)} %collective-permute-done.17.refs_0_, bf16[32,4224]{1,0:T(8,128)(2,1)S(1)} %collective-permute-done.18.refs_15_.refs_1_, ...), custom_call_target="tpu_custom_call" | custom-call | flops 4831838208 | bytes 18874368 | tf_op jit(solution)/shard_map/expert_chunk/pallas_call | solution.py:263
  93.9 10.8 %expert_chunk.6 = (bf16[64,4096]{1,0:T(8,128)(2,1)S(1)}, bf16[64,4096]{1,0:T(8,128)(2,1)S(1)}, bf16[128,4096]{1,0:T(8,128)(2,1)S(1)}) custom-call(bf16[32,4224]{1,0:T(8,128)(2,1)} %collective-permute-done.9.refs_0_, bf16[32,4224]{1,0:T(8,128)(2,1)S(1)} %collective-permute-done.10.refs_12_.refs_1_, ...), custom_call_target="tpu_custom_call" | custom-call | flops 4831838208 | bytes 18874368 | tf_op jit(solution)/shard_map/expert_chunk/pallas_call | solution.py:263
  104.8 0.9 collective-permute-start.35
  105.8 8.2 %collective-permute-done.35 = bf16[64,4096]{1,0:T(8,128)(2,1)S(1)} collective-permute-done((bf16[64,4096]{1,0:T(8,128)(2,1)S(1)}, bf16[64,4096]{1,0:T(8,128)(2,1)S(1)}, u32[]{:S(2)}, u32[]{:S(2)}) %collective-permute-start.35) | collective-permute-done | bytes 524320 | tf_op jit(solution)/shard_map/ppermute | solution.py:311
  114.2 0.6 collective-permute-start.36
  114.8 0.8 collective-permute-start.37
  115.6 1.2 collective-permute-start.43
  116.9 10.8 %expert_chunk.7 = (bf16[64,4096]{1,0:T(8,128)(2,1)S(1)}, bf16[64,4096]{1,0:T(8,128)(2,1)S(1)}, bf16[128,4096]{1,0:T(8,128)(2,1)S(1)}) custom-call(bf16[32,4224]{1,0:T(8,128)(2,1)S(1)} %copy-done.1, bf16[32,4224]{1,0:T(8,128)(2,1)S(1)} %collective-permute-done.2.refs_12_.refs_1_, bf16[32,4224]{1,0:T(8,128)(2,1)S(1)} %collective-permute-done.3.refs_13_.refs_2_, ...), custom_call_target="tpu_custom_call" | custom-call | flops 4831838208 | bytes 18874368 | tf_op jit(solution)/shard_map/expert_chunk/pallas_call | solution.py:263
  127.7 0.8 fusion.3
  128.5 1.0 collective-permute-start.44
  129.5 1.2 convert_add_fusion.2
  130.8 0.8 collective-permute-start.47
  131.6 1.2 add_convert_fusion.1.refs_1_
  132.8 1.0 collective-permute-start.45
  133.8 8.7 %attend.3.mine_1 = bf16[32,8192]{1,0:T(8,128)(2,1)S(1)} custom-call(s32[4]{0:T(128)S(1)} %copy-done.10, bf16[64,8192]{1,0:T(8,128)(2,1)S(1)} %copy-done.4, bf16[64,8192]{1,0:T(8,128)(2,1)} %collective-permute-done.q_other, bf16[64,1152]{1,0:T(8,128)(2,1)S(1)} %reshape.17.k_mine.v_mine.n_mine, ...), custom_call_target="tpu_custom_call" | custom-call | flops 5000000000 | bytes 5242880 | tf_op jit(solution)/shard_map/attend/pallas_call | solution.py:139
  142.7 1.4 collective-permute-start.48
  144.1 1.2 convert_add_fusion
  145.3 0.6 collective-permute-start.46
  146.1 5.4 %collective-permute-done.48 = bf16[32,4096]{1,0:T(8,128)(2,1)S(1)} collective-permute-done((bf16[32,4096]{1,0:T(8,128)(2,1)S(1)}, bf16[32,4096]{1,0:T(8,128)(2,1)S(1)}, u32[]{:S(2)}, u32[]{:S(2)}) %collective-permute-start.48) | collective-permute-done | bytes 262176 | tf_op jit(solution)/shard_map/ppermute | solution.py:311
  151.5 1.1 collective-permute-start.41
  152.7 3.2 %collective-permute-start.49 = (bf16[32,4096]{1,0:T(8,128)(2,1)S(1)}, bf16[32,4096]{1,0:T(8,128)(2,1)}, u32[]{:S(2)}, u32[]{:S(2)}) collective-permute-start(bf16[32,4096]{1,0:T(8,128)(2,1)S(1)} %fusion.2), channel_id=1, source_target_pairs={{0,16},{1,17},{2,18},{3,19},{4,20},{5,21},{6,22},{7,23},{8,24},{9,... | collective-permute-start | bytes 786440 | tf_op jit(solution)/shard_map/ppermute | solution.py:311
  155.9 4.8 %collective-permute-done.41 = bf16[64,4096]{1,0:T(8,128)(2,1)S(1)} collective-permute-done((bf16[64,4096]{1,0:T(8,128)(2,1)S(1)}, bf16[64,4096]{1,0:T(8,128)(2,1)S(1)}, u32[]{:S(2)}, u32[]{:S(2)}) %collective-permute-start.41) | collective-permute-done | bytes 524320 | tf_op jit(solution)/shard_map/ppermute | solution.py:311
  160.9 0.9 collective-permute-start.42
  161.8 0.8 copy-done.11
  162.6 0.8 copy-done.12
  163.4 4.4 %place_context.1 = bf16[64,8192]{1,0:T(8,128)(2,1)} custom-call(bf16[64,1152]{1,0:T(8,128)(2,1)} %copy-done.5, bf16[32,8192]{1,0:T(8,128)(2,1)} %copy-done, bf16[32,8192]{1,0:T(8,128)(2,1)} %copy-done.6, bf16[32,8192]{1,0:T(8,128)(2,1)} %copy-done.11, bf16[32,8192]{1,0:T(8,128)(2,1)} %copy-done.12), custom_call_target="tpu_custom_call" | custom-call | flops 100000000 | bytes 3145728 | tf_op jit(solution)/shard_map/place_context/pallas_call | solution.py:190
  167.7 2.5 %reshape.20 = bf16[32,2,8192]{2,1,0:T(2,128)(2,1)} reshape(bf16[64,8192]{1,0:T(8,128)(2,1)} %place_context.1) | data formatting | bytes 2097152 | tf_op jit(solution)/shard_map/reshape | solution.py:391
  170.3 1.8 %fusion.6 = bf16[32,4096]{1,0:T(8,128)(2,1)} fusion(f32[64,4096]{1,0:T(8,128)S(1)} %convert_add_fusion.1, bf16[32,4096]{1,0:T(8,128)(2,1)} %collective-permute-done.49, bf16[32,4096]{1,0:T(8,128)(2,1)} %collective-permute-done.44, bf16[32,4096]{1,0:T(8,128)(2,1)S(1)} %collective-permute-done.42), kind=kLoop, calls=%fused_computation.20 | loop fusion | flops 917504 | bytes 1572864 | tf_op jit(solution)/shard_map/convert_element_type | solution.py:387
  (98 shorter events, 4.0 us)
Async XLA Ops:
  2.1 39.1 %copy-start.2 = (bf16[64,8192]{1,0:T(8,128)(2,1)}, bf16[64,8192]{1,0:T(8,128)(2,1)S(1)}, u32[]{:S(2)}) copy-start(bf16[64,8192]{1,0:T(8,128)(2,1)S(1)} %reshape.18.q_mine) | copy-start | bytes 3145732
  2.1 39.1 %collective-permute-start = (bf16[64,8192]{1,0:T(8,128)(2,1)S(1)}, bf16[64,8192]{1,0:T(8,128)(2,1)}, u32[]{:S(2)}, u32[]{:S(2)}) collective-permute-start(bf16[64,8192]{1,0:T(8,128)(2,1)S(1)} %reshape.18.q_mine), channel_id=1, source_target_pairs={{0,1},{1,0},{2,3},{3,2},{4,5},{5,4},{6,7},{7,6},{8,9},{9,8},{10,11... | collective-permute-start | bytes 3145736 | tf_op jit(solution)/shard_map/ppermute | solution.py:323
  5.8 17.0 %collective-permute-start.9 = (bf16[32,4224]{1,0:T(8,128)(2,1)}, bf16[32,4224]{1,0:T(8,128)(2,1)}, u32[]{:S(2)}, u32[]{:S(2)}) collective-permute-start(bf16[32,4224]{1,0:T(8,128)(2,1)} %norm_message.1.refs_0_), channel_id=1, source_target_pairs={{0,16},{1,17},{2,18},{3,19},{4,20},{5,21},{6,22},{7,23},{8,24},{9,... | collective-permute-start | bytes 811016 | tf_op jit(solution)/shard_map/ppermute | solution.py:311
  9.5 13.9 %collective-permute-start.25 = (bf16[32,4224]{1,0:T(8,128)(2,1)}, bf16[32,4224]{1,0:T(8,128)(2,1)}, u32[]{:S(2)}, u32[]{:S(2)}) collective-permute-start(bf16[32,4224]{1,0:T(8,128)(2,1)} %norm_message.1.refs_0_), channel_id=1, source_target_pairs={{0,8},{1,9},{2,10},{3,11},{4,12},{5,13},{6,14},{7,15},{8,0},{9,1},... | collective-permute-start | bytes 811016 | tf_op jit(solution)/shard_map/ppermute | solution.py:311
  12.9 43.2 %slice-start = ((s8[6291456]{0:T(1024)(128)(4,1)}), s8[2097152]{0:T(1024)(128)(4,1)S(1)}, s32[]{:S(2)}) async-start(s8[6291456]{0:T(1024)(128)(4,1)} %bitcast.5), calls=%async_computation | async-start | bytes 4194304
  13.0 120.9 %copy-start.5 = (bf16[64,1152]{1,0:T(8,128)(2,1)}, bf16[64,1152]{1,0:T(8,128)(2,1)S(1)}, u32[]{:S(2)}) copy-start(bf16[64,1152]{1,0:T(8,128)(2,1)S(1)} %reshape.17.k_mine.v_mine.n_mine) | copy-start | bytes 442372
  13.0 43.1 %slice-start.1 = ((s8[6291456]{0:T(1024)(128)(4,1)}), s8[4194304]{0:T(1024)(128)(4,1)S(1)}, s32[]{:S(2)}) async-start(s8[6291456]{0:T(1024)(128)(4,1)} %bitcast.5), calls=%async_computation.1 | async-start | bytes 8388608
  13.0 1.6 collective-permute-start.1
  13.1 11.9 %collective-permute-start.2 = (bf16[32,4224]{1,0:T(8,128)(2,1)}, bf16[32,4224]{1,0:T(8,128)(2,1)S(1)}, u32[]{:S(2)}, u32[]{:S(2)}) collective-permute-start(bf16[32,4224]{1,0:T(8,128)(2,1)} %norm_message.1.refs_0_), channel_id=1, source_target_pairs={{0,2},{1,5},{2,0},{3,7},{4,6},{5,1},{6,4},{7,3},{8,10},{9,13},{10,... | collective-permute-start | bytes 811016 | tf_op jit(solution)/shard_map/ppermute | solution.py:311
  14.6 11.8 %collective-permute-start.3 = (bf16[32,4224]{1,0:T(8,128)(2,1)}, bf16[32,4224]{1,0:T(8,128)(2,1)S(1)}, u32[]{:S(2)}, u32[]{:S(2)}) collective-permute-start(bf16[32,4224]{1,0:T(8,128)(2,1)} %norm_message.1.refs_0_), channel_id=1, source_target_pairs={{0,4},{1,3},{2,6},{3,1},{4,0},{5,7},{6,2},{7,5},{8,12},{9,11},{10,... | collective-permute-start | bytes 811016 | tf_op jit(solution)/shard_map/ppermute | solution.py:311
  22.8 8.4 %collective-permute-start.17 = (bf16[32,4224]{1,0:T(8,128)(2,1)}, bf16[32,4224]{1,0:T(8,128)(2,1)S(1)}, u32[]{:S(2)}, u32[]{:S(2)}) collective-permute-start(bf16[32,4224]{1,0:T(8,128)(2,1)} %collective-permute-done.9.refs_0_), channel_id=1, source_target_pairs={{0,8},{1,9},{2,10},{3,11},{4,12},{5,13},{6,14},{7,15},{8,0},{9,1},... | collective-permute-start | bytes 811016 | tf_op jit(solution)/shard_map/ppermute | solution.py:311
  23.4 9.6 %collective-permute-start.26 = (bf16[32,4224]{1,0:T(8,128)(2,1)}, bf16[32,4224]{1,0:T(8,128)(2,1)S(1)}, u32[]{:S(2)}, u32[]{:S(2)}) collective-permute-start(bf16[32,4224]{1,0:T(8,128)(2,1)} %collective-permute-done.25.refs_0_), channel_id=1, source_target_pairs={{0,2},{1,5},{2,0},{3,7},{4,6},{5,1},{6,4},{7,3},{8,10},{9,13},{10,... | collective-permute-start | bytes 811016 | tf_op jit(solution)/shard_map/ppermute | solution.py:311
  24.9 9.6 %collective-permute-start.4 = (bf16[32,4224]{1,0:T(8,128)(2,1)S(1)}, bf16[32,4224]{1,0:T(8,128)(2,1)S(1)}, u32[]{:S(2)}, u32[]{:S(2)}) collective-permute-start(bf16[32,4224]{1,0:T(8,128)(2,1)S(1)} %collective-permute-done.2.refs_12_.refs_1_), channel_id=1, source_target_pairs={{0,4},{1,3},{2,6},{3,1},{4,0},{5,7},{6,2},{7,5},{8,12},{9,11},{10,... | collective-permute-start | bytes 811016 | tf_op jit(solution)/shard_map/ppermute | solution.py:311
  26.4 9.6 %collective-permute-start.27 = (bf16[32,4224]{1,0:T(8,128)(2,1)}, bf16[32,4224]{1,0:T(8,128)(2,1)S(1)}, u32[]{:S(2)}, u32[]{:S(2)}) collective-permute-start(bf16[32,4224]{1,0:T(8,128)(2,1)} %collective-permute-done.25.refs_0_), channel_id=1, source_target_pairs={{0,4},{1,3},{2,6},{3,1},{4,0},{5,7},{6,2},{7,5},{8,12},{9,11},{10,... | collective-permute-start | bytes 811016 | tf_op jit(solution)/shard_map/ppermute | solution.py:311
  31.2 5.3 %collective-permute-start.29 = (bf16[32,4224]{1,0:T(8,128)(2,1)}, bf16[32,4224]{1,0:T(8,128)(2,1)S(1)}, u32[]{:S(2)}, u32[]{:S(2)}) collective-permute-start(bf16[32,4224]{1,0:T(8,128)(2,1)} %collective-permute-done.25.refs_0_), channel_id=1, source_target_pairs={{0,1},{1,0},{2,3},{3,2},{4,5},{5,4},{6,7},{7,6},{8,9},{9,8},{10,11... | collective-permute-start | bytes 811016 | tf_op jit(solution)/shard_map/ppermute | solution.py:323
  33.0 8.2 %collective-permute-start.28 = (bf16[32,4224]{1,0:T(8,128)(2,1)S(1)}, bf16[32,4224]{1,0:T(8,128)(2,1)S(1)}, u32[]{:S(2)}, u32[]{:S(2)}) collective-permute-start(bf16[32,4224]{1,0:T(8,128)(2,1)S(1)} %collective-permute-done.26.refs_1_), channel_id=1, source_target_pairs={{0,4},{1,3},{2,6},{3,1},{4,0},{5,7},{6,2},{7,5},{8,12},{9,11},{10,... | collective-permute-start | bytes 811016 | tf_op jit(solution)/shard_map/ppermute | solution.py:311
  34.5 20.0 %collective-permute-start.18 = (bf16[32,4224]{1,0:T(8,128)(2,1)S(1)}, bf16[32,4224]{1,0:T(8,128)(2,1)S(1)}, u32[]{:S(2)}, u32[]{:S(2)}) collective-permute-start(bf16[32,4224]{1,0:T(8,128)(2,1)S(1)} %collective-permute-done.17.refs_0_), channel_id=1, source_target_pairs={{0,2},{1,5},{2,0},{3,7},{4,6},{5,1},{6,4},{7,3},{8,10},{9,13},{10,... | collective-permute-start | bytes 811016 | tf_op jit(solution)/shard_map/ppermute | solution.py:311
  36.0 20.0 %collective-permute-start.19 = (bf16[32,4224]{1,0:T(8,128)(2,1)S(1)}, bf16[32,4224]{1,0:T(8,128)(2,1)S(1)}, u32[]{:S(2)}, u32[]{:S(2)}) collective-permute-start(bf16[32,4224]{1,0:T(8,128)(2,1)S(1)} %collective-permute-done.17.refs_0_), channel_id=1, source_target_pairs={{0,4},{1,3},{2,6},{3,1},{4,0},{5,7},{6,2},{7,5},{8,12},{9,11},{10,... | collective-permute-start | bytes 811016 | tf_op jit(solution)/shard_map/ppermute | solution.py:311
  36.5 19.6 %collective-permute-start.30 = (bf16[32,4224]{1,0:T(8,128)(2,1)S(1)}, bf16[32,4224]{1,0:T(8,128)(2,1)S(1)}, u32[]{:S(2)}, u32[]{:S(2)}) collective-permute-start(bf16[32,4224]{1,0:T(8,128)(2,1)S(1)} %collective-permute-done.26.refs_1_), channel_id=1, source_target_pairs={{0,1},{1,0},{2,3},{3,2},{4,5},{5,4},{6,7},{7,6},{8,9},{9,8},{10,11... | collective-permute-start | bytes 811016 | tf_op jit(solution)/shard_map/ppermute | solution.py:323
  41.2 14.9 %collective-permute-start.31 = (bf16[32,4224]{1,0:T(8,128)(2,1)S(1)}, bf16[32,4224]{1,0:T(8,128)(2,1)S(1)}, u32[]{:S(2)}, u32[]{:S(2)}) collective-permute-start(bf16[32,4224]{1,0:T(8,128)(2,1)S(1)} %collective-permute-done.27.refs_2_), channel_id=1, source_target_pairs={{0,1},{1,0},{2,3},{3,2},{4,5},{5,4},{6,7},{7,6},{8,9},{9,8},{10,11... | collective-permute-start | bytes 811016 | tf_op jit(solution)/shard_map/ppermute | solution.py:323
  41.2 14.9 %collective-permute-start.32 = (bf16[32,4224]{1,0:T(8,128)(2,1)S(1)}, bf16[32,4224]{1,0:T(8,128)(2,1)S(1)}, u32[]{:S(2)}, u32[]{:S(2)}) collective-permute-start(bf16[32,4224]{1,0:T(8,128)(2,1)S(1)} %collective-permute-done.28.refs_3_), channel_id=1, source_target_pairs={{0,1},{1,0},{2,3},{3,2},{4,5},{5,4},{6,7},{7,6},{8,9},{9,8},{10,11... | collective-permute-start | bytes 811016 | tf_op jit(solution)/shard_map/ppermute | solution.py:323
  41.7 1.2 copy-start.3
  42.9 2.2 %copy-start.7 = (bf16[2,1024,1024]{2,1,0:T(8,128)(2,1)S(1)}, bf16[2,1024,1024]{2,1,0:T(8,128)(2,1)}, u32[]{:S(2)}) copy-start(bf16[2,1024,1024]{2,1,0:T(8,128)(2,1)} %value_ref.3) | copy-start | bytes 12582916
  54.5 59.5 %copy-start = (bf16[32,8192]{1,0:T(8,128)(2,1)}, bf16[32,8192]{1,0:T(8,128)(2,1)S(1)}, u32[]{:S(2)}) copy-start(bf16[32,8192]{1,0:T(8,128)(2,1)S(1)} %attend.2.refs_11_.mine_0) | copy-start | bytes 1572868
  54.5 13.4 %collective-permute-start.10 = (bf16[32,4224]{1,0:T(8,128)(2,1)}, bf16[32,4224]{1,0:T(8,128)(2,1)S(1)}, u32[]{:S(2)}, u32[]{:S(2)}) collective-permute-start(bf16[32,4224]{1,0:T(8,128)(2,1)} %collective-permute-done.9.refs_0_), channel_id=1, source_target_pairs={{0,2},{1,5},{2,0},{3,7},{4,6},{5,1},{6,4},{7,3},{8,10},{9,13},{10,... | collective-permute-start | bytes 811016 | tf_op jit(solution)/shard_map/ppermute | solution.py:311
  66.9 25.3 %collective-permute-start.33 = (bf16[128,4096]{1,0:T(8,128)(2,1)S(1)}, bf16[128,4096]{1,0:T(8,128)(2,1)S(1)}, u32[]{:S(2)}, u32[]{:S(2)}) collective-permute-start(bf16[128,4096]{1,0:T(8,128)(2,1)S(1)} %get-tuple-element.17), channel_id=1, source_target_pairs={{0,1},{1,0},{2,3},{3,2},{4,5},{5,4},{6,7},{7,6},{8,9},{9,8},{10,11... | collective-permute-start | bytes 3145736 | tf_op jit(solution)/shard_map/ppermute | solution.py:323
  67.0 6.7 %collective-permute-start.11 = (bf16[32,4224]{1,0:T(8,128)(2,1)}, bf16[32,4224]{1,0:T(8,128)(2,1)S(1)}, u32[]{:S(2)}, u32[]{:S(2)}) collective-permute-start(bf16[32,4224]{1,0:T(8,128)(2,1)} %collective-permute-done.9.refs_0_), channel_id=1, source_target_pairs={{0,4},{1,3},{2,6},{3,1},{4,0},{5,7},{6,2},{7,5},{8,12},{9,11},{10,... | collective-permute-start | bytes 811016 | tf_op jit(solution)/shard_map/ppermute | solution.py:311
  67.9 8.7 %collective-permute-start.12 = (bf16[32,4224]{1,0:T(8,128)(2,1)S(1)}, bf16[32,4224]{1,0:T(8,128)(2,1)S(1)}, u32[]{:S(2)}, u32[]{:S(2)}) collective-permute-start(bf16[32,4224]{1,0:T(8,128)(2,1)S(1)} %collective-permute-done.10.refs_12_.refs_1_), channel_id=1, source_target_pairs={{0,4},{1,3},{2,6},{3,1},{4,0},{5,7},{6,2},{7,5},{8,12},{9,11},{10,... | collective-permute-start | bytes 811016 | tf_op jit(solution)/shard_map/ppermute | solution.py:311
  69.1 10.4 %collective-permute-start.20 = (bf16[32,4224]{1,0:T(8,128)(2,1)S(1)}, bf16[32,4224]{1,0:T(8,128)(2,1)S(1)}, u32[]{:S(2)}, u32[]{:S(2)}) collective-permute-start(bf16[32,4224]{1,0:T(8,128)(2,1)S(1)} %collective-permute-done.18.refs_15_.refs_1_), channel_id=1, source_target_pairs={{0,4},{1,3},{2,6},{3,1},{4,0},{5,7},{6,2},{7,5},{8,12},{9,11},{10,... | collective-permute-start | bytes 811016 | tf_op jit(solution)/shard_map/ppermute | solution.py:311
  69.9 9.6 %collective-permute-start.21 = (bf16[32,4224]{1,0:T(8,128)(2,1)S(1)}, bf16[32,4224]{1,0:T(8,128)(2,1)S(1)}, u32[]{:S(2)}, u32[]{:S(2)}) collective-permute-start(bf16[32,4224]{1,0:T(8,128)(2,1)S(1)} %collective-permute-done.17.refs_0_), channel_id=1, source_target_pairs={{0,1},{1,0},{2,3},{3,2},{4,5},{5,4},{6,7},{7,6},{8,9},{9,8},{10,11... | collective-permute-start | bytes 811016 | tf_op jit(solution)/shard_map/ppermute | solution.py:323
  73.8 6.3 %collective-permute-start.22 = (bf16[32,4224]{1,0:T(8,128)(2,1)S(1)}, bf16[32,4224]{1,0:T(8,128)(2,1)S(1)}, u32[]{:S(2)}, u32[]{:S(2)}) collective-permute-start(bf16[32,4224]{1,0:T(8,128)(2,1)S(1)} %collective-permute-done.18.refs_15_.refs_1_), channel_id=1, source_target_pairs={{0,1},{1,0},{2,3},{3,2},{4,5},{5,4},{6,7},{7,6},{8,9},{9,8},{10,11... | collective-permute-start | bytes 811016 | tf_op jit(solution)/shard_map/ppermute | solution.py:323
  76.7 3.5 %collective-permute-start.23 = (bf16[32,4224]{1,0:T(8,128)(2,1)S(1)}, bf16[32,4224]{1,0:T(8,128)(2,1)S(1)}, u32[]{:S(2)}, u32[]{:S(2)}) collective-permute-start(bf16[32,4224]{1,0:T(8,128)(2,1)S(1)} %collective-permute-done.19.refs_16_.refs_2_), channel_id=1, source_target_pairs={{0,1},{1,0},{2,3},{3,2},{4,5},{5,4},{6,7},{7,6},{8,9},{9,8},{10,11... | collective-permute-start | bytes 811016 | tf_op jit(solution)/shard_map/ppermute | solution.py:323
  79.6 1.9 %collective-permute-start.24 = (bf16[32,4224]{1,0:T(8,128)(2,1)S(1)}, bf16[32,4224]{1,0:T(8,128)(2,1)S(1)}, u32[]{:S(2)}, u32[]{:S(2)}) collective-permute-start(bf16[32,4224]{1,0:T(8,128)(2,1)S(1)} %collective-permute-done.20.refs_3_), channel_id=1, source_target_pairs={{0,1},{1,0},{2,3},{3,2},{4,5},{5,4},{6,7},{7,6},{8,9},{9,8},{10,11... | collective-permute-start | bytes 811016 | tf_op jit(solution)/shard_map/ppermute | solution.py:323
  79.6 13.3 %collective-permute-start.13 = (bf16[32,4224]{1,0:T(8,128)(2,1)}, bf16[32,4224]{1,0:T(8,128)(2,1)S(1)}, u32[]{:S(2)}, u32[]{:S(2)}) collective-permute-start(bf16[32,4224]{1,0:T(8,128)(2,1)} %collective-permute-done.9.refs_0_), channel_id=1, source_target_pairs={{0,1},{1,0},{2,3},{3,2},{4,5},{5,4},{6,7},{7,6},{8,9},{9,8},{10,11... | collective-permute-start | bytes 811016 | tf_op jit(solution)/shard_map/ppermute | solution.py:323
  80.1 13.0 %collective-permute-start.14 = (bf16[32,4224]{1,0:T(8,128)(2,1)S(1)}, bf16[32,4224]{1,0:T(8,128)(2,1)S(1)}, u32[]{:S(2)}, u32[]{:S(2)}) collective-permute-start(bf16[32,4224]{1,0:T(8,128)(2,1)S(1)} %collective-permute-done.10.refs_12_.refs_1_), channel_id=1, source_target_pairs={{0,1},{1,0},{2,3},{3,2},{4,5},{5,4},{6,7},{7,6},{8,9},{9,8},{10,11... | collective-permute-start | bytes 811016 | tf_op jit(solution)/shard_map/ppermute | solution.py:323
  80.1 13.3 %collective-permute-start.15 = (bf16[32,4224]{1,0:T(8,128)(2,1)S(1)}, bf16[32,4224]{1,0:T(8,128)(2,1)S(1)}, u32[]{:S(2)}, u32[]{:S(2)}) collective-permute-start(bf16[32,4224]{1,0:T(8,128)(2,1)S(1)} %collective-permute-done.11.refs_13_.refs_2_), channel_id=1, source_target_pairs={{0,1},{1,0},{2,3},{3,2},{4,5},{5,4},{6,7},{7,6},{8,9},{9,8},{10,11... | collective-permute-start | bytes 811016 | tf_op jit(solution)/shard_map/ppermute | solution.py:323
  81.4 12.2 %collective-permute-start.16 = (bf16[32,4224]{1,0:T(8,128)(2,1)S(1)}, bf16[32,4224]{1,0:T(8,128)(2,1)S(1)}, u32[]{:S(2)}, u32[]{:S(2)}) collective-permute-start(bf16[32,4224]{1,0:T(8,128)(2,1)S(1)} %collective-permute-done.12.refs_14_.refs_3_), channel_id=1, source_target_pairs={{0,1},{1,0},{2,3},{3,2},{4,5},{5,4},{6,7},{7,6},{8,9},{9,8},{10,11... | collective-permute-start | bytes 811016 | tf_op jit(solution)/shard_map/ppermute | solution.py:323
  81.5 11.3 %copy-start.1 = (bf16[32,4224]{1,0:T(8,128)(2,1)S(1)}, bf16[32,4224]{1,0:T(8,128)(2,1)}, u32[]{:S(2)}) copy-start(bf16[32,4224]{1,0:T(8,128)(2,1)} %norm_message.1.refs_0_) | copy-start | bytes 811012
  92.3 12.5 %collective-permute-start.34 = (bf16[128,4096]{1,0:T(8,128)(2,1)S(1)}, bf16[128,4096]{1,0:T(8,128)(2,1)S(1)}, u32[]{:S(2)}, u32[]{:S(2)}) collective-permute-start(bf16[128,4096]{1,0:T(8,128)(2,1)S(1)} %get-tuple-element.20), channel_id=1, source_target_pairs={{0,1},{1,0},{2,3},{3,2},{4,5},{5,4},{6,7},{7,6},{8,9},{9,8},{10,11... | collective-permute-start | bytes 3145736 | tf_op jit(solution)/shard_map/ppermute | solution.py:323
  92.8 21.4 %collective-permute-start.5 = (bf16[32,4224]{1,0:T(8,128)(2,1)S(1)}, bf16[32,4224]{1,0:T(8,128)(2,1)S(1)}, u32[]{:S(2)}, u32[]{:S(2)}) collective-permute-start(bf16[32,4224]{1,0:T(8,128)(2,1)S(1)} %copy-done.1), channel_id=1, source_target_pairs={{0,1},{1,0},{2,3},{3,2},{4,5},{5,4},{6,7},{7,6},{8,9},{9,8},{10,11... | collective-permute-start | bytes 811016 | tf_op jit(solution)/shard_map/ppermute | solution.py:323
  93.0 21.8 %collective-permute-start.6 = (bf16[32,4224]{1,0:T(8,128)(2,1)S(1)}, bf16[32,4224]{1,0:T(8,128)(2,1)S(1)}, u32[]{:S(2)}, u32[]{:S(2)}) collective-permute-start(bf16[32,4224]{1,0:T(8,128)(2,1)S(1)} %collective-permute-done.2.refs_12_.refs_1_), channel_id=1, source_target_pairs={{0,1},{1,0},{2,3},{3,2},{4,5},{5,4},{6,7},{7,6},{8,9},{9,8},{10,11... | collective-permute-start | bytes 811016 | tf_op jit(solution)/shard_map/ppermute | solution.py:323
  93.4 22.2 %collective-permute-start.7 = (bf16[32,4224]{1,0:T(8,128)(2,1)S(1)}, bf16[32,4224]{1,0:T(8,128)(2,1)S(1)}, u32[]{:S(2)}, u32[]{:S(2)}) collective-permute-start(bf16[32,4224]{1,0:T(8,128)(2,1)S(1)} %collective-permute-done.3.refs_13_.refs_2_), channel_id=1, source_target_pairs={{0,1},{1,0},{2,3},{3,2},{4,5},{5,4},{6,7},{7,6},{8,9},{9,8},{10,11... | collective-permute-start | bytes 811016 | tf_op jit(solution)/shard_map/ppermute | solution.py:323
  93.6 23.3 %collective-permute-start.8 = (bf16[32,4224]{1,0:T(8,128)(2,1)S(1)}, bf16[32,4224]{1,0:T(8,128)(2,1)S(1)}, u32[]{:S(2)}, u32[]{:S(2)}) collective-permute-start(bf16[32,4224]{1,0:T(8,128)(2,1)S(1)} %collective-permute-done.4.refs_14_.refs_3_), channel_id=1, source_target_pairs={{0,1},{1,0},{2,3},{3,2},{4,5},{5,4},{6,7},{7,6},{8,9},{9,8},{10,11... | collective-permute-start | bytes 811016 | tf_op jit(solution)/shard_map/ppermute | solution.py:323
  104.8 9.2 %collective-permute-start.35 = (bf16[64,4096]{1,0:T(8,128)(2,1)S(1)}, bf16[64,4096]{1,0:T(8,128)(2,1)S(1)}, u32[]{:S(2)}, u32[]{:S(2)}) collective-permute-start(bf16[64,4096]{1,0:T(8,128)(2,1)S(1)} %add_convert_fusion.3.refs_12_), channel_id=1, source_target_pairs={{0,4},{1,3},{2,6},{3,1},{4,0},{5,7},{6,2},{7,5},{8,12},{9,11},{10,... | collective-permute-start | bytes 1572872 | tf_op jit(solution)/shard_map/ppermute | solution.py:311
  114.0 47.7 %collective-permute-start.38 = (bf16[32,8192]{1,0:T(8,128)(2,1)S(1)}, bf16[32,8192]{1,0:T(8,128)(2,1)S(1)}, u32[]{:S(2)}, u32[]{:S(2)}) collective-permute-start(bf16[32,8192]{1,0:T(8,128)(2,1)S(1)} %attend.2.refs_11_.mine_0), channel_id=1, source_target_pairs={{0,1},{1,0},{2,3},{3,2},{4,5},{5,4},{6,7},{7,6},{8,9},{9,8},{10,11... | collective-permute-start | bytes 1572872 | tf_op jit(solution)/shard_map/ppermute | solution.py:323
  114.2 17.4 %collective-permute-start.36 = (bf16[128,4096]{1,0:T(8,128)(2,1)S(1)}, bf16[128,4096]{1,0:T(8,128)(2,1)}, u32[]{:S(2)}, u32[]{:S(2)}) collective-permute-start(bf16[128,4096]{1,0:T(8,128)(2,1)S(1)} %get-tuple-element.23), channel_id=1, source_target_pairs={{0,1},{1,0},{2,3},{3,2},{4,5},{5,4},{6,7},{7,6},{8,9},{9,8},{10,11... | collective-permute-start | bytes 3145736 | tf_op jit(solution)/shard_map/ppermute | solution.py:323
  114.8 14.7 %collective-permute-start.37 = (bf16[64,4096]{1,0:T(8,128)(2,1)S(1)}, bf16[64,4096]{1,0:T(8,128)(2,1)}, u32[]{:S(2)}, u32[]{:S(2)}) collective-permute-start(bf16[64,4096]{1,0:T(8,128)(2,1)S(1)} %add_convert_fusion.2.refs_12_), channel_id=1, source_target_pairs={{0,4},{1,3},{2,6},{3,1},{4,0},{5,7},{6,2},{7,5},{8,12},{9,11},{10,... | collective-permute-start | bytes 1572872 | tf_op jit(solution)/shard_map/ppermute | solution.py:311
  115.6 12.1 %collective-permute-start.43 = (bf16[32,4096]{1,0:T(8,128)(2,1)S(1)}, bf16[32,4096]{1,0:T(8,128)(2,1)S(1)}, u32[]{:S(2)}, u32[]{:S(2)}) collective-permute-start(bf16[32,4096]{1,0:T(8,128)(2,1)S(1)} %slice.117.refs_13_), channel_id=1, source_target_pairs={{0,2},{1,5},{2,0},{3,7},{4,6},{5,1},{6,4},{7,3},{8,10},{9,13},{10,... | collective-permute-start | bytes 786440 | tf_op jit(solution)/shard_map/ppermute | solution.py:311
  116.9 17.0 %copy-start.4 = (bf16[64,8192]{1,0:T(8,128)(2,1)S(1)}, bf16[64,8192]{1,0:T(8,128)(2,1)}, u32[]{:S(2)}) copy-start(bf16[64,8192]{1,0:T(8,128)(2,1)} %copy-done.2) | copy-start | bytes 3145732
  116.9 17.0 %copy-start.8 = (bf16[2,1024,1024]{2,1,0:T(8,128)(2,1)S(1)}, bf16[2,1024,1024]{2,1,0:T(8,128)(2,1)}, u32[]{:S(2)}) copy-start(bf16[2,1024,1024]{2,1,0:T(8,128)(2,1)} %value_ref.3) | copy-start | bytes 12582916
  116.9 17.0 %copy-start.10 = (s32[4]{0:T(128)S(1)}, s32[4]{0:T(128)}, u32[]{:S(2)}) copy-start(s32[4]{0:T(128)} %lens_ref.3) | copy-start | bytes 52
  127.6 17.7 %collective-permute-start.40 = (bf16[128,4096]{1,0:T(8,128)(2,1)S(1)}, bf16[128,4096]{1,0:T(8,128)(2,1)S(1)}, u32[]{:S(2)}, u32[]{:S(2)}) collective-permute-start(bf16[128,4096]{1,0:T(8,128)(2,1)S(1)} %get-tuple-element.24), channel_id=1, source_target_pairs={{0,1},{1,0},{2,3},{3,2},{4,5},{5,4},{6,7},{7,6},{8,9},{9,8},{10,11... | collective-permute-start | bytes 3145736 | tf_op jit(solution)/shard_map/ppermute | solution.py:323
  128.5 41.8 %collective-permute-start.44 = (bf16[32,4096]{1,0:T(8,128)(2,1)}, bf16[32,4096]{1,0:T(8,128)(2,1)}, u32[]{:S(2)}, u32[]{:S(2)}) collective-permute-start(bf16[32,4096]{1,0:T(8,128)(2,1)} %fusion.3), channel_id=1, source_target_pairs={{0,8},{1,9},{2,10},{3,11},{4,12},{5,13},{6,14},{7,15},{8,0},{9,1},... | collective-permute-start | bytes 786440 | tf_op jit(solution)/shard_map/ppermute | solution.py:311
  130.8 11.8 %collective-permute-start.47 = (bf16[32,4096]{1,0:T(8,128)(2,1)S(1)}, bf16[32,4096]{1,0:T(8,128)(2,1)S(1)}, u32[]{:S(2)}, u32[]{:S(2)}) collective-permute-start(bf16[32,4096]{1,0:T(8,128)(2,1)S(1)} %slice.116.refs_2_), channel_id=1, source_target_pairs={{0,2},{1,5},{2,0},{3,7},{4,6},{5,1},{6,4},{7,3},{8,10},{9,13},{10,... | collective-permute-start | bytes 786440 | tf_op jit(solution)/shard_map/ppermute | solution.py:311
  132.8 9.9 %collective-permute-start.45 = (bf16[64,4096]{1,0:T(8,128)(2,1)S(1)}, bf16[64,4096]{1,0:T(8,128)(2,1)S(1)}, u32[]{:S(2)}, u32[]{:S(2)}) collective-permute-start(bf16[64,4096]{1,0:T(8,128)(2,1)S(1)} %add_convert_fusion.1.refs_1_), channel_id=1, source_target_pairs={{0,4},{1,3},{2,6},{3,1},{4,0},{5,7},{6,2},{7,5},{8,12},{9,11},{10,... | collective-permute-start | bytes 1572872 | tf_op jit(solution)/shard_map/ppermute | solution.py:311
  142.6 20.0 %copy-start.6 = (bf16[32,8192]{1,0:T(8,128)(2,1)}, bf16[32,8192]{1,0:T(8,128)(2,1)S(1)}, u32[]{:S(2)}) copy-start(bf16[32,8192]{1,0:T(8,128)(2,1)S(1)} %attend.3.mine_1) | copy-start | bytes 1572868
  142.6 20.0 %collective-permute-start.39 = (bf16[32,8192]{1,0:T(8,128)(2,1)S(1)}, bf16[32,8192]{1,0:T(8,128)(2,1)S(1)}, u32[]{:S(2)}, u32[]{:S(2)}) collective-permute-start(bf16[32,8192]{1,0:T(8,128)(2,1)S(1)} %attend.3.mine_1), channel_id=1, source_target_pairs={{0,1},{1,0},{2,3},{3,2},{4,5},{5,4},{6,7},{7,6},{8,9},{9,8},{10,11... | collective-permute-start | bytes 1572872 | tf_op jit(solution)/shard_map/ppermute | solution.py:323
  142.7 8.8 %collective-permute-start.48 = (bf16[32,4096]{1,0:T(8,128)(2,1)S(1)}, bf16[32,4096]{1,0:T(8,128)(2,1)S(1)}, u32[]{:S(2)}, u32[]{:S(2)}) collective-permute-start(bf16[32,4096]{1,0:T(8,128)(2,1)S(1)} %fusion), channel_id=1, source_target_pairs={{0,8},{1,9},{2,10},{3,11},{4,12},{5,13},{6,14},{7,15},{8,0},{9,1},... | collective-permute-start | bytes 786440 | tf_op jit(solution)/shard_map/ppermute | solution.py:311
  145.3 7.2 %collective-permute-start.46 = (bf16[32,4096]{1,0:T(8,128)(2,1)S(1)}, bf16[32,4096]{1,0:T(8,128)(2,1)S(1)}, u32[]{:S(2)}, u32[]{:S(2)}) collective-permute-start(bf16[32,4096]{1,0:T(8,128)(2,1)S(1)} %slice.114), channel_id=1, source_target_pairs={{0,2},{1,5},{2,0},{3,7},{4,6},{5,1},{6,4},{7,3},{8,10},{9,13},{10,... | collective-permute-start | bytes 786440 | tf_op jit(solution)/shard_map/ppermute | solution.py:311
  151.5 9.2 %collective-permute-start.41 = (bf16[64,4096]{1,0:T(8,128)(2,1)S(1)}, bf16[64,4096]{1,0:T(8,128)(2,1)S(1)}, u32[]{:S(2)}, u32[]{:S(2)}) collective-permute-start(bf16[64,4096]{1,0:T(8,128)(2,1)S(1)} %add_convert_fusion), channel_id=1, source_target_pairs={{0,4},{1,3},{2,6},{3,1},{4,0},{5,7},{6,2},{7,5},{8,12},{9,11},{10,... | collective-permute-start | bytes 1572872 | tf_op jit(solution)/shard_map/ppermute | solution.py:311
  152.7 17.6 %collective-permute-start.49 = (bf16[32,4096]{1,0:T(8,128)(2,1)S(1)}, bf16[32,4096]{1,0:T(8,128)(2,1)}, u32[]{:S(2)}, u32[]{:S(2)}) collective-permute-start(bf16[32,4096]{1,0:T(8,128)(2,1)S(1)} %fusion.2), channel_id=1, source_target_pairs={{0,16},{1,17},{2,18},{3,19},{4,20},{5,21},{6,22},{7,23},{8,24},{9,... | collective-permute-start | bytes 786440 | tf_op jit(solution)/shard_map/ppermute | solution.py:311
  160.9 9.4 %collective-permute-start.42 = (bf16[32,4096]{1,0:T(8,128)(2,1)S(1)}, bf16[32,4096]{1,0:T(8,128)(2,1)S(1)}, u32[]{:S(2)}, u32[]{:S(2)}) collective-permute-start(bf16[32,4096]{1,0:T(8,128)(2,1)S(1)} %slice.115), channel_id=1, source_target_pairs={{0,2},{1,5},{2,0},{3,7},{4,6},{5,1},{6,4},{7,3},{8,10},{9,13},{10,... | collective-permute-start | bytes 786440 | tf_op jit(solution)/shard_map/ppermute | solution.py:311
  161.8 0.8 copy-start.11
  162.6 0.8 copy-start.12
  (1 other events, 0.7 us)

commit v4 on v3

--- a/solution.py
+++ b/solution.py
@@ -15,6 +15,8 @@
 GROUP = SAMP * STEPS
 LANES = 128
 BAND = 64
+UNITS_STEP = 256
+DOWN_STEP = 1024
 LOG2E = 1.4426950408889634
 MIB = 1 << 20
 
@@ -76,15 +78,21 @@
     local, lens_ref, q_mine, q_other, k_mine, k_other, v_mine, v_other, n_mine, n_other,
     key_ref, value_ref, *refs
 ):
-    out_ref, q_ref, score_ref, weight_ref, total_ref = refs[-5:]
+    out_ref, q_ref, score_ref, weight_ref, total_ref, select_ref = refs[-6:]
     number = lax.axis_index("fan") * 2 + local
     length = lens_ref[number]
-    prompts = jnp.concatenate([n_mine[...], n_other[...]], axis=0).astype(jnp.float32)
-    chosen = prompts == number.astype(jnp.float32)
-    match = jnp.where(chosen, 1.0, 0.0).astype(jnp.bfloat16)
-    rank = rank_rows(match, LANES)
     lane = lax.broadcasted_iota(jnp.int32, (LANES, LANES), 1)
-    select = jnp.where(chosen & (rank == lane.astype(jnp.float32)), 1.0, 0.0).astype(jnp.bfloat16)
+
+    @pl.when(pl.program_id(0) == 0)
+    def _():
+        prompts = jnp.concatenate([n_mine[...], n_other[...]], axis=0).astype(jnp.float32)
+        chosen = prompts == number.astype(jnp.float32)
+        match = jnp.where(chosen, 1.0, 0.0).astype(jnp.bfloat16)
+        rank = rank_rows(match, LANES)
+        here = chosen & (rank == lane.astype(jnp.float32))
+        select_ref[...] = jnp.where(here, 1.0, 0.0).astype(jnp.bfloat16)
+
+    select = select_ref[...]
 
     def pick(mine, other):
         both = jnp.concatenate([mine[...], other[...]], axis=0)
@@ -153,6 +161,7 @@
             pltpu.VMEM((band, span + LANES), jnp.float32),
             pltpu.VMEM((band, span + LANES), jnp.bfloat16),
             pltpu.VMEM((band, HD), jnp.float32),
+            pltpu.VMEM((LANES, LANES), jnp.bfloat16),
         ],
         compiler_params=pltpu.CompilerParams(vmem_limit_bytes=24 * MIB),
         cost_estimate=cost(5e9, 5 * MIB),
@@ -160,25 +169,30 @@
     )(lens, *queries, *own, *own, *own, cache, cache, *after)
 
 
-def place_kernel(n_mine, mine_0, mine_1, other_0, other_1, out_ref):
+def place_kernel(n_mine, mine_0, mine_1, other_0, other_1, out_ref, place_ref):
     rows = out_ref.shape[0]
-    fan = lax.axis_index("fan")
-    prompts = n_mine[...].astype(jnp.float32)
-    lane = lax.broadcasted_iota(jnp.int32, (rows, LANES), 1).astype(jnp.float32)
-    every = jnp.ones((rows, rows), jnp.bfloat16)
-    place = jnp.zeros((rows, LANES), jnp.float32)
-    for side in range(2):
-        for local in range(2):
-            number = (fan if side == 0 else 1 - fan) * 2 + local
-            chosen = prompts == number.astype(jnp.float32)
-            match = jnp.where(chosen, 1.0, 0.0).astype(jnp.bfloat16)
-            rank = rank_rows(match, rows)
-            if side == 1:
-                rank = rank + (GROUP - dot(every, match))
-            here = chosen & (rank + (side * 2 + local) * GROUP == lane)
-            place = jnp.where(here, 1.0, place)
+
+    @pl.when(pl.program_id(0) == 0)
+    def _():
+        fan = lax.axis_index("fan")
+        prompts = n_mine[...].astype(jnp.float32)
+        lane = lax.broadcasted_iota(jnp.int32, (rows, LANES), 1).astype(jnp.float32)
+        every = jnp.ones((rows, rows), jnp.bfloat16)
+        place = jnp.zeros((rows, LANES), jnp.float32)
+        for side in range(2):
+            for local in range(2):
+                number = (fan if side == 0 else 1 - fan) * 2 + local
+                chosen = prompts == number.astype(jnp.float32)
+                match = jnp.where(chosen, 1.0, 0.0).astype(jnp.bfloat16)
+                rank = rank_rows(match, rows)
+                if side == 1:
+                    rank = rank + (GROUP - dot(every, match))
+                here = chosen & (rank + (side * 2 + local) * GROUP == lane)
+                place = jnp.where(here, 1.0, place)
+        place_ref[...] = place.astype(jnp.bfloat16)
+
     stacked = jnp.concatenate([mine_0[...], mine_1[...], other_0[...], other_1[...]], axis=0)
-    out_ref[...] = dot(place.astype(jnp.bfloat16), stacked).astype(jnp.bfloat16)
+    out_ref[...] = dot(place_ref[...], stacked).astype(jnp.bfloat16)
 
 
 def place_context(message, mine, other):
@@ -193,97 +207,120 @@
         out_shape=jax.ShapeDtypeStruct((rows, q_width), jnp.bfloat16),
         in_specs=[pl.BlockSpec((rows, LANES), lambda k: (0, marks)), block, block, block, block],
         out_specs=pl.BlockSpec((rows, width), lambda k: (0, k)),
+        scratch_shapes=[pltpu.VMEM((rows, LANES), jnp.bfloat16)],
         cost_estimate=cost(1e8, 3 * MIB),
         name="place_context",
     )(message, *mine, *other)
 
 
-def expert_kernel(pieces, *refs):
-    xs, (gate, up, down) = refs[:pieces], refs[pieces : pieces + 3]
-    keep, send, other = refs[-12:-9]
-    x, w_gate, w_up, w_down, units, x_sem, g_sem, u_sem, d_sem = refs[-9:]
+def units_kernel(pieces, *refs):
+    xs, (gate, up) = refs[:pieces], refs[pieces : pieces + 2]
+    units, scale, x, w_gate, w_up, x_sem, g_sem, u_sem = refs[-8:]
     width, hidden = gate.shape
     piece_rows = xs[0].shape[0]
-    step = 256
-    deep = 1024
     copies = []
     for i in range(pieces):
-        copies.append(
-            pltpu.make_async_copy(
-                xs[i], x.at[pl.ds(i * piece_rows, piece_rows)], x_sem.at[i]
-            )
-        )
-    gates, ups, downs = [], [], []
-    for i in range(hidden // step):
-        at = pl.ds(i * step, step)
+        at = pl.ds(i * piece_rows, piece_rows)
+        copies.append(pltpu.make_async_copy(xs[i], x.at[at], x_sem.at[i]))
+    gates, ups = [], []
+    for i in range(hidden // UNITS_STEP):
+        at = pl.ds(i * UNITS_STEP, UNITS_STEP)
         gates.append(pltpu.make_async_copy(gate.at[:, at], w_gate.at[:, at], g_sem.at[i]))
         ups.append(pltpu.make_async_copy(up.at[:, at], w_up.at[:, at], u_sem.at[i]))
-    for i in range(width // deep):
-        at = pl.ds(i * deep, deep)
-        downs.append(pltpu.make_async_copy(down.at[:, at], w_down.at[:, at], d_sem.at[i]))
     for copy in copies:
         copy.start()
-    for i in range(hidden // step):
+    for i in range(hidden // UNITS_STEP):
         gates[i].start()
         ups[i].start()
-    for copy in downs:
-        copy.start()
     for copy in copies:
         copy.wait()
-    for i in range(hidden // step):
-        at = slice(i * step, (i + 1) * step)
+    marks = x[:, width:].astype(jnp.float32)
+    lane = lax.broadcasted_iota(jnp.int32, marks.shape, 1)
+    mine = (lane % 16 == lax.axis_index("ep")) & (lane < 48)
+    weight = jnp.sum(jnp.where(mine, marks, 0.0), axis=1, keepdims=True)
+    scale[...] = jnp.broadcast_to(weight, scale.shape)
+    for i in range(hidden // UNITS_STEP):
+        at = slice(i * UNITS_STEP, (i + 1) * UNITS_STEP)
         gates[i].wait()
         opened = dot(x[:, :width], w_gate[:, at])
         ups[i].wait()
         raised = dot(x[:, :width], w_up[:, at])
         units[:, at] = (opened * jax.nn.sigmoid(opened) * raised).astype(jnp.bfloat16)
-    marks = x[:, width:].astype(jnp.float32)
-    lane = lax.broadcasted_iota(jnp.int32, marks.shape, 1)
-    mine = (lane % 16 == lax.axis_index("ep")) & (lane < 48)
-    weight = jnp.sum(jnp.where(mine, marks, 0.0), axis=1, keepdims=True)
-    half = pieces // 2 * piece_rows
-    near = half // 2
-    for i in range(width // deep):
-        downs[i].wait()
-        at = slice(i * deep, (i + 1) * deep)
-        result = (dot(units[...], w_down[:, at]) * weight).astype(jnp.bfloat16)
-        keep[:, at] = result[:near]
-        send[:, at] = result[near:half]
-        other[:, at] = result[half:]
-
-
-def expert_chunk(pieces, gate, up, down, after):
+
+
+def expert_units(pieces, gate, up, after):
     count = len(pieces)
     piece_rows, message = pieces[0].shape
     width, hidden = gate.shape
     rows = count * piece_rows
     anywhere = pl.BlockSpec(memory_space=pl.ANY)
-    stored = pl.BlockSpec(memory_space=pltpu.HBM)
     whole = pl.BlockSpec(memory_space=pltpu.VMEM)
+    steps = hidden // UNITS_STEP
     return pl.pallas_call(
-        functools.partial(expert_kernel, count),
+        functools.partial(units_kernel, count),
         out_shape=(
-            jax.ShapeDtypeStruct((rows // 4, width), jnp.bfloat16),
-            jax.ShapeDtypeStruct((rows // 4, width), jnp.bfloat16),
-            jax.ShapeDtypeStruct((rows // 2, width), jnp.bfloat16),
+            jax.ShapeDtypeStruct((rows, hidden), jnp.bfloat16),
+            jax.ShapeDtypeStruct((rows, LANES), jnp.float32),
         ),
-        in_specs=[stored] * (count + 3) + [anywhere] * len(after),
-        out_specs=(whole, whole, whole),
+        in_specs=[anywhere] * (count + 2 + len(after)),
+        out_specs=(whole, whole),
         scratch_shapes=[
             pltpu.VMEM((rows, message), jnp.bfloat16),
             pltpu.VMEM((width, hidden), jnp.bfloat16),
             pltpu.VMEM((width, hidden), jnp.bfloat16),
+            pltpu.SemaphoreType.DMA((count,)),
+            pltpu.SemaphoreType.DMA((steps,)),
+            pltpu.SemaphoreType.DMA((steps,)),
+        ],
+        compiler_params=pltpu.CompilerParams(vmem_limit_bytes=32 * MIB),
+        cost_estimate=cost(4 * rows * width * hidden, 4 * width * hidden),
+        name="expert_units",
+    )(*pieces, gate, up, *after)
+
+
+def results_kernel(splits, units, scale, down, *refs):
+    count = len(splits)
+    outs = refs[-count - 2 : -2]
+    w_down, sem = refs[-2:]
+    width = down.shape[1]
+    downs = []
+    for i in range(width // DOWN_STEP):
+        at = pl.ds(i * DOWN_STEP, DOWN_STEP)
+        downs.append(pltpu.make_async_copy(down.at[:, at], w_down.at[:, at], sem.at[i]))
+        downs[i].start()
+    weight = scale[:, :1]
+    for i in range(width // DOWN_STEP):
+        downs[i].wait()
+        at = slice(i * DOWN_STEP, (i + 1) * DOWN_STEP)
+        result = (dot(units[...], w_down[:, at]) * weight).astype(jnp.bfloat16)
+        for out, parts in zip(outs, splits):
+            filled = 0
+            for first, amount in parts:
+                out[filled : filled + amount, at] = result[first : first + amount]
+                filled += amount
+
+
+def expert_results(units, scale, down, splits, after):
+    rows, hidden = units.shape
+    width = down.shape[1]
+    anywhere = pl.BlockSpec(memory_space=pl.ANY)
+    whole = pl.BlockSpec(memory_space=pltpu.VMEM)
+    return pl.pallas_call(
+        functools.partial(results_kernel, splits),
+        out_shape=[
+            jax.ShapeDtypeStruct((sum(amount for _, amount in parts), width), jnp.bfloat16)
+            for parts in splits
+        ],
+        in_specs=[whole, whole] + [anywhere] * (1 + len(after)),
+        out_specs=[whole] * len(splits),
+        scratch_shapes=[
             pltpu.VMEM((hidden, width), jnp.bfloat16),
-            pltpu.VMEM((rows, hidden), jnp.bfloat16),
-            pltpu.SemaphoreType.DMA((count,)),
-            pltpu.SemaphoreType.DMA((hidden // 256,)),
-            pltpu.SemaphoreType.DMA((hidden // 256,)),
-            pltpu.SemaphoreType.DMA((width // 1024,)),
+            pltpu.SemaphoreType.DMA((width // DOWN_STEP,)),
         ],
-        compiler_params=pltpu.CompilerParams(vmem_limit_bytes=40 * MIB),
-        cost_estimate=cost(6 * rows * width * hidden, 6 * width * hidden),
-        name="expert_chunk",
-    )(*pieces, gate, up, down, *after)
+        compiler_params=pltpu.CompilerParams(vmem_limit_bytes=32 * MIB),
+        cost_estimate=cost(2 * rows * width * hidden, 2 * width * hidden),
+        name="expert_results",
+    )(units, scale, down, *after)
 
 
 def on_device(
@@ -316,6 +353,9 @@
     def cross(value):
         return swap(value, (2, 1))
 
+    def hold(value, *after):
+        return lax.optimization_barrier((value, *after))[0]
+
     def far(value, layer):
         return swap(value, (4 * layer, 4 * layer))
 
@@ -324,13 +364,8 @@
 
     token = norm_message(hidden, norm_gain, route_ids, route_logits)
     opposite = far(token, 2)
-    arrived = {0: token, 1: far(token, 1), 2: opposite, 3: far(opposite, 1)}
-    pieces = {}
-    for layer in (0, 1, 3, 2):
-        own = arrived[layer]
-        first = near(own)
-        four = [own, first, cross(own), cross(first)]
-        pieces[layer] = four + [beside(piece) for piece in four]
+    pair_b = jnp.concatenate([token, far(token, 1)], axis=0)
+    turned = far(opposite, 1)
 
     marks = jnp.broadcast_to(sample_prompt.astype(jnp.bfloat16)[:, None, None], (count, STEPS, LANES))
     q_mine = queries.reshape(rows, q_width)
@@ -338,57 +373,76 @@
     q_both = (q_mine, beside(q_mine))
     own_both = (own_mine, beside(own_mine))
 
-    def expert(layer, *after):
-        return expert_chunk(pieces[layer], w_gate[0], w_up[0], w_down[0], after)
-
-    def add_cores(result):
+    def add_cores(result, *after):
         keep, send, away = result
-        back = beside(away)
+        back = hold(beside(away), *after)
         half = send.shape[0]
         there = (send.astype(jnp.float32) + back[half:].astype(jnp.float32)).astype(jnp.bfloat16)
         return keep, back, there
 
-    def add_cross(keep, back, there):
-        half = keep.shape[0]
-        single = half // 2
-        turned = cross(there).astype(jnp.float32)
-        held = keep.astype(jnp.float32) + back[:half].astype(jnp.float32) + turned
-        return held[:single], held[single:].astype(jnp.bfloat16)
-
-    def add_near(held, passed):
-        return held + near(passed).astype(jnp.float32)
+    def add_cross(keep, back, there, *after):
+        single = keep.shape[0] // 2
+        total = keep.astype(jnp.float32) + back[: 2 * single].astype(jnp.float32)
+        total = total + hold(cross(there), *after).astype(jnp.float32)
+        return total[:single], total[single:].astype(jnp.bfloat16)
+
+    def add_near(held, passed, *after):
+        return held + hold(near(passed), *after).astype(jnp.float32)
 
     def add_far(total, layer):
         return far(total.astype(jnp.bfloat16), layer).astype(jnp.float32)
 
-    context_0 = attend(0, prompt_lens, q_both, own_both, prompt_kv, ())
-    result_1 = expert(1, context_0, *pieces[0][1:4], *pieces[3][1:3])
-    result_3 = expert(3, result_1[0], *pieces[2][1:4])
-    cores_1 = add_cores(result_1)
-    result_2 = expert(2, result_3[0], cores_1[2])
-    cores_3 = add_cores(result_3)
-    cross_1 = add_cross(*cores_1)
-    result_0 = expert(0, result_2[0], cores_3[2], cross_1[1])
-    cores_2 = add_cores(result_2)
-    cross_3 = add_cross(*cores_3)
-    near_1 = add_near(*cross_1)
-    far_1 = add_far(near_1, 1)
-    context_1 = attend(
-        1, prompt_lens, q_both, own_both, prompt_kv, (result_0[0], cores_2[2], cross_3[1])
-    )
-    cores_0 = add_cores(result_0)
-    cross_2 = add_cross(*cores_2)
-    near_3 = add_near(*cross_3)
-    far_3 = add_far(near_3, 1)
-    cross_0 = add_cross(*cores_0)
-    near_2 = add_near(*cross_2)
-    far_2 = add_far(near_2 + far_3, 2)
-    near_0 = add_near(*cross_0)
-    expert_out = (near_0 + far_1 + far_2).astype(jnp.bfloat16)
+    tokens = hidden.shape[0]
+    both = 2 * tokens
+    whole = [
+        [(0, 2 * both)],
+        [(2 * both, 2 * both)],
+        [(4 * both, 4 * both)],
+    ]
+
+    def single(at):
+        def rows_of(first, amount):
+            return [((first + i) * both + at * tokens, tokens) for i in range(amount)]
+
+        return [rows_of(0, 2), rows_of(2, 2), rows_of(4, 4)]
+
+    gate, up, down = w_gate[0], w_up[0], w_down[0]
+    first_b = near(pair_b)
+    cross_b = cross(pair_b)
+    context_0 = attend(0, prompt_lens, q_both, own_both, prompt_kv, (pair_b, opposite))
+    first_b = hold(first_b, context_0)
+    four_b = [pair_b, first_b, cross_b, cross(first_b)]
+    pieces_b = four_b + [beside(piece) for piece in four_b]
+    pair_a = jnp.concatenate([opposite, hold(turned, context_0)], axis=0)
+    units_b, scale_b = expert_units(pieces_b, gate, up, (context_0, pair_a))
+    first_a = hold(near(pair_a), units_b)
+    cross_a = hold(cross(pair_a), units_b)
+    four_a = [pair_a, first_a, cross_a, cross(first_a)]
+    pieces_a = four_a + [beside(piece) for piece in four_a]
+    result_b = expert_results(units_b, scale_b, down, whole, (first_a, cross_a))
+    units_a, scale_a = expert_units(pieces_a, gate, up, (result_b[0],))
+    cores_b = add_cores(result_b, units_a)
+    result_3 = expert_results(units_a, scale_a, down, single(1), (cores_b[2],))
+    result_2 = expert_results(units_a, scale_a, down, single(0), (result_3[0],))
+    cores_3 = add_cores(result_3, result_2[0])
+    cores_2 = add_cores(result_2, cores_3[2])
+    cross_b = add_cross(*cores_b, cores_2[2])
+    context_1 = attend(1, prompt_lens, q_both, own_both, prompt_kv, (cross_b[1],))
+    cross_3 = add_cross(*cores_3, context_1)
+    near_b = add_near(*cross_b, cross_3[1])
+    far_1 = add_far(near_b[tokens:], 1)
+    cross_2 = add_cross(*cores_2, cross_3[1])
 
     context_mine = [context_0, context_1]
     context_other = [beside(value) for value in context_mine]
-    context = place_context(own_mine, context_mine, context_other).reshape(count, STEPS, q_width)
+    own_late = hold(own_mine, cross_2[1])
+    context = place_context(own_late, context_mine, context_other).reshape(count, STEPS, q_width)
+
+    near_3 = add_near(*cross_3, context)
+    far_3 = add_far(near_3, 1)
+    near_2 = add_near(*cross_2, near_3)
+    far_2 = add_far(near_2 + far_3, 2)
+    expert_out = (near_b[:tokens] + far_1 + far_2).astype(jnp.bfloat16)
     return (context, expert_out)
 
 

time: 173 us -> 187 us (1.081)
  waiting for transfers between devices: 46.1 us -> 62.3 us
  starting transfers between devices: 38.2 us -> 26 us
  local copies, waits for them, and re-layouts: 11.3 us -> 19.5 us
  Pallas kernels: 66.8 us -> 70.4 us
  other arithmetic: 8.75 us -> 6.77 us
    ppermute x26 -> x18, waiting for transfers between devices: 45.2 us -> 60.3 us  [swap(): return lax.ppermute(value, ('ep', 'fan'), pairs)]
    ppermute x26 -> x18, starting transfers between devices: 33.3 us -> 23.4 us  [swap(): return lax.ppermute(value, ('ep', 'fan'), pairs)]
    unnamed x30 -> x53, local copies, waits for them, and re-layouts: 5.73 us -> 13.4 us
    pallas_call x4 -> x5, Pallas kernels: 43.1 us -> 47.7 us  [the longest x2 30.8 us: expert_units(): pl.pallas_call(functools.partial(units_kernel, count), out_shape=(jax.Sha...]
    ppermute x24 -> x15, starting transfers between devices: 4.83 us -> 2.6 us  [beside(): return lax.ppermute(value, 'fan', [(0, 1), (1, 0)])]
    add x4 -> x5, other arithmetic: 2.78 us -> 4.12 us  [the longest x2 2.38 us: add_near(): return held + hold(near(passed), *after).astype(jnp.float32)]
  transfers between devices with their start and end apart: 50 -> 33, of which waited for: 11 -> 10; matrix products, arithmetic and copies ran while one was open for 6% -> 6% of each run, Pallas kernels for 39% -> 32%
where the time goes in v4:
time: 187 us; the launch traced here: 186 us
  Pallas kernels  70.4 us (38%)
  waiting for transfers between devices  62.3 us (33%)
  starting transfers between devices  26 us (14%)
  local copies, waits for them, and re-layouts  19.5 us (10%)
  other arithmetic  6.77 us (4%)
    ppermute x18, waiting for transfers between devices, swap(): return lax.ppermute(value, ('ep', 'fan'), pairs)  60.3 us
    pallas_call x2, Pallas kernels, expert_units(): pl.pallas_call(functools.partial(units_kernel, count), out_shape=(jax.Sha...  30.8 us
    ppermute x18, starting transfers between devices, swap(): return lax.ppermute(value, ('ep', 'fan'), pairs)  23.4 us
    pallas_call x3, Pallas kernels, expert_results(): pl.pallas_call(functools.partial(results_kernel, splits), out_shape=[jax....  16.9 us
    pallas_call x2, Pallas kernels, attend(): pl.pallas_call(functools.partial(attend_kernel, local), grid=(KVH,), out_...  16.6 us
    unnamed x53, local copies, waits for them, and re-layouts  13.4 us
    pallas_call x1, Pallas kernels, place_context(): pl.pallas_call(place_kernel, grid=(q_width // width,), out_shape=jax.Shap...  4.21 us
  transfers between devices with their start and end apart: 33, of which 10 were waited for; matrix products, arithmetic and copies ran while one was open for 6% of the time, Pallas kernels for 32%

profile of v4, /device:TPU:0, one launch (start us, length us, event | category | flops | bytes accessed | tf_op | source)
XLA Modules:
  0.0 186.1 jit_solution(7246856674908950773)
XLA Ops:
  0.7 1.5 reshape.19.q_mine
  2.2 0.5 collective-permute-start.2
  2.7 0.6 reshape.18.gain_ref
  3.3 1.9 %norm_message.1 = bf16[32,4224]{1,0:T(8,128)(2,1)} custom-call(bf16[32,4096]{1,0:T(8,128)(2,1)} %hidden_ref.1, bf16[1,4096]{1,0:T(2,128)(2,1)} %reshape.18.gain_ref, s32[8,32]{1,0:T(8,128)} %bitcast.16, f32[8,32]{1,0:T(8,128)} %bitcast.17), custom_call_target="tpu_custom_call" | custom-call | flops 1000000 | bytes 524288 | tf_op jit(solution)/shard_map/norm_message/pallas_call | solution.py:62
  5.2 2.6 %collective-permute-start.4 = (bf16[32,4224]{1,0:T(8,128)(2,1)}, bf16[32,4224]{1,0:T(8,128)(2,1)S(1)}, u32[]{:S(2)}, u32[]{:S(2)}) collective-permute-start(bf16[32,4224]{1,0:T(8,128)(2,1)} %norm_message.1), channel_id=1, source_target_pairs={{0,8},{1,9},{2,10},{3,11},{4,12},{5,13},{6,14},{7,15},{8,0},{9,1},... | collective-permute-start | bytes 811016 | tf_op jit(solution)/shard_map/ppermute | solution.py:348
  7.8 2.6 %collective-permute-start = (bf16[32,4224]{1,0:T(8,128)(2,1)}, bf16[32,4224]{1,0:T(8,128)(2,1)S(1)}, u32[]{:S(2)}, u32[]{:S(2)}) collective-permute-start(bf16[32,4224]{1,0:T(8,128)(2,1)} %norm_message.1), channel_id=1, source_target_pairs={{0,16},{1,17},{2,18},{3,19},{4,20},{5,21},{6,22},{7,23},{8,24},{9,... | collective-permute-start | bytes 811016 | tf_op jit(solution)/shard_map/ppermute | solution.py:348
  10.4 0.1 broadcast_in_dim.2
  10.5 0.1 pad_maximum_fusion.1
  10.8 10.0 %collective-permute-done.4 = bf16[32,4224]{1,0:T(8,128)(2,1)S(1)} collective-permute-done((bf16[32,4224]{1,0:T(8,128)(2,1)}, bf16[32,4224]{1,0:T(8,128)(2,1)S(1)}, u32[]{:S(2)}, u32[]{:S(2)}) %collective-permute-start.4) | collective-permute-done | bytes 270368 | tf_op jit(solution)/shard_map/ppermute | solution.py:348
  20.8 1.1 pad_maximum_fusion.refs_0_
  22.0 1.7 collective-permute-start.6
  23.7 1.5 collective-permute-start.7
  25.4 2.2 %copy-done.6 = bf16[2,1024,1024]{2,1,0:T(8,128)(2,1)S(1)} copy-done((bf16[2,1024,1024]{2,1,0:T(8,128)(2,1)S(1)}, bf16[2,1024,1024]{2,1,0:T(8,128)(2,1)}, u32[]{:S(2)}) %copy-start.6) | copy-done | bytes 4194328
  27.6 8.3 %attend.2.refs_10_.mine_0 = bf16[32,8192]{1,0:T(8,128)(2,1)S(1)} custom-call(s32[4]{0:T(128)S(1)} %copy-done.10, bf16[64,8192]{1,0:T(8,128)(2,1)S(1)} %reshape.19.q_mine, bf16[64,8192]{1,0:T(8,128)(2,1)S(1)} %collective-permute-done.2.q_other, bf16[64,1152]{1,0:T(8,128)(2,1)S(1)} %reshape.17.k_mine.v_mine.n_mine, ...), custom_call_target="tpu_custom_call" | custom-call | flops 5000000000 | bytes 5242880 | tf_op jit(solution)/shard_map/attend/pallas_call | solution.py:147
  35.9 1.2 collective-permute-done.6.refs_1_
  37.1 0.8 collective-permute-start.8
  38.0 0.5 collective-permute-start.10
  38.5 7.9 %collective-permute-done.8.refs_3_ = bf16[64,4224]{1,0:T(8,128)(2,1)S(1)} collective-permute-done((bf16[64,4224]{1,0:T(8,128)(2,1)S(1)}, bf16[64,4224]{1,0:T(8,128)(2,1)S(1)}, u32[]{:S(2)}, u32[]{:S(2)}) %collective-permute-start.8) | collective-permute-done | bytes 540704 | tf_op jit(solution)/shard_map/ppermute | solution.py:348
  46.5 0.9 collective-permute-start.13
  47.4 1.5 collective-permute-start.5
  48.9 15.4 %expert_units.2 = (bf16[512,768]{1,0:T(8,128)(2,1)S(1)}, f32[512,128]{1,0:T(8,128)S(1)}) custom-call(bf16[64,4224]{1,0:T(8,128)(2,1)S(1)} %pad_maximum_fusion.refs_0_, bf16[64,4224]{1,0:T(8,128)(2,1)S(1)} %collective-permute-done.6.refs_1_, bf16[64,4224]{1,0:T(8,128)(2,1)S(1)} %collective-permute-done.7.refs_2_, ...), custom_call_target="tpu_custom_call" | custom-call | flops 6442450944 | bytes 12582912 | tf_op jit(solution)/shard_map/expert_units/pallas_call | solution.py:259
  64.3 2.8 %copy-done.4 = bf16[1,768,4096]{2,1,0:T(8,128)(2,1)S(1)} copy-done((bf16[1,768,4096]{2,1,0:T(8,128)(2,1)S(1)}, bf16[1,768,4096]{2,1,0:T(8,128)(2,1)}, u32[]{:S(2)}) %copy-start.4) | copy-done | bytes 6291480
  67.1 5.7 %expert_results.3 = (bf16[128,4096]{1,0:T(8,128)(2,1)S(1)}, bf16[128,4096]{1,0:T(8,128)(2,1)S(1)}, bf16[256,4096]{1,0:T(8,128)(2,1)S(1)}) custom-call(bf16[512,768]{1,0:T(8,128)(2,1)S(1)} %get-tuple-element.31.units, f32[512,128]{1,0:T(8,128)S(1)} %get-tuple-element.34.scale, bf16[768,4096]{1,0:T(8,128)(2,1)S(1)} %bitcast.13, ...), custom_call_target="tpu_custom_call" | custom-call | flops 3221225472 | bytes 6291456 | tf_op jit(solution)/shard_map/expert_results/pallas_call | solution.py:308
  72.9 1.6 collective-permute-start.14
  74.5 0.5 collective-permute-start.17
  75.0 7.3 %collective-permute-done.14.refs_3_ = bf16[64,4224]{1,0:T(8,128)(2,1)S(1)} collective-permute-done((bf16[64,4224]{1,0:T(8,128)(2,1)S(1)}, bf16[64,4224]{1,0:T(8,128)(2,1)S(1)}, u32[]{:S(2)}, u32[]{:S(2)}) %collective-permute-start.14) | collective-permute-done | bytes 540704 | tf_op jit(solution)/shard_map/ppermute | solution.py:348
  82.3 1.9 %collective-permute-done.18.refs_7_ = bf16[64,4224]{1,0:T(8,128)(2,1)S(1)} collective-permute-done((bf16[64,4224]{1,0:T(8,128)(2,1)S(1)}, bf16[64,4224]{1,0:T(8,128)(2,1)S(1)}, u32[]{:S(2)}, u32[]{:S(2)}) %collective-permute-start.18) | collective-permute-done | bytes 540704 | tf_op jit(solution)/shard_map/ppermute | solution.py:363
  84.3 2.8 %copy-done.3 = bf16[1,4096,768]{2,1,0:T(8,128)(2,1)S(1)} copy-done((bf16[1,4096,768]{2,1,0:T(8,128)(2,1)S(1)}, bf16[1,4096,768]{2,1,0:T(8,128)(2,1)}, u32[]{:S(2)}) %copy-start.3) | copy-done | bytes 6291480
  87.0 15.4 %expert_units.3 = (bf16[512,768]{1,0:T(8,128)(2,1)S(1)}, f32[512,128]{1,0:T(8,128)S(1)}) custom-call(bf16[64,4224]{1,0:T(8,128)(2,1)S(1)} %constant_dynamic-update-slice_fusion.refs_11_.refs_0_, bf16[64,4224]{1,0:T(8,128)(2,1)S(1)} %collective-permute-done.5.refs_0_.refs_1_, bf16[64,4224]{1,0:T(8,128)(2,1)S(1)} %collective-permute-done.13.refs_1_.refs_2_, ...), custom_call_target="tpu_custom_call" | custom-call | flops 6442450944 | bytes 12582912 | tf_op jit(solution)/shard_map/expert_units/pallas_call | solution.py:259
  102.5 0.2 add_convert_fusion.refs_0_
  102.7 1.1 copy-done.15
  103.8 2.8 %copy-done.5 = bf16[1,768,4096]{2,1,0:T(8,128)(2,1)S(1)} copy-done((bf16[1,768,4096]{2,1,0:T(8,128)(2,1)S(1)}, bf16[1,768,4096]{2,1,0:T(8,128)(2,1)}, u32[]{:S(2)}) %copy-start.5) | copy-done | bytes 6291480
  106.6 5.7 %expert_results.4 = (bf16[64,4096]{1,0:T(8,128)(2,1)S(1)}, bf16[64,4096]{1,0:T(8,128)(2,1)S(1)}, bf16[128,4096]{1,0:T(8,128)(2,1)S(1)}) custom-call(bf16[512,768]{1,0:T(8,128)(2,1)S(1)} %get-tuple-element.36.units, f32[512,128]{1,0:T(8,128)S(1)} %get-tuple-element.37.scale, bf16[768,4096]{1,0:T(8,128)(2,1)S(1)} %bitcast.14, ...), custom_call_target="tpu_custom_call" | custom-call | flops 3221225472 | bytes 6291456 | tf_op jit(solution)/shard_map/expert_results/pallas_call | solution.py:308
  112.3 0.2 collective-permute-start.21
  112.5 5.5 %expert_results.5 = (bf16[64,4096]{1,0:T(8,128)(2,1)S(1)}, bf16[64,4096]{1,0:T(8,128)(2,1)S(1)}, bf16[128,4096]{1,0:T(8,128)(2,1)S(1)}) custom-call(bf16[512,768]{1,0:T(8,128)(2,1)S(1)} %get-tuple-element.36.units, f32[512,128]{1,0:T(8,128)S(1)} %get-tuple-element.37.scale, bf16[768,4096]{1,0:T(8,128)(2,1)S(1)} %bitcast.15, ...), custom_call_target="tpu_custom_call" | custom-call | flops 3221225472 | bytes 6291456 | tf_op jit(solution)/shard_map/expert_results/pallas_call | solution.py:308
  118.1 0.4 collective-permute-start.20
  118.5 0.1 collective-permute-start.25
  118.7 1.5 collective-permute-start.24
  120.2 0.1 add_convert_fusion.2
  120.3 0.6 collective-permute-start.23
  120.9 0.1 add_convert_fusion.1
  121.0 1.6 collective-permute-start.22
  122.6 10.8 %collective-permute-done.24 = bf16[128,4096]{1,0:T(8,128)(2,1)S(1)} collective-permute-done((bf16[128,4096]{1,0:T(8,128)(2,1)S(1)}, bf16[128,4096]{1,0:T(8,128)(2,1)S(1)}, u32[]{:S(2)}, u32[]{:S(2)}) %collective-permute-start.24) | collective-permute-done | bytes 1048608 | tf_op jit(solution)/shard_map/ppermute | solution.py:348
  133.5 0.4 convert_add_fusion
  134.0 1.4 collective-permute-start.27
  135.4 8.3 %attend.3.mine_1 = bf16[32,8192]{1,0:T(8,128)(2,1)S(1)} custom-call(s32[4]{0:T(128)S(1)} %copy-done.10, bf16[64,8192]{1,0:T(8,128)(2,1)S(1)} %reshape.19.q_mine, bf16[64,8192]{1,0:T(8,128)(2,1)S(1)} %copy-done.9, bf16[64,1152]{1,0:T(8,128)(2,1)S(1)} %reshape.17.k_mine.v_mine.n_mine, bf16[64,1152]{1,0:T(8,128)(2,1)S(1)} %collective-permute-done.3.k_other.v_other.n_other, ...), custom_call_target="tpu_custom_call" | custom-call | flops 5000000000 | bytes 5242880 | tf_op jit(solution)/shard_map/attend/pallas_call | solution.py:147
  143.8 1.1 convert_add_fusion.2
  145.0 1.1 slice.93
  146.0 0.7 collective-permute-start.30
  146.8 4.7 %collective-permute-done.22 = bf16[64,4096]{1,0:T(8,128)(2,1)S(1)} collective-permute-done((bf16[64,4096]{1,0:T(8,128)(2,1)S(1)}, bf16[64,4096]{1,0:T(8,128)(2,1)S(1)}, u32[]{:S(2)}, u32[]{:S(2)}) %collective-permute-start.22) | collective-permute-done | bytes 524320 | tf_op jit(solution)/shard_map/ppermute | solution.py:348
  151.4 0.2 convert_add_fusion.1
  151.7 2.0 %collective-permute-start.29 = (bf16[32,4096]{1,0:T(8,128)(2,1)S(1)}, bf16[32,4096]{1,0:T(8,128)(2,1)S(1)}, u32[]{:S(2)}, u32[]{:S(2)}) collective-permute-start(bf16[32,4096]{1,0:T(8,128)(2,1)S(1)} %slice.92), channel_id=1, source_target_pairs={{0,2},{1,5},{2,0},{3,7},{4,6},{5,1},{6,4},{7,3},{8,10},{9,13},{10,... | collective-permute-start | bytes 786440 | tf_op jit(solution)/shard_map/ppermute | solution.py:348
  153.7 0.8 copy-done.17
  154.5 0.8 copy-done.18
  155.3 4.2 %place_context.1 = bf16[64,8192]{1,0:T(8,128)(2,1)} custom-call(bf16[64,1152]{1,0:T(8,128)(2,1)} %copy-done, bf16[32,8192]{1,0:T(8,128)(2,1)} %copy-done.1, bf16[32,8192]{1,0:T(8,128)(2,1)} %copy-done.2, bf16[32,8192]{1,0:T(8,128)(2,1)} %copy-done.17, bf16[32,8192]{1,0:T(8,128)(2,1)} %copy-done.18), custom_call_target="tpu_custom_call" | custom-call | flops 100000000 | bytes 3145728 | tf_op jit(solution)/shard_map/place_context/pallas_call | solution.py:204
  159.5 2.7 %reshape.20 = bf16[32,2,8192]{2,1,0:T(2,128)(2,1)} reshape(bf16[64,8192]{1,0:T(8,128)(2,1)} %place_context.1) | data formatting | bytes 2097152 | tf_op jit(solution)/shard_map/reshape | solution.py:439
  162.2 1.2 slice_add_fusion.1
  163.6 1.1 slice_add_fusion
  164.7 2.1 %collective-permute-start.28 = (bf16[32,4096]{1,0:T(8,128)(2,1)S(1)}, bf16[32,4096]{1,0:T(8,128)(2,1)S(1)}, u32[]{:S(2)}, u32[]{:S(2)}) collective-permute-start(bf16[32,4096]{1,0:T(8,128)(2,1)S(1)} %slice.91), channel_id=1, source_target_pairs={{0,8},{1,9},{2,10},{3,11},{4,12},{5,13},{6,14},{7,15},{8,0},{9,1},... | collective-permute-start | bytes 786440 | tf_op jit(solution)/shard_map/ppermute | solution.py:348
  166.8 8.8 %collective-permute-done.31 = bf16[32,4096]{1,0:T(8,128)(2,1)S(1)} collective-permute-done((bf16[32,4096]{1,0:T(8,128)(2,1)S(1)}, bf16[32,4096]{1,0:T(8,128)(2,1)S(1)}, u32[]{:S(2)}, u32[]{:S(2)}) %collective-permute-start.31) | collective-permute-done | bytes 262176 | tf_op jit(solution)/shard_map/ppermute | solution.py:348
  175.7 0.1 collective-permute-start.32
  175.8 3.0 %collective-permute-done.28 = bf16[32,4096]{1,0:T(8,128)(2,1)S(1)} collective-permute-done((bf16[32,4096]{1,0:T(8,128)(2,1)S(1)}, bf16[32,4096]{1,0:T(8,128)(2,1)S(1)}, u32[]{:S(2)}, u32[]{:S(2)}) %collective-permute-start.28) | collective-permute-done | bytes 262176 | tf_op jit(solution)/shard_map/ppermute | solution.py:348
  178.8 6.6 %collective-permute-done.32 = bf16[32,4096]{1,0:T(8,128)(2,1)S(1)} collective-permute-done((bf16[32,4096]{1,0:T(8,128)(2,1)S(1)}, bf16[32,4096]{1,0:T(8,128)(2,1)S(1)}, u32[]{:S(2)}, u32[]{:S(2)}) %collective-permute-start.32) | collective-permute-done | bytes 262176 | tf_op jit(solution)/shard_map/ppermute | solution.py:348
  185.4 0.8 fusion.3
  (89 shorter events, 0.9 us)
Async XLA Ops:
  0.6 2.1 %copy-start.20 = (bf16[4096]{0:T(1024)(128)(2,1)S(1)}, bf16[4096]{0:T(1024)(128)(2,1)}, u32[]{:S(2)}) copy-start(bf16[4096]{0:T(1024)(128)(2,1)} %param.18) | copy-start | bytes 24580
  0.6 9.8 %copy-start.21 = (s32[32]{0:T(128)S(1)}, s32[32]{0:T(128)}, u32[]{:S(2)}) copy-start(s32[32]{0:T(128)} %param.16) | copy-start | bytes 388
  0.7 9.9 %copy-start.19 = (bf16[32,2,1024]{2,1,0:T(2,128)(2,1)S(1)}, bf16[32,2,1024]{2,1,0:T(2,128)(2,1)}, u32[]{:S(2)}) copy-start(bf16[32,2,1024]{2,1,0:T(2,128)(2,1)} %param.13) | copy-start | bytes 393220
  0.7 24.7 %copy-start.10 = (s32[4]{0:T(128)S(1)}, s32[4]{0:T(128)}, u32[]{:S(2)}) copy-start(s32[4]{0:T(128)} %lens_ref.3) | copy-start | bytes 52
  2.2 23.2 %collective-permute-start.2 = (bf16[64,8192]{1,0:T(8,128)(2,1)S(1)}, bf16[64,8192]{1,0:T(8,128)(2,1)S(1)}, u32[]{:S(2)}, u32[]{:S(2)}) collective-permute-start(bf16[64,8192]{1,0:T(8,128)(2,1)S(1)} %reshape.19.q_mine), channel_id=1, source_target_pairs={{0,1},{1,0},{2,3},{3,2},{4,5},{5,4},{6,7},{7,6},{8,9},{9,8},{10,11... | collective-permute-start | bytes 3145736 | tf_op jit(solution)/shard_map/ppermute | solution.py:363
  5.2 15.6 %collective-permute-start.4 = (bf16[32,4224]{1,0:T(8,128)(2,1)}, bf16[32,4224]{1,0:T(8,128)(2,1)S(1)}, u32[]{:S(2)}, u32[]{:S(2)}) collective-permute-start(bf16[32,4224]{1,0:T(8,128)(2,1)} %norm_message.1), channel_id=1, source_target_pairs={{0,8},{1,9},{2,10},{3,11},{4,12},{5,13},{6,14},{7,15},{8,0},{9,1},... | collective-permute-start | bytes 811016 | tf_op jit(solution)/shard_map/ppermute | solution.py:348
  7.8 17.4 %collective-permute-start = (bf16[32,4224]{1,0:T(8,128)(2,1)}, bf16[32,4224]{1,0:T(8,128)(2,1)S(1)}, u32[]{:S(2)}, u32[]{:S(2)}) collective-permute-start(bf16[32,4224]{1,0:T(8,128)(2,1)} %norm_message.1), channel_id=1, source_target_pairs={{0,16},{1,17},{2,18},{3,19},{4,20},{5,21},{6,22},{7,23},{8,24},{9,... | collective-permute-start | bytes 811016 | tf_op jit(solution)/shard_map/ppermute | solution.py:348
  10.8 124.6 %copy-start = (bf16[64,1152]{1,0:T(8,128)(2,1)}, bf16[64,1152]{1,0:T(8,128)(2,1)S(1)}, u32[]{:S(2)}) copy-start(bf16[64,1152]{1,0:T(8,128)(2,1)S(1)} %reshape.17.k_mine.v_mine.n_mine) | copy-start | bytes 442372
  10.8 14.5 %collective-permute-start.3 = (bf16[64,1152]{1,0:T(8,128)(2,1)S(1)}, bf16[64,1152]{1,0:T(8,128)(2,1)S(1)}, u32[]{:S(2)}, u32[]{:S(2)}) collective-permute-start(bf16[64,1152]{1,0:T(8,128)(2,1)S(1)} %reshape.17.k_mine.v_mine.n_mine), channel_id=1, source_target_pairs={{0,1},{1,0},{2,3},{3,2},{4,5},{5,4},{6,7},{7,6},{8,9},{9,8},{10,11... | collective-permute-start | bytes 442376 | tf_op jit(solution)/shard_map/ppermute | solution.py:363
  20.8 28.0 %slice-start = ((s8[6291456]{0:T(1024)(128)(4,1)}), s8[4194304]{0:T(1024)(128)(4,1)S(1)}, s32[]{:S(2)}) async-start(s8[6291456]{0:T(1024)(128)(4,1)} %bitcast.5), calls=%async_computation | async-start | bytes 8388608
  20.8 28.0 %slice-start.2 = ((s8[6291456]{0:T(1024)(128)(4,1)}), s8[4194304]{0:T(1024)(128)(4,1)S(1)}, s32[]{:S(2)}) async-start(s8[6291456]{0:T(1024)(128)(4,1)} %bitcast.9), calls=%async_computation.2 | async-start | bytes 8388608
  22.0 26.9 %slice-start.1 = ((s8[6291456]{0:T(1024)(128)(4,1)}), s8[2097152]{0:T(1024)(128)(4,1)S(1)}, s32[]{:S(2)}) async-start(s8[6291456]{0:T(1024)(128)(4,1)} %bitcast.5), calls=%async_computation.1 | async-start | bytes 4194304
  22.0 26.9 %slice-start.3 = ((s8[6291456]{0:T(1024)(128)(4,1)}), s8[2097152]{0:T(1024)(128)(4,1)S(1)}, s32[]{:S(2)}) async-start(s8[6291456]{0:T(1024)(128)(4,1)} %bitcast.9), calls=%async_computation.3 | async-start | bytes 4194304
  22.0 15.1 %collective-permute-start.6 = (bf16[64,4224]{1,0:T(8,128)(2,1)S(1)}, bf16[64,4224]{1,0:T(8,128)(2,1)S(1)}, u32[]{:S(2)}, u32[]{:S(2)}) collective-permute-start(bf16[64,4224]{1,0:T(8,128)(2,1)S(1)} %pad_maximum_fusion.refs_0_), channel_id=1, source_target_pairs={{0,2},{1,5},{2,0},{3,7},{4,6},{5,1},{6,4},{7,3},{8,10},{9,13},{10,... | collective-permute-start | bytes 1622024 | tf_op jit(solution)/shard_map/ppermute | solution.py:348
  23.7 14.2 %collective-permute-start.7 = (bf16[64,4224]{1,0:T(8,128)(2,1)S(1)}, bf16[64,4224]{1,0:T(8,128)(2,1)S(1)}, u32[]{:S(2)}, u32[]{:S(2)}) collective-permute-start(bf16[64,4224]{1,0:T(8,128)(2,1)S(1)} %pad_maximum_fusion.refs_0_), channel_id=1, source_target_pairs={{0,4},{1,3},{2,6},{3,1},{4,0},{5,7},{6,2},{7,5},{8,12},{9,11},{10,... | collective-permute-start | bytes 1622024 | tf_op jit(solution)/shard_map/ppermute | solution.py:348
  25.3 22.1 %collective-permute-start.9 = (bf16[64,4224]{1,0:T(8,128)(2,1)S(1)}, bf16[64,4224]{1,0:T(8,128)(2,1)S(1)}, u32[]{:S(2)}, u32[]{:S(2)}) collective-permute-start(bf16[64,4224]{1,0:T(8,128)(2,1)S(1)} %pad_maximum_fusion.refs_0_), channel_id=1, source_target_pairs={{0,1},{1,0},{2,3},{3,2},{4,5},{5,4},{6,7},{7,6},{8,9},{9,8},{10,11... | collective-permute-start | bytes 1622024 | tf_op jit(solution)/shard_map/ppermute | solution.py:363
  25.3 13.3 %collective-permute-start.1 = (bf16[32,4224]{1,0:T(8,128)(2,1)S(1)}, bf16[32,4224]{1,0:T(8,128)(2,1)S(1)}, u32[]{:S(2)}, u32[]{:S(2)}) collective-permute-start(bf16[32,4224]{1,0:T(8,128)(2,1)S(1)} %collective-permute-done.refs_1_), channel_id=1, source_target_pairs={{0,8},{1,9},{2,10},{3,11},{4,12},{5,13},{6,14},{7,15},{8,0},{9,1},... | collective-permute-start | bytes 811016 | tf_op jit(solution)/shard_map/ppermute | solution.py:348
  25.4 2.2 %copy-start.6 = (bf16[2,1024,1024]{2,1,0:T(8,128)(2,1)S(1)}, bf16[2,1024,1024]{2,1,0:T(8,128)(2,1)}, u32[]{:S(2)}) copy-start(bf16[2,1024,1024]{2,1,0:T(8,128)(2,1)} %value_ref.3) | copy-start | bytes 12582916
  27.6 8.3 %copy-start.8 = (bf16[64,8192]{1,0:T(8,128)(2,1)}, bf16[64,8192]{1,0:T(8,128)(2,1)S(1)}, u32[]{:S(2)}) copy-start(bf16[64,8192]{1,0:T(8,128)(2,1)S(1)} %collective-permute-done.2.q_other) | copy-start | bytes 3145732
  35.8 82.7 %copy-start.1 = (bf16[32,8192]{1,0:T(8,128)(2,1)}, bf16[32,8192]{1,0:T(8,128)(2,1)S(1)}, u32[]{:S(2)}) copy-start(bf16[32,8192]{1,0:T(8,128)(2,1)S(1)} %attend.2.refs_10_.mine_0) | copy-start | bytes 1572868
  37.1 9.4 %collective-permute-start.8 = (bf16[64,4224]{1,0:T(8,128)(2,1)S(1)}, bf16[64,4224]{1,0:T(8,128)(2,1)S(1)}, u32[]{:S(2)}, u32[]{:S(2)}) collective-permute-start(bf16[64,4224]{1,0:T(8,128)(2,1)S(1)} %collective-permute-done.6.refs_1_), channel_id=1, source_target_pairs={{0,4},{1,3},{2,6},{3,1},{4,0},{5,7},{6,2},{7,5},{8,12},{9,11},{10,... | collective-permute-start | bytes 1622024 | tf_op jit(solution)/shard_map/ppermute | solution.py:348
  37.9 10.9 %collective-permute-start.11 = (bf16[64,4224]{1,0:T(8,128)(2,1)S(1)}, bf16[64,4224]{1,0:T(8,128)(2,1)S(1)}, u32[]{:S(2)}, u32[]{:S(2)}) collective-permute-start(bf16[64,4224]{1,0:T(8,128)(2,1)S(1)} %collective-permute-done.7.refs_2_), channel_id=1, source_target_pairs={{0,1},{1,0},{2,3},{3,2},{4,5},{5,4},{6,7},{7,6},{8,9},{9,8},{10,11... | collective-permute-start | bytes 1622024 | tf_op jit(solution)/shard_map/ppermute | solution.py:363
  38.0 10.8 %collective-permute-start.10 = (bf16[64,4224]{1,0:T(8,128)(2,1)S(1)}, bf16[64,4224]{1,0:T(8,128)(2,1)S(1)}, u32[]{:S(2)}, u32[]{:S(2)}) collective-permute-start(bf16[64,4224]{1,0:T(8,128)(2,1)S(1)} %collective-permute-done.6.refs_1_), channel_id=1, source_target_pairs={{0,1},{1,0},{2,3},{3,2},{4,5},{5,4},{6,7},{7,6},{8,9},{9,8},{10,11... | collective-permute-start | bytes 1622024 | tf_op jit(solution)/shard_map/ppermute | solution.py:363
  46.4 2.4 %collective-permute-start.12 = (bf16[64,4224]{1,0:T(8,128)(2,1)S(1)}, bf16[64,4224]{1,0:T(8,128)(2,1)S(1)}, u32[]{:S(2)}, u32[]{:S(2)}) collective-permute-start(bf16[64,4224]{1,0:T(8,128)(2,1)S(1)} %collective-permute-done.8.refs_3_), channel_id=1, source_target_pairs={{0,1},{1,0},{2,3},{3,2},{4,5},{5,4},{6,7},{7,6},{8,9},{9,8},{10,11... | collective-permute-start | bytes 1622024 | tf_op jit(solution)/shard_map/ppermute | solution.py:363
  46.5 17.9 %collective-permute-start.13 = (bf16[64,4224]{1,0:T(8,128)(2,1)S(1)}, bf16[64,4224]{1,0:T(8,128)(2,1)S(1)}, u32[]{:S(2)}, u32[]{:S(2)}) collective-permute-start(bf16[64,4224]{1,0:T(8,128)(2,1)S(1)} %constant_dynamic-update-slice_fusion.refs_11_.refs_0_), channel_id=1, source_target_pairs={{0,4},{1,3},{2,6},{3,1},{4,0},{5,7},{6,2},{7,5},{8,12},{9,11},{10,... | collective-permute-start | bytes 1622024 | tf_op jit(solution)/shard_map/ppermute | solution.py:348
  47.4 17.0 %collective-permute-start.5 = (bf16[64,4224]{1,0:T(8,128)(2,1)S(1)}, bf16[64,4224]{1,0:T(8,128)(2,1)S(1)}, u32[]{:S(2)}, u32[]{:S(2)}) collective-permute-start(bf16[64,4224]{1,0:T(8,128)(2,1)S(1)} %constant_dynamic-update-slice_fusion.refs_11_.refs_0_), channel_id=1, source_target_pairs={{0,2},{1,5},{2,0},{3,7},{4,6},{5,1},{6,4},{7,3},{8,10},{9,13},{10,... | collective-permute-start | bytes 1622024 | tf_op jit(solution)/shard_map/ppermute | solution.py:348
  64.3 2.8 %copy-start.4 = (bf16[1,768,4096]{2,1,0:T(8,128)(2,1)S(1)}, bf16[1,768,4096]{2,1,0:T(8,128)(2,1)}, u32[]{:S(2)}) copy-start(bf16[1,768,4096]{2,1,0:T(8,128)(2,1)} %param.23) | copy-start | bytes 18874372
  72.8 29.6 %collective-permute-start.19 = (bf16[256,4096]{1,0:T(8,128)(2,1)S(1)}, bf16[256,4096]{1,0:T(8,128)(2,1)S(1)}, u32[]{:S(2)}, u32[]{:S(2)}) collective-permute-start(bf16[256,4096]{1,0:T(8,128)(2,1)S(1)} %get-tuple-element.39), channel_id=1, source_target_pairs={{0,1},{1,0},{2,3},{3,2},{4,5},{5,4},{6,7},{7,6},{8,9},{9,8},{10,11... | collective-permute-start | bytes 6291464 | tf_op jit(solution)/shard_map/ppermute | solution.py:363
  72.9 9.4 %collective-permute-start.14 = (bf16[64,4224]{1,0:T(8,128)(2,1)S(1)}, bf16[64,4224]{1,0:T(8,128)(2,1)S(1)}, u32[]{:S(2)}, u32[]{:S(2)}) collective-permute-start(bf16[64,4224]{1,0:T(8,128)(2,1)S(1)} %collective-permute-done.5.refs_0_.refs_1_), channel_id=1, source_target_pairs={{0,4},{1,3},{2,6},{3,1},{4,0},{5,7},{6,2},{7,5},{8,12},{9,11},{10,... | collective-permute-start | bytes 1622024 | tf_op jit(solution)/shard_map/ppermute | solution.py:348
  74.5 7.8 %collective-permute-start.15 = (bf16[64,4224]{1,0:T(8,128)(2,1)S(1)}, bf16[64,4224]{1,0:T(8,128)(2,1)S(1)}, u32[]{:S(2)}, u32[]{:S(2)}) collective-permute-start(bf16[64,4224]{1,0:T(8,128)(2,1)S(1)} %constant_dynamic-update-slice_fusion.refs_11_.refs_0_), channel_id=1, source_target_pairs={{0,1},{1,0},{2,3},{3,2},{4,5},{5,4},{6,7},{7,6},{8,9},{9,8},{10,11... | collective-permute-start | bytes 1622024 | tf_op jit(solution)/shard_map/ppermute | solution.py:363
  74.5 7.8 %collective-permute-start.17 = (bf16[64,4224]{1,0:T(8,128)(2,1)S(1)}, bf16[64,4224]{1,0:T(8,128)(2,1)S(1)}, u32[]{:S(2)}, u32[]{:S(2)}) collective-permute-start(bf16[64,4224]{1,0:T(8,128)(2,1)S(1)} %collective-permute-done.13.refs_1_.refs_2_), channel_id=1, source_target_pairs={{0,1},{1,0},{2,3},{3,2},{4,5},{5,4},{6,7},{7,6},{8,9},{9,8},{10,11... | collective-permute-start | bytes 1622024 | tf_op jit(solution)/shard_map/ppermute | solution.py:363
  75.0 7.3 %collective-permute-start.16 = (bf16[64,4224]{1,0:T(8,128)(2,1)S(1)}, bf16[64,4224]{1,0:T(8,128)(2,1)S(1)}, u32[]{:S(2)}, u32[]{:S(2)}) collective-permute-start(bf16[64,4224]{1,0:T(8,128)(2,1)S(1)} %collective-permute-done.5.refs_0_.refs_1_), channel_id=1, source_target_pairs={{0,1},{1,0},{2,3},{3,2},{4,5},{5,4},{6,7},{7,6},{8,9},{9,8},{10,11... | collective-permute-start | bytes 1622024 | tf_op jit(solution)/shard_map/ppermute | solution.py:363
  82.3 1.9 %collective-permute-start.18 = (bf16[64,4224]{1,0:T(8,128)(2,1)S(1)}, bf16[64,4224]{1,0:T(8,128)(2,1)S(1)}, u32[]{:S(2)}, u32[]{:S(2)}) collective-permute-start(bf16[64,4224]{1,0:T(8,128)(2,1)S(1)} %collective-permute-done.14.refs_3_), channel_id=1, source_target_pairs={{0,1},{1,0},{2,3},{3,2},{4,5},{5,4},{6,7},{7,6},{8,9},{9,8},{10,11... | collective-permute-start | bytes 1622024 | tf_op jit(solution)/shard_map/ppermute | solution.py:363
  84.3 2.8 %copy-start.3 = (bf16[1,4096,768]{2,1,0:T(8,128)(2,1)S(1)}, bf16[1,4096,768]{2,1,0:T(8,128)(2,1)}, u32[]{:S(2)}) copy-start(bf16[1,4096,768]{2,1,0:T(8,128)(2,1)} %param.22) | copy-start | bytes 18874372
  102.5 1.3 copy-start.15
  103.8 2.8 %copy-start.5 = (bf16[1,768,4096]{2,1,0:T(8,128)(2,1)S(1)}, bf16[1,768,4096]{2,1,0:T(8,128)(2,1)}, u32[]{:S(2)}) copy-start(bf16[1,768,4096]{2,1,0:T(8,128)(2,1)} %param.23) | copy-start | bytes 18874372
  112.3 7.8 %collective-permute-start.21 = (bf16[128,4096]{1,0:T(8,128)(2,1)S(1)}, bf16[128,4096]{1,0:T(8,128)(2,1)S(1)}, u32[]{:S(2)}, u32[]{:S(2)}) collective-permute-start(bf16[128,4096]{1,0:T(8,128)(2,1)S(1)} %get-tuple-element.45), channel_id=1, source_target_pairs={{0,1},{1,0},{2,3},{3,2},{4,5},{5,4},{6,7},{7,6},{8,9},{9,8},{10,11... | collective-permute-start | bytes 3145736 | tf_op jit(solution)/shard_map/ppermute | solution.py:363
  118.1 15.4 %copy-start.16 = (bf16[256,4096]{1,0:T(8,128)(2,1)S(1)}, bf16[256,4096]{1,0:T(8,128)(2,1)}, u32[]{:S(2)}) copy-start(bf16[256,4096]{1,0:T(8,128)(2,1)} %copy-done.15) | copy-start | bytes 6291460
  118.1 2.8 %collective-permute-start.20 = (bf16[128,4096]{1,0:T(8,128)(2,1)S(1)}, bf16[128,4096]{1,0:T(8,128)(2,1)S(1)}, u32[]{:S(2)}, u32[]{:S(2)}) collective-permute-start(bf16[128,4096]{1,0:T(8,128)(2,1)S(1)} %get-tuple-element.43), channel_id=1, source_target_pairs={{0,1},{1,0},{2,3},{3,2},{4,5},{5,4},{6,7},{7,6},{8,9},{9,8},{10,11... | collective-permute-start | bytes 3145736 | tf_op jit(solution)/shard_map/ppermute | solution.py:363
  118.5 35.2 %collective-permute-start.25 = (bf16[32,8192]{1,0:T(8,128)(2,1)S(1)}, bf16[32,8192]{1,0:T(8,128)(2,1)S(1)}, u32[]{:S(2)}, u32[]{:S(2)}) collective-permute-start(bf16[32,8192]{1,0:T(8,128)(2,1)S(1)} %attend.2.refs_10_.mine_0), channel_id=1, source_target_pairs={{0,1},{1,0},{2,3},{3,2},{4,5},{5,4},{6,7},{7,6},{8,9},{9,8},{10,11... | collective-permute-start | bytes 1572872 | tf_op jit(solution)/shard_map/ppermute | solution.py:363
  118.7 14.8 %collective-permute-start.24 = (bf16[128,4096]{1,0:T(8,128)(2,1)S(1)}, bf16[128,4096]{1,0:T(8,128)(2,1)S(1)}, u32[]{:S(2)}, u32[]{:S(2)}) collective-permute-start(bf16[128,4096]{1,0:T(8,128)(2,1)S(1)} %add_convert_fusion.refs_0_), channel_id=1, source_target_pairs={{0,4},{1,3},{2,6},{3,1},{4,0},{5,7},{6,2},{7,5},{8,12},{9,11},{10,... | collective-permute-start | bytes 3145736 | tf_op jit(solution)/shard_map/ppermute | solution.py:348
  120.3 23.5 %collective-permute-start.23 = (bf16[64,4096]{1,0:T(8,128)(2,1)S(1)}, bf16[64,4096]{1,0:T(8,128)(2,1)S(1)}, u32[]{:S(2)}, u32[]{:S(2)}) collective-permute-start(bf16[64,4096]{1,0:T(8,128)(2,1)S(1)} %add_convert_fusion.2), channel_id=1, source_target_pairs={{0,4},{1,3},{2,6},{3,1},{4,0},{5,7},{6,2},{7,5},{8,12},{9,11},{10,... | collective-permute-start | bytes 1572872 | tf_op jit(solution)/shard_map/ppermute | solution.py:348
  121.0 14.4 %copy-start.7 = (bf16[2,1024,1024]{2,1,0:T(8,128)(2,1)S(1)}, bf16[2,1024,1024]{2,1,0:T(8,128)(2,1)}, u32[]{:S(2)}) copy-start(bf16[2,1024,1024]{2,1,0:T(8,128)(2,1)} %value_ref.3) | copy-start | bytes 12582916
  121.0 14.4 %copy-start.9 = (bf16[64,8192]{1,0:T(8,128)(2,1)S(1)}, bf16[64,8192]{1,0:T(8,128)(2,1)}, u32[]{:S(2)}) copy-start(bf16[64,8192]{1,0:T(8,128)(2,1)} %copy-done.8) | copy-start | bytes 3145732
  121.0 30.4 %collective-permute-start.22 = (bf16[64,4096]{1,0:T(8,128)(2,1)S(1)}, bf16[64,4096]{1,0:T(8,128)(2,1)S(1)}, u32[]{:S(2)}, u32[]{:S(2)}) collective-permute-start(bf16[64,4096]{1,0:T(8,128)(2,1)S(1)} %add_convert_fusion.1), channel_id=1, source_target_pairs={{0,4},{1,3},{2,6},{3,1},{4,0},{5,7},{6,2},{7,5},{8,12},{9,11},{10,... | collective-permute-start | bytes 1572872 | tf_op jit(solution)/shard_map/ppermute | solution.py:348
  133.9 9.8 %copy-start.11 = (f32[128,4096]{1,0:T(8,128)}, f32[128,4096]{1,0:T(8,128)S(1)}, u32[]{:S(2)}) copy-start(f32[128,4096]{1,0:T(8,128)S(1)} %convert_add_fusion) | copy-start | bytes 6291460
  134.0 28.3 %collective-permute-start.27 = (bf16[64,4096]{1,0:T(8,128)(2,1)S(1)}, bf16[64,4096]{1,0:T(8,128)(2,1)}, u32[]{:S(2)}, u32[]{:S(2)}) collective-permute-start(bf16[64,4096]{1,0:T(8,128)(2,1)S(1)} %slice.90.refs_0_), channel_id=1, source_target_pairs={{0,2},{1,5},{2,0},{3,7},{4,6},{5,1},{6,4},{7,3},{8,10},{9,13},{10,... | collective-permute-start | bytes 1572872 | tf_op jit(solution)/shard_map/ppermute | solution.py:348
  143.7 7.9 %copy-start.2 = (bf16[32,8192]{1,0:T(8,128)(2,1)}, bf16[32,8192]{1,0:T(8,128)(2,1)S(1)}, u32[]{:S(2)}) copy-start(bf16[32,8192]{1,0:T(8,128)(2,1)S(1)} %attend.3.mine_1) | copy-start | bytes 1572868
  143.7 10.8 %collective-permute-start.26 = (bf16[32,8192]{1,0:T(8,128)(2,1)S(1)}, bf16[32,8192]{1,0:T(8,128)(2,1)S(1)}, u32[]{:S(2)}, u32[]{:S(2)}) collective-permute-start(bf16[32,8192]{1,0:T(8,128)(2,1)S(1)} %attend.3.mine_1), channel_id=1, source_target_pairs={{0,1},{1,0},{2,3},{3,2},{4,5},{5,4},{6,7},{7,6},{8,9},{9,8},{10,11... | collective-permute-start | bytes 1572872 | tf_op jit(solution)/shard_map/ppermute | solution.py:363
  146.0 16.2 %collective-permute-start.30 = (bf16[32,4096]{1,0:T(8,128)(2,1)S(1)}, bf16[32,4096]{1,0:T(8,128)(2,1)}, u32[]{:S(2)}, u32[]{:S(2)}) collective-permute-start(bf16[32,4096]{1,0:T(8,128)(2,1)S(1)} %slice.93), channel_id=1, source_target_pairs={{0,2},{1,5},{2,0},{3,7},{4,6},{5,1},{6,4},{7,3},{8,10},{9,13},{10,... | collective-permute-start | bytes 786440 | tf_op jit(solution)/shard_map/ppermute | solution.py:348
  151.6 2.1 %copy-start.13 = (f32[64,4096]{1,0:T(8,128)}, f32[64,4096]{1,0:T(8,128)S(1)}, u32[]{:S(2)}) copy-start(f32[64,4096]{1,0:T(8,128)S(1)} %convert_add_fusion.1) | copy-start | bytes 3145732
  151.7 15.1 %collective-permute-start.29 = (bf16[32,4096]{1,0:T(8,128)(2,1)S(1)}, bf16[32,4096]{1,0:T(8,128)(2,1)S(1)}, u32[]{:S(2)}, u32[]{:S(2)}) collective-permute-start(bf16[32,4096]{1,0:T(8,128)(2,1)S(1)} %slice.92), channel_id=1, source_target_pairs={{0,2},{1,5},{2,0},{3,7},{4,6},{5,1},{6,4},{7,3},{8,10},{9,13},{10,... | collective-permute-start | bytes 786440 | tf_op jit(solution)/shard_map/ppermute | solution.py:348
  153.7 0.8 copy-start.17
  154.5 0.8 copy-start.18
  159.5 4.0 %copy-start.12 = (f32[128,4096]{1,0:T(8,128)S(1)}, f32[128,4096]{1,0:T(8,128)}, u32[]{:S(2)}) copy-start(f32[128,4096]{1,0:T(8,128)} %copy-done.11) | copy-start | bytes 6291460
  162.2 13.4 %copy-start.14 = (f32[64,4096]{1,0:T(8,128)S(1)}, f32[64,4096]{1,0:T(8,128)}, u32[]{:S(2)}) copy-start(f32[64,4096]{1,0:T(8,128)} %copy-done.13) | copy-start | bytes 3145732
  163.5 12.1 %collective-permute-start.31 = (bf16[32,4096]{1,0:T(8,128)(2,1)S(1)}, bf16[32,4096]{1,0:T(8,128)(2,1)S(1)}, u32[]{:S(2)}, u32[]{:S(2)}) collective-permute-start(bf16[32,4096]{1,0:T(8,128)(2,1)S(1)} %slice_add_fusion.1), channel_id=1, source_target_pairs={{0,8},{1,9},{2,10},{3,11},{4,12},{5,13},{6,14},{7,15},{8,0},{9,1},... | collective-permute-start | bytes 786440 | tf_op jit(solution)/shard_map/ppermute | solution.py:348
  164.7 14.0 %collective-permute-start.28 = (bf16[32,4096]{1,0:T(8,128)(2,1)S(1)}, bf16[32,4096]{1,0:T(8,128)(2,1)S(1)}, u32[]{:S(2)}, u32[]{:S(2)}) collective-permute-start(bf16[32,4096]{1,0:T(8,128)(2,1)S(1)} %slice.91), channel_id=1, source_target_pairs={{0,8},{1,9},{2,10},{3,11},{4,12},{5,13},{6,14},{7,15},{8,0},{9,1},... | collective-permute-start | bytes 786440 | tf_op jit(solution)/shard_map/ppermute | solution.py:348
  175.7 9.7 %collective-permute-start.32 = (bf16[32,4096]{1,0:T(8,128)(2,1)S(1)}, bf16[32,4096]{1,0:T(8,128)(2,1)S(1)}, u32[]{:S(2)}, u32[]{:S(2)}) collective-permute-start(bf16[32,4096]{1,0:T(8,128)(2,1)S(1)} %fusion.1), channel_id=1, source_target_pairs={{0,16},{1,17},{2,18},{3,19},{4,20},{5,21},{6,22},{7,23},{8,24},{9,... | collective-permute-start | bytes 786440 | tf_op jit(solution)/shard_map/ppermute | solution.py:348
